TPU v7x, 32 devices: a whole 2x2x4 slice. The times are simulated.
32 devices in a mesh: ctx: 8 (over z, y), tp: 4 (over x, core).
Axes of the slice: x: 2, y: 2, z: 4, core: 2. Of those that a mesh axis runs over, the one named last changes fastest.
Arguments:
- tokens: bfloat16 [64, 5, 16, 2304], P('tp', None, 'ctx'), may hold values from -6 to 6
- doc_ids: int32 [5, 1024], replicated, may hold values from 0 to 3, as said below
- attn_in_gain: bfloat16 [2304], replicated, may hold values from 0.099609375 to 1.8984375
- query_weight: bfloat16 [2304, 2048], P(None, 'tp'), may hold values from -0.125 to 0.125
- key_weight: bfloat16 [2304, 1024], P(None, 'tp'), may hold values from -0.125 to 0.125
- value_weight: bfloat16 [2304, 1024], P(None, 'tp'), may hold values from -0.125 to 0.125
- output_weight: bfloat16 [2048, 2304], P('tp'), may hold values from -0.125 to 0.125
- attn_out_gain: bfloat16 [2304], replicated, may hold values from 0.099609375 to 1.8984375
- ffw_in_gain: bfloat16 [2304], replicated, may hold values from 0.099609375 to 1.8984375
- gate_weight: bfloat16 [2304, 9216], P(None, 'tp'), may hold values from -0.125 to 0.125
- up_weight: bfloat16 [2304, 9216], P(None, 'tp'), may hold values from -0.125 to 0.125
- down_weight: bfloat16 [9216, 2304], P('tp'), may hold values from -0.0625 to 0.0625
- ffw_out_gain: bfloat16 [2304], replicated, may hold values from 0.099609375 to 1.8984375
- cotangent: bfloat16 [64, 5, 16, 2304], P('tp', None, 'ctx'), may hold values from -6 to 6
Outputs:
- layer_out: bfloat16 [64, 5, 16, 2304], P('tp', None, 'ctx')
- tokens_grad: float32 [64, 5, 16, 2304], P('tp', None, 'ctx')
- attn_in_gain_grad: float32 [2304], P('ctx')
- query_weight_grad: float32 [2304, 2048], P('ctx', 'tp')
- key_weight_grad: float32 [2304, 1024], P('ctx', 'tp')
- value_weight_grad: float32 [2304, 1024], P('ctx', 'tp')
- output_weight_grad: float32 [2048, 2304], P('tp', 'ctx')
- attn_out_gain_grad: float32 [2304], P('ctx')
- ffw_in_gain_grad: float32 [2304], P('ctx')
- gate_weight_grad: float32 [2304, 9216], P('ctx', 'tp')
- up_weight_grad: float32 [2304, 9216], P('ctx', 'tp')
- down_weight_grad: float32 [9216, 2304], P('tp', 'ctx')
- ffw_out_gain_grad: float32 [2304], P('ctx')
Inputs may be any that keep to these rules, and one draw needn't show every extreme that they name: `doc_ids`: in each sequence the document numbers start at 0 and rise by 0 or 1 from one position to the next. One sequence is a single document; every other sequence holds exactly four documents.
All inputs are finite; a program needn't handle non-finite values.
Results may differ from a plain program's by a relative error of at most 0.025.
Values may be sent and summed in bfloat16 or wider, within the bound.
A program may use at most 256 MiB of HBM per device.

v0:
```python
import math

import jax
import jax.numpy as jnp
from jax import lax
from jax.sharding import PartitionSpec as P

HD = 256


EPS = 1e-06
CAP = 50.0
BASE = 10000.0


def rms_scale(values, gain):
    return values * lax.rsqrt(jnp.mean(values * values, axis=-1, keepdims=True) + EPS) * gain


def rotate(values, positions):
    half_dim = values.shape[-1] // 2
    frequency = BASE ** (-jnp.arange(half_dim).astype(jnp.float32) / half_dim)
    angles = positions.astype(jnp.float32)[..., None, None] * frequency
    cosine = jnp.cos(angles)
    sine_part = jnp.sin(angles)
    lower_half = values[..., :half_dim]
    upper_half = values[..., half_dim:]
    return jnp.concatenate(
        [
            lower_half * cosine - upper_half * sine_part,
            upper_half * cosine + lower_half * sine_part,
        ],
        -1,
    )


def seq_starts(doc_ids):
    index = jnp.arange(doc_ids.shape[1], dtype=jnp.int32)
    change = jnp.concatenate(
        [jnp.ones((doc_ids.shape[0], 1), bool), doc_ids[:, 1:] != doc_ids[:, :-1]], 1
    )
    return lax.cummax(jnp.where(change, index[None, :], jnp.zeros_like(doc_ids)), axis=1)


def gelu_times(gate, up_val):
    return jax.nn.gelu(gate, approximate=True) * up_val


def body(
    tokens,
    doc_ids,
    attn_in_gain,
    query_weight,
    key_weight,
    value_weight,
    output_weight,
    attn_out_gain,
    ffw_in_gain,
    gate_weight,
    up_weight,
    down_weight,
    ffw_out_gain,
    cotangent,
):
    f32 = jnp.float32
    bf16 = jnp.bfloat16
    stretch_rows, seq_count, slot_count, model_width = tokens.shape
    ctx_count = lax.axis_size("ctx")
    tp_count = lax.axis_size("tp")
    ctx_rank = lax.axis_index("ctx")
    stretch_len = stretch_rows * tp_count
    length = 2 * stretch_len * ctx_count
    local_rows = stretch_rows * seq_count * slot_count
    local_heads = query_weight.shape[1] // HD
    local_kv = key_weight.shape[1] // HD
    group_size = local_heads // local_kv
    score_scale = HD ** (-0.5)
    block_len = math.gcd(length, 512)
    block_count = length // block_len
    starts = seq_starts(doc_ids)
    slot_stretch = jnp.stack([ctx_rank, 2 * ctx_count - 1 - ctx_rank])
    stretch_iota = jnp.arange(stretch_len, dtype=jnp.int32)
    query_tok = slot_stretch[:, None] * stretch_len + stretch_iota[None, :]
    query_start = jnp.stack(
        [
            lax.dynamic_slice_in_dim(starts, slot_stretch[0] * stretch_len, stretch_len, 1),
            lax.dynamic_slice_in_dim(starts, slot_stretch[1] * stretch_len, stretch_len, 1),
        ],
        1,
    )
    query_pos = query_tok[None] - query_start
    rows_pos = jnp.transpose(query_pos, (2, 0, 1))
    key_slot = jnp.arange(2 * ctx_count, dtype=jnp.int32)
    key_stretch = jnp.where(key_slot % 2 == 0, key_slot // 2, 2 * ctx_count - 1 - key_slot // 2)
    key_tok = (key_stretch[:, None] * stretch_len + stretch_iota[None, :]).reshape(length)
    row_tok = query_tok.reshape(2 * stretch_len)
    row_start = query_start.reshape(seq_count, 2 * stretch_len)
    inputs = tokens.reshape(local_rows, model_width).astype(f32)
    normed_f, norm_back_in = jax.vjp(rms_scale, inputs, attn_in_gain.astype(f32))
    normed_in = normed_f.astype(bf16)
    block_rows = lax.all_gather(normed_in, "tp", axis=0, tiled=True)
    normed_all = block_rows
    query_proj = jnp.dot(block_rows, query_weight, preferred_element_type=f32)
    key_proj = jnp.dot(block_rows, key_weight, preferred_element_type=f32)
    value_proj = jnp.dot(block_rows, value_weight, preferred_element_type=f32)
    query_rot = rotate(
        query_proj.reshape(stretch_len, seq_count, 2, local_heads, HD), rows_pos
    ).astype(bf16)
    key_rot = rotate(key_proj.reshape(stretch_len, seq_count, 2, local_kv, HD), rows_pos).astype(
        bf16
    )
    value_low = value_proj.astype(bf16)
    queries = jnp.transpose(
        query_rot.reshape(stretch_len, seq_count, 2, local_kv, group_size, HD), (1, 3, 4, 2, 0, 5)
    ).reshape(seq_count, local_kv, group_size, 2 * stretch_len, HD)
    keys_local = jnp.transpose(
        key_rot.reshape(stretch_len, seq_count, 2, local_kv * HD), (1, 2, 0, 3)
    )
    values_local = jnp.transpose(
        value_low.reshape(stretch_len, seq_count, 2, local_kv * HD), (1, 2, 0, 3)
    )
    keys_all, values_all = (
        lax.all_gather(keys_local, "ctx", axis=1, tiled=True),
        lax.all_gather(values_local, "ctx", axis=1, tiled=True),
    )
    keys_all = keys_all.reshape(seq_count, length, local_kv, HD)
    values_all = values_all.reshape(seq_count, length, local_kv, HD)

    def block_scores(offset):
        key_block = lax.dynamic_slice_in_dim(keys_all, offset, block_len, 1)
        key_index = lax.dynamic_slice_in_dim(key_tok, offset, block_len)
        allowed = (key_index[None, None, :] <= row_tok[None, :, None]) & (
            key_index[None, None, :] >= row_start[:, :, None]
        )
        raw_scores = jnp.einsum("skgrd,sbkd->skgrb", queries, key_block, preferred_element_type=f32)
        capped_tanh = jnp.tanh(raw_scores * (score_scale / CAP))
        weights_exp = jnp.where(allowed[:, None, None], jnp.exp(CAP * capped_tanh), 0.0)
        return (key_block, capped_tanh, weights_exp)

    def forward_step(step, state_now):
        weight_total, running = state_now
        offset = step * block_len
        key_block, capped_tanh, weights_exp = block_scores(offset)
        value_block = lax.dynamic_slice_in_dim(values_all, offset, block_len, 1)
        weight_total = weight_total + jnp.sum(weights_exp, axis=-1)
        running = running + jnp.einsum(
            "skgrb,sbkd->skgrd", weights_exp.astype(bf16), value_block, preferred_element_type=f32
        )
        return (weight_total, running)

    zero_total = jnp.zeros((seq_count, local_kv, group_size, 2 * stretch_len), f32)
    zero_running = jnp.zeros((seq_count, local_kv, group_size, 2 * stretch_len, HD), f32)
    weight_total, running = lax.fori_loop(0, block_count, forward_step, (zero_total, zero_running))
    attn_f = running / weight_total[..., None]
    attn_rows = jnp.transpose(
        attn_f.astype(bf16).reshape(seq_count, local_kv, group_size, 2, stretch_len, HD),
        (4, 0, 3, 1, 2, 5),
    ).reshape(local_rows * tp_count, local_heads * HD)
    attn_branch = lax.psum_scatter(
        jnp.dot(attn_rows, output_weight, preferred_element_type=f32),
        "tp",
        scatter_dimension=0,
        tiled=True,
    )
    attn_normed, norm_back_attn = jax.vjp(rms_scale, attn_branch, attn_out_gain.astype(f32))
    resid = inputs + attn_normed
    ffw_normed, norm_back_ffw_in = jax.vjp(rms_scale, resid, ffw_in_gain.astype(f32))
    ffw_in = ffw_normed.astype(bf16)
    block_rows = lax.all_gather(ffw_in, "tp", axis=0, tiled=True)
    ffw_all = block_rows
    gate_val = jnp.dot(block_rows, gate_weight, preferred_element_type=f32)
    up_val = jnp.dot(block_rows, up_weight, preferred_element_type=f32)
    mixed_f, mixed_back = jax.vjp(gelu_times, gate_val, up_val)
    mixed_act = mixed_f.astype(bf16)
    ffw_branch = lax.psum_scatter(
        jnp.dot(mixed_act, down_weight, preferred_element_type=f32),
        "tp",
        scatter_dimension=0,
        tiled=True,
    )
    ffw_out_normed, norm_back_ffw_out = jax.vjp(rms_scale, ffw_branch, ffw_out_gain.astype(f32))
    layer_out = (resid + ffw_out_normed).astype(bf16).reshape(tokens.shape)
    upstream = cotangent.reshape(local_rows, model_width).astype(f32)
    ffw_branch_grad, ffw_out_gain_part = norm_back_ffw_out(upstream)
    block_rows = lax.all_gather(ffw_branch_grad.astype(bf16), "tp", axis=0, tiled=True)
    ffw_grad_all = block_rows
    mixed_grad = jnp.einsum("rd,fd->rf", block_rows, down_weight, preferred_element_type=f32)
    down_part = jnp.einsum("rf,rd->fd", mixed_act, ffw_grad_all, preferred_element_type=f32)
    gate_grad_f, up_grad_f = mixed_back(mixed_grad)
    gate_grad = gate_grad_f.astype(bf16)
    up_grad = up_grad_f.astype(bf16)
    gate_part = jnp.einsum("rd,rf->df", ffw_all, gate_grad, preferred_element_type=f32)
    up_part = jnp.einsum("rd,rf->df", ffw_all, up_grad, preferred_element_type=f32)
    ffw_in_grad = lax.psum_scatter(
        jnp.einsum("rf,df->rd", gate_grad, gate_weight, preferred_element_type=f32)
        + jnp.einsum("rf,df->rd", up_grad, up_weight, preferred_element_type=f32),
        "tp",
        scatter_dimension=0,
        tiled=True,
    )
    resid_part, ffw_in_gain_part = norm_back_ffw_in(ffw_in_grad)
    resid_grad = upstream + resid_part
    branch_grad, attn_out_gain_part = norm_back_attn(resid_grad)
    block_rows = lax.all_gather(branch_grad.astype(bf16), "tp", axis=0, tiled=True)
    attn_rows_grad = jnp.einsum("rd,hd->rh", block_rows, output_weight, preferred_element_type=f32)
    output_part = jnp.einsum("rh,rd->hd", attn_rows, block_rows, preferred_element_type=f32)
    attn_grad = jnp.transpose(
        attn_rows_grad.reshape(stretch_len, seq_count, 2, local_kv, group_size, HD),
        (1, 3, 4, 2, 0, 5),
    ).reshape(seq_count, local_kv, group_size, 2 * stretch_len, HD)
    row_dot = jnp.sum(attn_grad * attn_f, axis=-1)
    scaled_grad = (attn_grad / weight_total[..., None]).astype(bf16)
    row_shift = row_dot / weight_total

    def backward_step(step, state_now):
        query_acc, key_acc, value_acc = state_now
        offset = step * block_len
        key_block, capped_tanh, weights_exp = block_scores(offset)
        value_block = lax.dynamic_slice_in_dim(values_all, offset, block_len, 1)
        weight_grad = jnp.einsum(
            "skgrd,sbkd->skgrb", scaled_grad, value_block, preferred_element_type=f32
        )
        score_grad = (
            weights_exp
            * (weight_grad - row_shift[..., None])
            * (score_scale * (1.0 - capped_tanh * capped_tanh))
        ).astype(bf16)
        query_acc = query_acc + jnp.einsum(
            "skgrb,sbkd->skgrd", score_grad, key_block, preferred_element_type=f32
        )
        key_block_grad = jnp.einsum(
            "skgrb,skgrd->sbkd", score_grad, queries, preferred_element_type=f32
        )
        value_block_grad = jnp.einsum(
            "skgrb,skgrd->sbkd", weights_exp.astype(bf16), scaled_grad, preferred_element_type=f32
        )
        key_acc = lax.dynamic_update_slice_in_dim(key_acc, key_block_grad, offset, 1)
        value_acc = lax.dynamic_update_slice_in_dim(value_acc, value_block_grad, offset, 1)
        return (query_acc, key_acc, value_acc)

    zero_keys = jnp.zeros((seq_count, length, local_kv, HD), f32)
    query_acc, key_acc, value_acc = lax.fori_loop(
        0, block_count, backward_step, (zero_running, zero_keys, zero_keys)
    )
    key_sum, value_sum = (
        lax.psum_scatter(
            key_acc.reshape(seq_count, 2 * ctx_count, stretch_len, local_kv * HD).astype(
                jnp.bfloat16
            ),
            "ctx",
            scatter_dimension=1,
            tiled=True,
        ).astype(jnp.float32),
        lax.psum_scatter(
            value_acc.reshape(seq_count, 2 * ctx_count, stretch_len, local_kv * HD).astype(
                jnp.bfloat16
            ),
            "ctx",
            scatter_dimension=1,
            tiled=True,
        ).astype(jnp.float32),
    )
    key_rows_grad = jnp.transpose(key_sum, (2, 0, 1, 3)).reshape(
        stretch_len, seq_count, 2, local_kv, HD
    )
    key_proj_grad = (
        rotate(key_rows_grad, -rows_pos).astype(bf16).reshape(local_rows * tp_count, local_kv * HD)
    )
    value_proj_grad = (
        jnp.transpose(value_sum, (2, 0, 1, 3))
        .astype(bf16)
        .reshape(local_rows * tp_count, local_kv * HD)
    )
    query_rows_grad = jnp.transpose(
        query_acc.reshape(seq_count, local_kv, group_size, 2, stretch_len, HD), (4, 0, 3, 1, 2, 5)
    ).reshape(stretch_len, seq_count, 2, local_heads, HD)
    query_proj_grad = (
        rotate(query_rows_grad, -rows_pos)
        .astype(bf16)
        .reshape(local_rows * tp_count, local_heads * HD)
    )
    query_part = jnp.einsum("rd,rh->dh", normed_all, query_proj_grad, preferred_element_type=f32)
    key_part = jnp.einsum("rd,rh->dh", normed_all, key_proj_grad, preferred_element_type=f32)
    value_part = jnp.einsum("rd,rh->dh", normed_all, value_proj_grad, preferred_element_type=f32)
    summed = jnp.einsum("rh,dh->rd", query_proj_grad, query_weight, preferred_element_type=f32)
    summed = summed + jnp.einsum("rh,dh->rd", key_proj_grad, key_weight, preferred_element_type=f32)
    normed_grad = lax.psum_scatter(
        (
            summed
            + jnp.einsum("rh,dh->rd", value_proj_grad, value_weight, preferred_element_type=f32)
        ).astype(jnp.bfloat16),
        "tp",
        scatter_dimension=0,
        tiled=True,
    ).astype(jnp.float32)
    input_part, attn_in_gain_part = norm_back_in(normed_grad)
    tokens_grad = (resid_grad + input_part).reshape(tokens.shape)
    (
        query_sum,
        key_wsum,
        value_wsum,
        output_sum,
        gate_sum,
        up_sum,
        down_sum,
        attn_in_gain_sum,
        attn_out_gain_sum,
        ffw_in_gain_sum,
        ffw_out_gain_sum,
    ) = (
        lax.psum_scatter(
            query_part.astype(jnp.bfloat16), "ctx", scatter_dimension=0, tiled=True
        ).astype(jnp.float32),
        lax.psum_scatter(
            key_part.astype(jnp.bfloat16), "ctx", scatter_dimension=0, tiled=True
        ).astype(jnp.float32),
        lax.psum_scatter(
            value_part.astype(jnp.bfloat16), "ctx", scatter_dimension=0, tiled=True
        ).astype(jnp.float32),
        lax.psum_scatter(
            output_part.astype(jnp.bfloat16), "ctx", scatter_dimension=1, tiled=True
        ).astype(jnp.float32),
        lax.psum_scatter(
            gate_part.astype(jnp.bfloat16), "ctx", scatter_dimension=0, tiled=True
        ).astype(jnp.float32),
        lax.psum_scatter(
            up_part.astype(jnp.bfloat16), "ctx", scatter_dimension=0, tiled=True
        ).astype(jnp.float32),
        lax.psum_scatter(
            down_part.astype(jnp.bfloat16), "ctx", scatter_dimension=1, tiled=True
        ).astype(jnp.float32),
        lax.psum_scatter(
            attn_in_gain_part.astype(jnp.bfloat16), "ctx", scatter_dimension=0, tiled=True
        ).astype(jnp.float32),
        lax.psum_scatter(
            attn_out_gain_part.astype(jnp.bfloat16), "ctx", scatter_dimension=0, tiled=True
        ).astype(jnp.float32),
        lax.psum_scatter(
            ffw_in_gain_part.astype(jnp.bfloat16), "ctx", scatter_dimension=0, tiled=True
        ).astype(jnp.float32),
        lax.psum_scatter(
            ffw_out_gain_part.astype(jnp.bfloat16), "ctx", scatter_dimension=0, tiled=True
        ).astype(jnp.float32),
    )
    attn_in_gain_grad, attn_out_gain_grad, ffw_in_gain_grad, ffw_out_gain_grad = lax.psum(
        (attn_in_gain_sum, attn_out_gain_sum, ffw_in_gain_sum, ffw_out_gain_sum), "tp"
    )
    return (
        layer_out,
        tokens_grad,
        attn_in_gain_grad,
        query_sum,
        key_wsum,
        value_wsum,
        output_sum,
        attn_out_gain_grad,
        ffw_in_gain_grad,
        gate_sum,
        up_sum,
        down_sum,
        ffw_out_gain_grad,
    )


def solution(mesh):
    placed = (
        P("tp", None, "ctx", None),
        P(),
        P(),
        P(None, "tp"),
        P(None, "tp"),
        P(None, "tp"),
        P("tp", None),
        P(),
        P(),
        P(None, "tp"),
        P(None, "tp"),
        P("tp", None),
        P(),
        P("tp", None, "ctx", None),
    )
    return jax.shard_map(
        body,
        mesh=mesh,
        in_specs=placed,
        out_specs=(
            P("tp", None, "ctx", None),
            P("tp", None, "ctx", None),
            P("ctx"),
            P("ctx", "tp"),
            P("ctx", "tp"),
            P("ctx", "tp"),
            P("tp", "ctx"),
            P("ctx"),
            P("ctx"),
            P("ctx", "tp"),
            P("ctx", "tp"),
            P("tp", "ctx"),
            P("ctx"),
        ),
        check_vma=False,
    )
```

profile of v0, /device:TPU:0, one launch (start us, length us, event | category | flops | bytes accessed | tf_op | source)
XLA Modules:
  0.0 1664.2 jit_solution(6656788764321738299)
XLA Ops:
  7.3 3.1 reshape.582
  18.3 3.5 reduce-window.6
  28.3 18.7 %all-gather.7.cloned.1.call-done = bf16[640,2304]{1,0:T(8,128)(2,1)} async-done(((bf16[160,2304]{1,0:T(8,128)(2,1)}), bf16[640,2304]{1,0:T(8,128)(2,1)}) %all-gather.7.cloned.1.call-update) | async-done | bytes 2949136 | tf_op jit(solution)/shard_map/all_gather | solution.py:101
  47.0 3.6 fusion.95
  54.6 3.1 convolution_convert_fusion.7
  60.8 10.5 multiply_cosine_fusion.2
  71.3 5.3 fusion.96
  82.3 27.0 %all-gather.9.cloned.1.call-done = bf16[5,16,64,256]{3,2,0,1:T(8,128)(2,1)} async-done(((bf16[5,2,64,256]{3,2,0,1:T(8,128)(2,1)}), bf16[5,16,64,256]{3,2,0,1:T(8,128)(2,1)}) %all-gather.9.cloned.1.call-update) | async-done | bytes 2621456 | tf_op jit(solution)/shard_map/all_gather | solution.py:123
  109.3 3.6 copy.76
  112.9 52.5 %all-gather.11.cloned.1.call-done = bf16[5,16,64,256]{3,2,0,1:T(8,128)(2,1)} async-done(((bf16[5,2,64,256]{3,2,0,1:T(8,128)(2,1)}), bf16[5,16,64,256]{3,2,0,1:T(8,128)(2,1)}) %all-gather.11.cloned.1.call-update) | async-done | bytes 2621456 | tf_op jit(solution)/shard_map/all_gather | solution.py:124
  165.3 3.6 copy.80
  168.9 17.7 %while.36 = (s32[]{:T(128)}, f32[5,1,2,128]{3,2,1,0:T(2,128)S(1)}, f32[5,1,2,128,256]{4,3,2,0,1:T(8,128)}, s32[1024]{0:T(1024)S(1)}, s32[5,2,64]{2,1,0:T(2,128)}...) while((s32[]{:T(128)}, f32[5,1,2,128]{3,2,1,0:T(2,128)S(1)}, ...), condition=%wide.wide.region_5.6_spmd.clone, body=%wide.wide.region_3.5_spmd.clone.sunk | while | flops 677709184 | bytes 12288730 | solution.py:153
  169.6 3.7 fusion.181
  173.3 4.3 fusion.182
  178.2 3.7 fusion.181
  181.9 4.7 fusion.182
  189.8 4.2 fusion.97
  194.7 53.8 %reduce-scatter.14.cloned.1.call-done = f32[160,2304]{1,0:T(8,128)} async-done(((f32[640,2304]{1,0:T(8,128)}), f32[160,2304]{1,0:T(8,128)}) %reduce-scatter.14.cloned.1.call-update) | async-done | bytes 1474576 | tf_op jit(solution)/shard_map/reduce_scatter | solution.py:159
  254.8 27.3 %all-gather.13.cloned.1.call-done = bf16[640,2304]{1,0:T(8,128)(2,1)} async-done(((bf16[160,2304]{1,0:T(8,128)(2,1)}), bf16[640,2304]{1,0:T(8,128)(2,1)}) %all-gather.13.cloned.1.call-update) | async-done | bytes 2949136 | tf_op jit(solution)/shard_map/all_gather | solution.py:169
  282.1 10.7 fusion.98
  292.8 15.6 multiply_convert_fusion.1
  308.5 10.2 fusion.99
  321.7 52.9 %reduce-scatter.16.cloned.1.call-done = f32[160,2304]{1,0:T(8,128)} async-done(((f32[640,2304]{1,0:T(8,128)}), f32[160,2304]{1,0:T(8,128)}) %reduce-scatter.16.cloned.1.call-update) | async-done | bytes 1474576 | tf_op jit(solution)/shard_map/reduce_scatter | solution.py:175
  381.9 27.1 %all-gather.15.cloned.1.call-done = bf16[640,2304]{1,0:T(8,128)(2,1)} async-done(((bf16[160,2304]{1,0:T(8,128)(2,1)}), bf16[640,2304]{1,0:T(8,128)(2,1)}) %all-gather.15.cloned.1.call-update) | async-done | bytes 2949136 | tf_op jit(solution)/shard_map/all_gather | solution.py:185
  409.0 17.1 %multiply_convert_fusion = (bf16[640,2304]{1,0:T(8,128)(2,1)S(1)}, bf16[640,2304]{1,0:T(8,128)(2,1)S(1)}) fusion(f32[640,2304]{1,0:T(8,128)} %copy-done.51, f32[640,2304]{1,0:T(8,128)} %get-tuple-element.540, bf16[640,2304]{1,0:T(8,128)(2,1)} %all-gather.15.cloned.1.call-done, bf16[2304,2304]{1,0:T(8,128)(2,1)} %param.29), kind=kOutput, calls=%fused_computation.73 | convolution fusion | flops 6830161920 | bytes 31260672 | tf_op jit(solution)/shard_map/rd,fd->rf/dot_general | solution.py:187
  426.1 14.3 fusion.100
  440.4 13.9 convolution_add_fusion
  454.4 55.9 %reduce-scatter.18.cloned.1.call-done = f32[160,2304]{1,0:T(8,128)} async-done(((f32[640,2304]{1,0:T(8,128)}), f32[160,2304]{1,0:T(8,128)}) %reduce-scatter.18.cloned.1.call-update) | async-done | bytes 1474576 | tf_op jit(solution)/shard_map/reduce_scatter | solution.py:194
  513.2 3.4 multiply_reduce_fusion.2
  519.3 27.3 %all-gather.17.cloned.1.call-done = bf16[640,2304]{1,0:T(8,128)(2,1)} async-done(((bf16[160,2304]{1,0:T(8,128)(2,1)}), bf16[640,2304]{1,0:T(8,128)(2,1)}) %all-gather.17.cloned.1.call-update) | async-done | bytes 2949136 | tf_op jit(solution)/shard_map/all_gather | solution.py:204
  546.5 4.6 fusion.101
  551.2 3.1 reshape.574
  559.6 33.6 %while.37 = (s32[]{:T(128)}, f32[5,1,2,128,256]{4,3,2,0,1:T(8,128)}, bf16[5,1024,1,256]{3,1,0,2:T(8,128)(2,1)}, bf16[5,1024,1,256]{3,1,0,2:T(8,128)(2,1)}, s32[1...) while((s32[]{:T(128)}, ...), condition=%wide.wide.region_17.18_spmd.clone, body=%wide.wide.region_16.17_spmd.clone.sunk | while | flops 1688273024 | bytes 79775624 | solution.py:242
  559.6 3.4 fusion.193
  563.7 3.5 fusion.194
  567.2 3.2 fusion.195
  576.2 3.4 fusion.193
  580.3 3.5 fusion.194
  583.8 3.5 fusion.195
  593.2 3.6 copy.86
  596.8 3.6 copy.90
  604.8 3.5 convolution_convert_fusion.4
  608.5 5.3 convolution_convert_fusion.3
  613.9 13.5 convolution_convert_fusion.2
  627.5 13.4 convolution_convert_fusion.1
  641.3 13.4 convolution_convert_fusion
  655.4 12.1 reduce-scatter.20.cloned.1.call-done
  670.3 4.1 convolution_convert_fusion.6
  674.5 67.0 %reduce-scatter.22.cloned.1.call-done = bf16[5,2,64,256]{3,2,0,1:T(8,128)(2,1)} async-done(((bf16[5,16,64,256]{3,2,0,1:T(8,128)(2,1)}), bf16[5,2,64,256]{3,2,0,1:T(8,128)(2,1)}) %reduce-scatter.22.cloned.1.call-update) | async-done | bytes 327696 | tf_op jit(solution)/shard_map/reduce_scatter | solution.py:254
  742.9 4.0 convolution_convert_fusion.5
  747.2 3.5 fusion.102
  757.8 55.8 %reduce-scatter.26.cloned.1.call-done = bf16[288,512]{1,0:T(8,128)(2,1)} async-done(((bf16[2304,512]{1,0:T(8,128)(2,1)}), bf16[288,512]{1,0:T(8,128)(2,1)}) %reduce-scatter.26.cloned.1.call-update) | async-done | bytes 294928 | tf_op jit(solution)/shard_map/reduce_scatter | solution.py:311
  815.5 70.1 %reduce-scatter.32.cloned.1.call-done = bf16[512,288]{0,1:T(8,128)(2,1)} async-done(((bf16[512,2304]{0,1:T(8,128)(2,1)}), bf16[512,288]{0,1:T(8,128)(2,1)}) %reduce-scatter.32.cloned.1.call-update) | async-done | bytes 294928 | tf_op jit(solution)/shard_map/reduce_scatter | solution.py:320
  887.4 181.1 %reduce-scatter.34.cloned.1.call-done = bf16[288,2304]{1,0:T(8,128)(2,1)} async-done(((bf16[2304,2304]{1,0:T(8,128)(2,1)}), bf16[288,2304]{1,0:T(8,128)(2,1)}) %reduce-scatter.34.cloned.1.call-update) | async-done | bytes 1327120 | tf_op jit(solution)/shard_map/reduce_scatter | solution.py:323
  1068.5 3.0 convert_element_type.281
  1071.5 179.5 %reduce-scatter.36.cloned.1.call-done = bf16[288,2304]{1,0:T(8,128)(2,1)} async-done(((bf16[2304,2304]{1,0:T(8,128)(2,1)}), bf16[288,2304]{1,0:T(8,128)(2,1)}) %reduce-scatter.36.cloned.1.call-update) | async-done | bytes 1327120 | tf_op jit(solution)/shard_map/reduce_scatter | solution.py:326
  1254.0 179.9 %reduce-scatter.38.cloned.1.call-done = bf16[2304,288]{0,1:T(8,128)(2,1)} async-done(((bf16[2304,2304]{0,1:T(8,128)(2,1)}), bf16[2304,288]{0,1:T(8,128)(2,1)}) %reduce-scatter.38.cloned.1.call-update) | async-done | bytes 1327120 | tf_op jit(solution)/shard_map/reduce_scatter | solution.py:329
  1436.9 63.4 %reduce-scatter.28.cloned.1.call-done = bf16[288,256]{1,0:T(8,128)(2,1)} async-done(((bf16[2304,256]{1,0:T(8,128)(2,1)}), bf16[288,256]{1,0:T(8,128)(2,1)}) %reduce-scatter.28.cloned.1.call-update) | async-done | bytes 147472 | tf_op jit(solution)/shard_map/reduce_scatter | solution.py:314
  1502.0 64.8 %reduce-scatter.30.cloned.1.call-done = bf16[288,256]{1,0:T(8,128)(2,1)} async-done(((bf16[2304,256]{1,0:T(8,128)(2,1)}), bf16[288,256]{1,0:T(8,128)(2,1)}) %reduce-scatter.30.cloned.1.call-update) | async-done | bytes 147472 | tf_op jit(solution)/shard_map/reduce_scatter | solution.py:317
  1568.4 36.7 %reduce-scatter.24.cloned.1.call-done = bf16[160,2304]{1,0:T(8,128)(2,1)} async-done(((bf16[640,2304]{1,0:T(8,128)(2,1)}), bf16[160,2304]{1,0:T(8,128)(2,1)}) %reduce-scatter.24.cloned.1.call-update) | async-done | bytes 737296 | tf_op jit(solution)/shard_map/reduce_scatter | solution.py:287
  1606.9 3.5 fusion.62
  1610.4 3.1 reshape.581
  1613.5 37.1 %all-reduce.6 = (bf16[2304]{0:T(1024)(128)(2,1)S(1)}, bf16[2304]{0:T(1024)(128)(2,1)S(1)}, bf16[2304]{0:T(1024)(128)(2,1)S(1)}, bf16[2304]{0:T(1024)(128)(2,1)S(1)}) all-reduce(bf16[2304]{0:T(1024)(128)(2,1)S(1)} %get-tuple-element.455, bf16[2304]{0:T(1024)(128)(2,1)S(1)} %copy-done.34, ...), channel_id=8, replica_groups=mesh['ctx'=8,'tp'=4] {'ctx'}, use_global_device_ids=true, to_apply=%region_23.24.clone | all-reduce | flops 9216 | bytes 36864
  1650.8 6.7 all-reduce.5
  (281 shorter events, 104.5 us)
Async XLA Ops:
  7.2 182.6 %copy-start = (bf16[512,2304]{1,0:T(8,128)(2,1)S(1)}, bf16[512,2304]{1,0:T(8,128)(2,1)}, u32[]{:S(2)}) copy-start(bf16[512,2304]{1,0:T(8,128)(2,1)} %param.24) | copy-start | bytes 7077892
  7.2 3.2 copy-start.20
  7.2 39.7 %all-gather.7.cloned.1.call-start = ((), (), s32[]{:S(2)}) async-start(), calls=%async_computation.13 | async-start | bytes 3686400 | tf_op jit(solution)/shard_map/all_gather | solution.py:101
  11.2 35.7 %copy-start.24 = (bf16[2304,256]{1,0:T(8,128)(2,1)S(1)}, bf16[2304,256]{1,0:T(8,128)(2,1)}, u32[]{:S(2)}) copy-start(bf16[2304,256]{1,0:T(8,128)(2,1)} %param.22) | copy-start | bytes 3538948
  12.0 38.5 %copy-start.27 = (f32[2304]{0:T(1024)}, f32[2304]{0:T(1024)S(1)}, u32[]{:S(2)}) copy-start(f32[2304]{0:T(1024)S(1)} %convert_element_type.236) | copy-start | bytes 27652
  13.6 4.7 copy-start.39
  16.7 92.7 %all-gather.9.cloned.1.call-start = ((), (), s32[]{:S(2)}) async-start(), calls=%async_computation.14 | async-start | bytes 2949120 | tf_op jit(solution)/shard_map/all_gather | solution.py:123
  28.2 24.0 %copy-start.44 = (f32[128]{0:T(128)}, f32[128]{0:T(128)S(1)}, u32[]{:S(2)}) copy-start(f32[128]{0:T(128)S(1)} %multiply_power_fusion) | copy-start | bytes 1540
  54.5 4.3 copy-start.32
  54.5 110.8 %all-gather.11.cloned.1.call-start = ((), (), s32[]{:S(2)}) async-start(), calls=%async_computation.15 | async-start | bytes 2949120 | tf_op jit(solution)/shard_map/all_gather | solution.py:124
  58.6 189.9 %reduce-scatter.14.cloned.1.call-start = ((), (), s32[]{:S(2)}) async-start(), calls=%async_computation.16 | async-start | bytes 7372800 | tf_op jit(solution)/shard_map/reduce_scatter | solution.py:159
  112.9 56.0 %copy-start.50 = (s32[2]{0:T(128)S(1)}, s32[2]{0:T(128)}, u32[]{:S(2)}) copy-start(s32[2]{0:T(128)} %copy-done.49) | copy-start | bytes 28
  194.1 88.0 %all-gather.13.cloned.1.call-start = ((), (), s32[]{:S(2)}) async-start(), calls=%async_computation.17 | async-start | bytes 3686400 | tf_op jit(solution)/shard_map/all_gather | solution.py:169
  254.5 120.1 %reduce-scatter.16.cloned.1.call-start = ((), (), s32[]{:S(2)}) async-start(), calls=%async_computation.18 | async-start | bytes 7372800 | tf_op jit(solution)/shard_map/reduce_scatter | solution.py:175
  282.1 10.7 copy-start.47
  282.1 26.4 %slice-start = ((s8[10616832]{0:T(1024)(128)(4,1)}), s8[4194304]{0:T(1024)(128)(4,1)S(1)}, s32[]{:S(2)}) async-start(s8[10616832]{0:T(1024)(128)(4,1)} %bitcast.308), calls=%async_computation.32 | async-start | bytes 8388608
  282.1 26.4 %slice-start.1 = ((s8[10616832]{0:T(1024)(128)(4,1)}), s8[4194304]{0:T(1024)(128)(4,1)S(1)}, s32[]{:S(2)}) async-start(s8[10616832]{0:T(1024)(128)(4,1)} %bitcast.308), calls=%async_computation.33 | async-start | bytes 8388608
  292.8 15.7 copy-start.51
  292.8 15.7 slice-start.2
  318.7 3.0 copy-start.43
  318.7 90.3 %all-gather.15.cloned.1.call-start = ((), (), s32[]{:S(2)}) async-start(), calls=%async_computation.19 | async-start | bytes 3686400 | tf_op jit(solution)/shard_map/all_gather | solution.py:185
  374.6 4.6 copy-start.6
  374.6 4.6 copy-start.9
  374.6 4.6 copy-start.10
  381.4 128.8 %reduce-scatter.18.cloned.1.call-start = ((), (), s32[]{:S(2)}) async-start(), calls=%async_computation.20 | async-start | bytes 7372800 | tf_op jit(solution)/shard_map/reduce_scatter | solution.py:194
  426.1 14.3 copy-start.53
  426.1 14.3 copy-start.52
  454.3 92.2 %all-gather.17.cloned.1.call-start = ((), (), s32[]{:S(2)}) async-start(), calls=%async_computation.21 | async-start | bytes 3686400 | tf_op jit(solution)/shard_map/all_gather | solution.py:204
  510.2 3.0 copy-start.7
  510.2 3.0 copy-start.8
  516.6 2.6 copy-start.29
  519.0 148.6 %reduce-scatter.20.cloned.1.call-start = ((), (), s32[]{:S(2)}) async-start(), calls=%async_computation.22 | async-start | bytes 2949120 | tf_op jit(solution)/shard_map/reduce_scatter | solution.py:246
  551.2 4.6 copy-start.16
  567.2 3.2 copy-start.12
  570.4 2.4 copy-start.2
  570.4 3.5 copy-start.14
  570.9 3.8 copy-start.13
  583.8 3.6 copy-start.12
  587.4 2.4 copy-start.2
  587.4 3.5 copy-start.14
  587.9 3.8 copy-start.13
  596.8 144.7 %reduce-scatter.22.cloned.1.call-start = ((), (), s32[]{:S(2)}) async-start(), calls=%async_computation.23 | async-start | bytes 2949120 | tf_op jit(solution)/shard_map/reduce_scatter | solution.py:254
  600.4 2.3 copy-start.22
  600.4 2.3 copy-start.23
  600.4 213.2 %reduce-scatter.26.cloned.1.call-start = ((), (), s32[]{:S(2)}) async-start(), calls=%async_computation.25 | async-start | bytes 2654208 | tf_op jit(solution)/shard_map/reduce_scatter | solution.py:311
  602.7 2.0 copy-start.46
  604.8 3.8 copy-start.18
  608.3 277.3 %reduce-scatter.32.cloned.1.call-start = ((), (), s32[]{:S(2)}) async-start(), calls=%async_computation.28 | async-start | bytes 2654208 | tf_op jit(solution)/shard_map/reduce_scatter | solution.py:320
  613.9 454.6 %reduce-scatter.34.cloned.1.call-start = ((), (), s32[]{:S(2)}) async-start(), calls=%async_computation.29 | async-start | bytes 11943936 | tf_op jit(solution)/shard_map/reduce_scatter | solution.py:323
  627.4 623.5 %reduce-scatter.36.cloned.1.call-start = ((), (), s32[]{:S(2)}) async-start(), calls=%async_computation.30 | async-start | bytes 11943936 | tf_op jit(solution)/shard_map/reduce_scatter | solution.py:326
  640.9 793.0 %reduce-scatter.38.cloned.1.call-start = ((), (), s32[]{:S(2)}) async-start(), calls=%async_computation.31 | async-start | bytes 11943936 | tf_op jit(solution)/shard_map/reduce_scatter | solution.py:329
  654.7 13.9 copy-start.45
  654.7 845.6 %reduce-scatter.28.cloned.1.call-start = ((), (), s32[]{:S(2)}) async-start(), calls=%async_computation.26 | async-start | bytes 1327104 | tf_op jit(solution)/shard_map/reduce_scatter | solution.py:314
  674.4 892.3 %reduce-scatter.30.cloned.1.call-start = ((), (), s32[]{:S(2)}) async-start(), calls=%async_computation.27 | async-start | bytes 1327104 | tf_op jit(solution)/shard_map/reduce_scatter | solution.py:317
  746.9 3.8 copy-start.25
  747.0 858.2 %reduce-scatter.24.cloned.1.call-start = ((), (), s32[]{:S(2)}) async-start(), calls=%async_computation.24 | async-start | bytes 3686400 | tf_op jit(solution)/shard_map/reduce_scatter | solution.py:287
  1254.0 351.1 %copy-start.4 = (f32[160,2304]{1,0:T(8,128)S(1)}, f32[160,2304]{1,0:T(8,128)}, u32[]{:S(2)}) copy-start(f32[160,2304]{1,0:T(8,128)} %reshape.582) | copy-start | bytes 4423684
  1254.0 351.1 %copy-start.28 = (f32[2304]{0:T(1024)S(1)}, f32[2304]{0:T(1024)}, u32[]{:S(2)}) copy-start(f32[2304]{0:T(1024)} %copy-done.27) | copy-start | bytes 27652
  1254.0 351.1 %copy-start.38 = (f32[160]{0:T(256)S(1)}, f32[160]{0:T(256)}, u32[]{:S(2)}) copy-start(f32[160]{0:T(256)} %copy-done.37) | copy-start | bytes 1924
  1254.0 352.9 %copy-start.40 = (f32[160]{0:T(256)S(1)}, f32[160]{0:T(256)}, u32[]{:S(2)}) copy-start(f32[160]{0:T(256)} %copy-done.39) | copy-start | bytes 1924
  1606.9 50.6 %copy-start.1 = (bf16[512,2304]{1,0:T(8,128)(2,1)S(1)}, bf16[512,2304]{1,0:T(8,128)(2,1)}, u32[]{:S(2)}) copy-start(bf16[512,2304]{1,0:T(8,128)(2,1)} %param.24) | copy-start | bytes 7077892
  1610.4 3.1 copy-start.34
  1610.4 3.1 copy-start.35
  1610.4 3.1 copy-start.36
  (17 other events, 18.6 us)
Sparse Core Ops, SparseCore 0:
  16.8 30.1 all-gather.6
  54.6 54.6 all-gather.8
  112.1 53.2 all-gather.10
  194.2 54.2 reduce-scatter.13
  254.6 27.4 all-gather.12
  318.8 55.7 reduce-scatter.15
  381.5 27.4 all-gather.14
  454.4 55.7 reduce-scatter.17
  519.1 27.4 all-gather.16
  596.9 70.5 reduce-scatter.19
  672.0 69.3 reduce-scatter.21
  745.8 67.8 reduce-scatter.25
  817.5 67.9 reduce-scatter.31
  889.4 179.0 reduce-scatter.33
  1071.9 179.0 reduce-scatter.35
  1254.9 179.0 reduce-scatter.37
  1437.1 63.1 reduce-scatter.27
  1503.6 63.1 reduce-scatter.29
  1569.3 35.7 reduce-scatter.23
where the time goes:
time: 1670 us; the launch traced here: 1660 us
  waiting for transfers between devices  1250 us (75%)
  matrix products  206 us (12%)
  other arithmetic  75.5 us (5%)
  local copies, waits for them, and re-layouts  67.3 us (4%)
  blocking collectives  43.8 us (3%)
    reduce_scatter x1, waiting for transfers between devices, body(): lax.psum_scatter(gate_part.astype(jnp.bfloat16), 'ctx', scatter_dimension...  181 us
    reduce_scatter x1, waiting for transfers between devices, body(): lax.psum_scatter(down_part.astype(jnp.bfloat16), 'ctx', scatter_dimension...  180 us
    reduce_scatter x1, waiting for transfers between devices, body(): lax.psum_scatter(up_part.astype(jnp.bfloat16), 'ctx', scatter_dimension=0...  179 us
    reduce_scatter x1, waiting for transfers between devices, body(): lax.psum_scatter(output_part.astype(jnp.bfloat16), 'ctx', scatter_dimensi...  70.1 us
    reduce_scatter x1, waiting for transfers between devices, body(): lax.psum_scatter(value_acc.reshape(seq_count, 2 * ctx_count, stretch_len,...  67 us
    reduce_scatter x1, waiting for transfers between devices, body(): lax.psum_scatter(value_part.astype(jnp.bfloat16), 'ctx', scatter_dimensio...  64.8 us
    reduce_scatter x1, waiting for transfers between devices, body(): lax.psum_scatter(key_part.astype(jnp.bfloat16), 'ctx', scatter_dimension=...  63.4 us
    reduce_scatter x1, waiting for transfers between devices, body(): lax.psum_scatter(jnp.einsum('rf,df->rd', gate_grad, gate_weight, preferre...  55.9 us
  transfers between devices with their start and end apart: 19, of which 19 were waited for; matrix products, arithmetic and copies ran while one was open for 8% of the time, Pallas kernels for 0%

commit v1 on v0

v1 whole, which is shorter than its diff:
```python
import functools

import jax
import jax.numpy as jnp
from jax import lax
from jax.experimental import pallas as pl
from jax.experimental.pallas import tpu as pltpu
from jax.sharding import PartitionSpec as P

HD = 256
EPS = 1e-06
CAP = 50.0
BASE = 10000.0
MIB = 1 << 20
F32 = jnp.float32
BF16 = jnp.bfloat16
VMEM = pltpu.VMEM
MESH = pl.DeviceIdType.MESH


def bits_of(mask):
    return [b for b in range(mask.bit_length()) if mask >> b & 1]


def flipped(index, mask):
    for b in bits_of(mask):
        index = index + (1 - 2 * ((index // (1 << b)) % 2)) * (1 << b)
    return index


def without(mask, bit):
    return (mask >> bit + 1 << bit) | (mask & (1 << bit) - 1)


def submasks(bits):
    masks = [0]
    for b in bits:
        masks = masks + [m | 1 << b for m in masks]
    return masks


def greet(axis, count):
    me = lax.axis_index(axis)
    barrier = pltpu.get_barrier_semaphore()
    steps = count.bit_length() - 1
    for b in range(steps):
        pl.semaphore_signal(
            barrier, inc=1, device_id={axis: flipped(me, 1 << b)}, device_id_type=MESH
        )
    pl.semaphore_wait(barrier, steps)


def remote(axis, src, dst, sems, at, partner):
    return pltpu.make_async_remote_copy(
        src_ref=src,
        dst_ref=dst,
        send_sem=sems[0].at[at],
        recv_sem=sems[1].at[at],
        device_id={axis: partner},
        device_id_type=MESH,
    )


def tp_kernel(fn, count, items, n_in, n_out, scatter, gather, *refs):
    refs = list(refs)
    part = refs.pop(0) if scatter else None
    ins = [refs.pop(0) for _ in range(n_in)]
    whole = refs.pop(0) if gather else None
    outs = [refs.pop(0) for _ in range(n_out)]
    if scatter:
        landed, sendbuf = refs.pop(0), refs.pop(0)
        rs_sems = (refs.pop(0), refs.pop(0))
    if gather:
        ag_sems = (refs.pop(0), refs.pop(0))
    me = lax.axis_index("tp")
    steps = count.bit_length() - 1
    order = list(range(steps))
    greet("tp", count)

    def rs_copy(item, step, sub):
        bit = 1 << order[step]
        mask = bit | sub
        src = part.at[item, :, flipped(me, mask)] if step == 0 else sendbuf.at[item, mask]
        return remote("tp", src, landed.at[item, mask], rs_sems, (item, mask), flipped(me, bit))

    def rs_sum(item, mask, upto):
        total = part[item, :, flipped(me, mask)].astype(F32)
        for step in range(upto):
            total = total + landed[item, 1 << order[step] | mask].astype(F32)
        return total

    def rs_subs(step):
        return submasks(order[step + 1 :])

    def ag_copy(item, step, mask):
        bit = 1 << order[steps - 1 - step]
        block = whole.at[item, :, flipped(me, mask)]
        return remote("tp", block, block, ag_sems, (item, mask | bit), flipped(me, bit))

    def ag_masks(step):
        return submasks([order[steps - 1 - s] for s in range(step)])

    if scatter:
        for item in range(items):
            for sub in rs_subs(0):
                rs_copy(item, 0, sub).start()
        for step in range(1, steps):
            for item in range(items):
                for sub in rs_subs(step - 1):
                    rs_copy(item, step - 1, sub).wait_recv()
                for sub in rs_subs(step):
                    mask = 1 << order[step] | sub
                    sendbuf[item, mask] = rs_sum(item, mask, step).astype(BF16)
                    rs_copy(item, step, sub).start()
    for item in range(items):
        total = None
        if scatter:
            for sub in rs_subs(steps - 1):
                rs_copy(item, steps - 1, sub).wait_recv()
            total = rs_sum(item, 0, steps)
        sent = fn(item, total, ins, outs)
        if gather:
            whole[item, :, me] = sent.astype(BF16)
            for step in range(steps):
                ag_copy(item, step, 0).start()
    if gather:
        for got in range(steps):
            for item in range(items):
                for mask in ag_masks(got):
                    ag_copy(item, got, mask).wait_recv()
                    for step in range(got + 1, steps):
                        ag_copy(item, step, mask | 1 << order[steps - 1 - got]).start()
        for step in range(steps):
            for item in range(items):
                for mask in ag_masks(step):
                    ag_copy(item, step, mask).wait_send()
    if scatter:
        for step in range(steps):
            for item in range(items):
                for sub in rs_subs(step):
                    rs_copy(item, step, sub).wait_send()


def tp_exchange(name, cid, fn, ins, outs, part=None, gather=True):
    count = lax.axis_size("tp")
    rows_shape = ins[0].shape
    items, slots, rows, width = rows_shape
    scatter = part is not None
    out_shape = list(outs)
    if gather:
        out_shape = [jax.ShapeDtypeStruct((items, slots, count, rows, width), BF16)] + out_shape
    scratch = []
    dma = pltpu.SemaphoreType.DMA((items, count))
    if scatter:
        scratch += [VMEM((items, count, slots, rows, width), BF16)] * 2 + [dma, dma]
    if gather:
        scratch += [dma, dma]
    args = ([part] if scatter else []) + list(ins)
    return pl.pallas_call(
        functools.partial(
            tp_kernel, fn, count, items, len(ins), len(outs), scatter, gather
        ),
        out_shape=out_shape,
        in_specs=[pl.BlockSpec(memory_space=VMEM)] * len(args),
        out_specs=[pl.BlockSpec(memory_space=VMEM)] * len(out_shape),
        scratch_shapes=scratch,
        compiler_params=pltpu.CompilerParams(
            collective_id=cid, has_side_effects=True, vmem_limit_bytes=40 * MIB
        ),
        name=name,
    )(*args)


def ctx_orders(items, steps):
    usual = list(range(steps))[::-1]
    if steps < 2:
        return [usual] * items
    other = usual[:-2] + [usual[-1], usual[-2]]
    return [other if i % 4 == 3 else usual for i in range(items)]


def ctx_gather_kernel(count, items, block, whole, send_sem, recv_sem, local_sem):
    me = lax.axis_index("ctx")
    steps = count.bit_length() - 1
    orders = ctx_orders(items, steps)
    own = pltpu.make_async_copy(block, whole.at[:, me], local_sem)
    own.start()
    greet("ctx", count)

    def copy(item, step, mask):
        bit = 1 << orders[item][step]
        dst = whole.at[item, flipped(me, mask)]
        src = block.at[item] if mask == 0 else dst
        return remote(
            "ctx", src, dst, (send_sem, recv_sem), (item, mask | bit), flipped(me, bit)
        )

    def masks(item, step):
        return submasks(orders[item][:step])

    for step in range(steps):
        for item in range(items):
            copy(item, step, 0).start()
    for got in range(steps):
        for item in range(items):
            for mask in masks(item, got):
                copy(item, got, mask).wait_recv()
                for step in range(got + 1, steps):
                    copy(item, step, mask | 1 << orders[item][got]).start()
    for step in range(steps):
        for item in range(items):
            for mask in masks(item, step):
                copy(item, step, mask).wait_send()
    own.wait()


def ctx_gather(block, cid):
    count = lax.axis_size("ctx")
    items, rows, cols = block.shape
    dma = pltpu.SemaphoreType.DMA((items, count))
    return pl.pallas_call(
        functools.partial(ctx_gather_kernel, count, items),
        out_shape=jax.ShapeDtypeStruct((items, count, rows, cols), block.dtype),
        in_specs=[pl.BlockSpec(memory_space=VMEM)],
        out_specs=pl.BlockSpec(memory_space=VMEM),
        scratch_shapes=[dma, dma, pltpu.SemaphoreType.DMA],
        compiler_params=pltpu.CompilerParams(
            collective_id=cid, has_side_effects=True, vmem_limit_bytes=56 * MIB
        ),
        name="ctx_gather",
    )(block)


def ctx_scatter_kernel(count, items, part, out, landed, sendbuf, send_sem, recv_sem):
    me = lax.axis_index("ctx")
    steps = count.bit_length() - 1
    orders = [order[::-1] for order in ctx_orders(items, steps)]
    greet("ctx", count)

    def copy(item, step, sub):
        bit = 1 << orders[item][step]
        mask = bit | sub
        first = orders[item][0]
        src = part.at[item, flipped(me, mask)] if step == 0 else sendbuf.at[item, without(mask, first)]
        return remote(
            "ctx", src, landed.at[item, mask], (send_sem, recv_sem), (item, mask), flipped(me, bit)
        )

    def total_of(item, mask, upto):
        total = part[item, flipped(me, mask)].astype(F32)
        for step in range(upto):
            total = total + landed[item, 1 << orders[item][step] | mask].astype(F32)
        return total

    def subs(item, step):
        return submasks(orders[item][step + 1 :])

    for item in range(items):
        for sub in subs(item, 0):
            copy(item, 0, sub).start()
    for step in range(1, steps):
        for item in range(items):
            for sub in subs(item, step - 1):
                copy(item, step - 1, sub).wait_recv()
            for sub in subs(item, step):
                mask = 1 << orders[item][step] | sub
                slot = without(mask, orders[item][0])
                sendbuf[item, slot] = total_of(item, mask, step).astype(BF16)
                copy(item, step, sub).start()
    for item in range(items):
        for sub in subs(item, steps - 1):
            copy(item, steps - 1, sub).wait_recv()
        out[item] = total_of(item, 0, steps)
    for step in range(steps):
        for item in range(items):
            for sub in subs(item, step):
                copy(item, step, sub).wait_send()


def ctx_scatter(part, cid):
    count = lax.axis_size("ctx")
    items, _, rows, cols = part.shape
    dma = pltpu.SemaphoreType.DMA((items, count))
    return pl.pallas_call(
        functools.partial(ctx_scatter_kernel, count, items),
        out_shape=jax.ShapeDtypeStruct((items, rows, cols), F32),
        in_specs=[pl.BlockSpec(memory_space=VMEM)],
        out_specs=pl.BlockSpec(memory_space=VMEM),
        scratch_shapes=[
            VMEM(part.shape, BF16),
            VMEM((items, count // 2, rows, cols), BF16),
            dma,
            dma,
        ],
        compiler_params=pltpu.CompilerParams(
            collective_id=cid, has_side_effects=True, vmem_limit_bytes=56 * MIB
        ),
        name="ctx_scatter",
    )(part)


def halve(part, order):
    count = lax.axis_size("ctx")
    steps = count.bit_length() - 1
    me = lax.axis_index("ctx")
    left = list(range(steps))[::-1]
    total = part.reshape((2,) * steps + (part.shape[0] // count, part.shape[1]))
    for at, b in enumerate(order):
        axis = left.index(b)
        left.remove(b)
        mine = (me >> b) & 1
        give = lax.dynamic_index_in_dim(total, 1 - mine, axis, keepdims=False)
        keep = lax.dynamic_index_in_dim(total, mine, axis, keepdims=False)
        got = lax.ppermute(give, "ctx", [(i, i ^ (1 << b)) for i in range(count)])
        total = keep.astype(F32) + got.astype(F32)
        if at < steps - 1:
            total = total.astype(BF16)
    return total


def inv_rms(v):
    return lax.rsqrt(jnp.mean(v * v, axis=-1, keepdims=True) + EPS)


def rms_back(dy, v, g):
    r = inv_rms(v)
    dg = jnp.sum(dy * v * r, axis=tuple(range(v.ndim - 1)), keepdims=True)
    gdy = g * dy
    dv = r * gdy - v * (r * r * r) * jnp.mean(gdy * v, axis=-1, keepdims=True)
    return dv, dg.reshape(1, -1)


def add_to(ref, item, value):
    ref[...] = value if item == 0 else ref[...] + value


def enter_rows(item, _, ins, outs):
    tokens, gain = ins
    v = tokens[item].astype(F32)
    return v * inv_rms(v) * gain[...].astype(F32)


def mid_rows(item, branch, ins, outs):
    tokens, attn_gain, ffw_gain = ins
    branch_out, resid_out = outs
    branch_out[item] = branch
    resid = tokens[item].astype(F32) + branch * inv_rms(branch) * attn_gain[...].astype(F32)
    resid_out[item] = resid
    return resid * inv_rms(resid) * ffw_gain[...].astype(F32)


def turn_rows(item, branch, ins, outs):
    resid, cotangent, gain = ins
    layer_out, gain_grad = outs
    g = gain[...].astype(F32)
    layer_out[item] = (resid[item] + branch * inv_rms(branch) * g).astype(BF16)
    dv, dg = rms_back(cotangent[item].astype(F32), branch, g)
    add_to(gain_grad, item, dg)
    return dv


def mid_back_rows(item, ffw_grad, ins, outs):
    resid, branch, cotangent, ffw_gain, attn_gain = ins
    resid_grad_out, ffw_gain_grad, attn_gain_grad = outs
    dv, dg = rms_back(ffw_grad, resid[item], ffw_gain[...].astype(F32))
    add_to(ffw_gain_grad, item, dg)
    resid_grad = cotangent[item].astype(F32) + dv
    resid_grad_out[item] = resid_grad
    dv, dg = rms_back(resid_grad, branch[item], attn_gain[...].astype(F32))
    add_to(attn_gain_grad, item, dg)
    return dv


def leave_rows(item, normed_grad, ins, outs):
    tokens, resid_grad, gain = ins
    tokens_grad, gain_grad = outs
    dv, dg = rms_back(normed_grad, tokens[item].astype(F32), gain[...].astype(F32))
    add_to(gain_grad, item, dg)
    tokens_grad[item] = resid_grad[item] + dv


def rotate(values, cosine, sine):
    half_dim = values.shape[-1] // 2
    low, high = values[..., :half_dim], values[..., half_dim:]
    return jnp.concatenate([low * cosine - high * sine, high * cosine + low * sine], -1)


def gelu_times(gate, up_val):
    return jax.nn.gelu(gate, approximate=True) * up_val


def body(
    tokens,
    doc_ids,
    attn_in_gain,
    query_weight,
    key_weight,
    value_weight,
    output_weight,
    attn_out_gain,
    ffw_in_gain,
    gate_weight,
    up_weight,
    down_weight,
    ffw_out_gain,
    cotangent,
):
    stretch_rows, seqs, slots, width = tokens.shape
    ctx_count = lax.axis_size("ctx")
    tp_count = lax.axis_size("tp")
    ctx_rank = lax.axis_index("ctx")
    stretch = stretch_rows * tp_count
    length = 2 * stretch * ctx_count
    rows = stretch * slots
    all_rows = seqs * rows
    local_heads = query_weight.shape[1] // HD
    local_kv = key_weight.shape[1] // HD
    group = local_heads // local_kv
    scale = HD ** (-0.5)
    own = (seqs, slots, stretch_rows, width)
    steps = ctx_count.bit_length() - 1
    usual = list(range(steps))
    other = usual if steps < 2 else [1, 0] + usual[2:]

    slot_stretch = jnp.stack([ctx_rank, 2 * ctx_count - 1 - ctx_rank])
    iota = jnp.arange(stretch, dtype=jnp.int32)
    query_tok = slot_stretch[:, None] * stretch + iota[None, :]
    row_tok = query_tok.reshape(rows)
    row_doc = jnp.concatenate(
        [lax.dynamic_slice_in_dim(doc_ids, slot_stretch[i] * stretch, stretch, 1) for i in (0, 1)],
        1,
    )
    row_start = jnp.sum(
        (doc_ids[:, None, :] < row_doc[:, :, None]).astype(jnp.int32), axis=-1
    )
    row_pos = row_tok[None] - row_start
    frequency = BASE ** (-jnp.arange(HD // 2).astype(F32) / (HD // 2))
    angles = row_pos.astype(F32)[..., None] * frequency
    cosine = jnp.cos(angles)[:, :, None, :]
    sine = jnp.sin(angles)[:, :, None, :]
    key_slot = jnp.arange(2 * ctx_count, dtype=jnp.int32)
    key_stretch = jnp.where(key_slot % 2 == 0, key_slot // 2, 2 * ctx_count - 1 - key_slot // 2)
    key_tok = (key_stretch[:, None] * stretch + iota[None, :]).reshape(length)
    allowed = (key_tok[None, None, :] <= row_tok[None, :, None]) & (
        key_tok[None, None, :] >= row_start[:, :, None]
    )

    def wide(gain):
        return gain.reshape(1, width)

    mine = jnp.transpose(tokens, (1, 2, 0, 3))
    upstream = jnp.transpose(cotangent, (1, 2, 0, 3))
    f32_rows = jax.ShapeDtypeStruct(own, F32)
    gain_shape = jax.ShapeDtypeStruct((1, width), F32)

    (normed_all,) = tp_exchange("enter", 1, enter_rows, [mine, wide(attn_in_gain)], [])
    normed_all = normed_all.reshape(all_rows, width)
    dot = functools.partial(jnp.dot, preferred_element_type=F32)
    ein = functools.partial(jnp.einsum, preferred_element_type=F32)
    keys = rotate(
        dot(normed_all, key_weight).reshape(seqs, rows, local_kv, HD), cosine, sine
    ).astype(BF16)
    values = dot(normed_all, value_weight).astype(BF16)
    queries = rotate(
        dot(normed_all, query_weight).reshape(seqs, rows, local_heads, HD), cosine, sine
    ).astype(BF16)
    kv = jnp.concatenate(
        [keys.reshape(seqs, rows, local_kv * HD), values.reshape(seqs, rows, local_kv * HD)], 0
    )
    kv_all = ctx_gather(kv, 2).reshape(2, seqs, length, local_kv, HD)
    keys_all, values_all = kv_all[0], kv_all[1]
    grouped = queries.reshape(seqs, rows, local_kv, group, HD)

    raw = ein("srkgd,sukd->skgru", grouped, keys_all)
    tanh = jnp.tanh(raw * (scale / CAP))
    exps = jnp.where(allowed[:, None, None], jnp.exp(CAP * tanh), 0.0)
    total = jnp.sum(exps, axis=-1)
    exps_low = exps.astype(BF16)
    attn = ein("skgru,sukd->srkgd", exps_low, values_all)
    total_rows = jnp.transpose(total, (0, 3, 1, 2))[..., None]
    attn = attn / total_rows
    attn_rows = attn.astype(BF16).reshape(all_rows, local_heads * HD)
    part = dot(attn_rows, output_weight).astype(BF16)

    def by_owner(value):
        return value.reshape(seqs, slots, tp_count, stretch_rows, width)

    ffw_all, branch, resid = tp_exchange(
        "middle",
        3,
        mid_rows,
        [mine, wide(attn_out_gain), wide(ffw_in_gain)],
        [f32_rows, f32_rows],
        by_owner(part),
    )
    ffw_all = ffw_all.reshape(all_rows, width)
    gate = dot(ffw_all, gate_weight)
    up = dot(ffw_all, up_weight)
    mixed, mixed_back = jax.vjp(gelu_times, gate, up)
    mixed = mixed.astype(BF16)
    part = dot(mixed, down_weight).astype(BF16)
    ffw_grad_all, layer_out, ffw_out_gain_part = tp_exchange(
        "turn",
        4,
        turn_rows,
        [resid, upstream, wide(ffw_out_gain)],
        [jax.ShapeDtypeStruct(own, BF16), gain_shape],
        by_owner(part),
    )
    ffw_grad_all = ffw_grad_all.reshape(all_rows, width)
    down_part = ein("rd,rf->df", ffw_grad_all, mixed).astype(BF16)
    down_sum = halve(down_part, usual)
    mixed_grad = ein("rd,fd->rf", ffw_grad_all, down_weight)
    gate_grad, up_grad = mixed_back(mixed_grad)
    gate_grad = gate_grad.astype(BF16)
    up_grad = up_grad.astype(BF16)
    gate_part = ein("rd,rf->df", ffw_all, gate_grad).astype(BF16)
    gate_sum = halve(gate_part, usual)
    up_part = ein("rd,rf->df", ffw_all, up_grad).astype(BF16)
    cut = up_part.shape[1] // 2
    up_sum = jnp.concatenate(
        [halve(up_part[:, :cut], other), halve(up_part[:, cut:], usual)], 1
    )
    part = (
        ein("rf,df->rd", gate_grad, gate_weight) + ein("rf,df->rd", up_grad, up_weight)
    ).astype(BF16)
    branch_grad_all, resid_grad, ffw_in_gain_part, attn_out_gain_part = tp_exchange(
        "middle_back",
        5,
        mid_back_rows,
        [resid, branch, upstream, wide(ffw_in_gain), wide(attn_out_gain)],
        [f32_rows, gain_shape, gain_shape],
        by_owner(part),
    )
    branch_grad_all = branch_grad_all.reshape(all_rows, width)
    output_part = ein("rd,rh->dh", branch_grad_all, attn_rows).astype(BF16)
    output_sum = halve(output_part, other)
    attn_grad = ein("rd,hd->rh", branch_grad_all, output_weight).reshape(attn.shape)
    row_dot = jnp.sum(attn_grad * attn, axis=-1)
    scaled = (attn_grad / total_rows).astype(BF16)
    shift = jnp.transpose(row_dot, (0, 2, 3, 1)) / total
    weight_grad = ein("srkgd,sukd->skgru", scaled, values_all)
    score_grad = (
        exps * (weight_grad - shift[..., None]) * (scale * (1.0 - tanh * tanh))
    ).astype(BF16)
    query_acc = ein("skgru,sukd->srkgd", score_grad, keys_all)
    key_acc = ein("skgru,srkgd->sukd", score_grad, grouped)
    value_acc = ein("skgru,srkgd->sukd", exps_low, scaled)
    kv_acc = jnp.concatenate([key_acc, value_acc], 0).astype(BF16)
    kv_sum = ctx_scatter(kv_acc.reshape(2 * seqs, ctx_count, rows, local_kv * HD), 6)
    key_grad = rotate(kv_sum[:seqs].reshape(seqs, rows, local_kv, HD), cosine, -sine)
    key_grad = key_grad.astype(BF16).reshape(all_rows, local_kv * HD)
    value_grad = kv_sum[seqs:].astype(BF16).reshape(all_rows, local_kv * HD)
    query_grad = rotate(query_acc.reshape(seqs, rows, local_heads, HD), cosine, -sine)
    query_grad = query_grad.astype(BF16).reshape(all_rows, local_heads * HD)
    qkv_grad = jnp.concatenate([query_grad, key_grad, value_grad], 1)
    qkv_weight = jnp.concatenate([query_weight, key_weight, value_weight], 1)
    part = ein("rh,dh->rd", qkv_grad, qkv_weight).astype(BF16)
    qkv_part = ein("rd,rh->dh", normed_all, qkv_grad).astype(BF16)
    qkv_sum = halve(qkv_part, usual)
    tokens_grad, attn_in_gain_part = tp_exchange(
        "leave",
        7,
        leave_rows,
        [mine, resid_grad, wide(attn_in_gain)],
        [f32_rows, gain_shape],
        by_owner(part),
        gather=False,
    )
    gains = jnp.concatenate(
        [attn_in_gain_part, attn_out_gain_part, ffw_in_gain_part, ffw_out_gain_part], 0
    )
    gains = lax.psum(gains, ("ctx", "tp"))
    share = width // ctx_count
    gains = lax.dynamic_slice_in_dim(gains, ctx_rank * share, share, 1)
    heads_end = local_heads * HD
    keys_end = heads_end + local_kv * HD
    return (
        jnp.transpose(layer_out, (2, 0, 1, 3)),
        jnp.transpose(tokens_grad, (2, 0, 1, 3)),
        gains[0],
        qkv_sum[:, :heads_end],
        qkv_sum[:, heads_end:keys_end],
        qkv_sum[:, keys_end:],
        output_sum.T,
        gains[1],
        gains[2],
        gate_sum,
        up_sum,
        down_sum.T,
        gains[3],
    )


def solution(mesh):
    placed = (
        P("tp", None, "ctx", None),
        P(),
        P(),
        P(None, "tp"),
        P(None, "tp"),
        P(None, "tp"),
        P("tp", None),
        P(),
        P(),
        P(None, "tp"),
        P(None, "tp"),
        P("tp", None),
        P(),
        P("tp", None, "ctx", None),
    )
    return jax.shard_map(
        body,
        mesh=mesh,
        in_specs=placed,
        out_specs=(
            P("tp", None, "ctx", None),
            P("tp", None, "ctx", None),
            P("ctx"),
            P("ctx", "tp"),
            P("ctx", "tp"),
            P("ctx", "tp"),
            P("tp", "ctx"),
            P("ctx"),
            P("ctx"),
            P("ctx", "tp"),
            P("ctx", "tp"),
            P("tp", "ctx"),
            P("ctx"),
        ),
        check_vma=False,
    )
```

time: 1670 us -> 1080 us (0.65)
  waiting for transfers between devices: 1250 us -> 394 us
  Pallas kernels: 0 us -> 305 us
  matrix products: 206 us -> 158 us
  local copies, waits for them, and re-layouts: 67.3 us -> 106 us
  other arithmetic: 75.5 us -> 53.6 us
    reduce_scatter x13 -> x0, waiting for transfers between devices: 1070 us -> none  [the longest x1 181 us: body(): lax.psum_scatter(gate_part.astype(jnp.bfloat16), 'ctx', scatter_dimension...]
    ppermute x0 -> x18, waiting for transfers between devices: none -> 394 us  [halve(): got = lax.ppermute(give, 'ctx', [(i, i ^ 1 << b) for i in range(count)])]
    pallas_call x0 -> x7, Pallas kernels: none -> 305 us  [the longest x5 156 us: tp_exchange(): pl.pallas_call(functools.partial(tp_kernel, fn, count, items, len(ins), l...]
    all_gather x6 -> x0, waiting for transfers between devices: 180 us -> none  [the longest x1 52.5 us: body(): lax.all_gather(values_local, 'ctx', axis=1, tiled=True)]
    dot_general x35 -> x23, matrix products: 206 us -> 158 us  [the longest x1 18.5 us: body(): mixed_grad = ein('rd,fd->rf', ffw_grad_all, down_weight)]
    unnamed x1 -> x0, blocking collectives: 37.1 us -> none
    dynamic_slice x5 -> x12, local copies, waits for them, and re-layouts: 1.08 us -> 37 us  [the longest x5 21.9 us: halve(): keep = lax.dynamic_index_in_dim(total, mine, axis, keepdims=False)]
    psum x1, blocking collectives: 6.68 us -> 41 us  [body(): gains = lax.psum(gains, ('ctx', 'tp'))]
  transfers between devices with their start and end apart: 19 -> 18, of which waited for: 19 -> 8; matrix products, arithmetic and copies ran while one was open for 8% -> 17% of each run, Pallas kernels for 0% -> 10%
where the time goes in v1:
time: 1080 us; the launch traced here: 1070 us
  waiting for transfers between devices  394 us (36%)
  Pallas kernels  305 us (28%)
  matrix products  158 us (15%)
  local copies, waits for them, and re-layouts  106 us (10%)
  other arithmetic  53.6 us (5%)
  blocking collectives  41 us (4%)
  starting transfers between devices  11.1 us (1%)
    ppermute x18, waiting for transfers between devices, halve(): got = lax.ppermute(give, 'ctx', [(i, i ^ 1 << b) for i in range(count)])  394 us
    pallas_call x5, Pallas kernels, tp_exchange(): pl.pallas_call(functools.partial(tp_kernel, fn, count, items, len(ins), l...  156 us
    pallas_call x1, Pallas kernels, ctx_scatter(): pl.pallas_call(functools.partial(ctx_scatter_kernel, count, items), out_s...  84 us
    pallas_call x1, Pallas kernels, ctx_gather(): pl.pallas_call(functools.partial(ctx_gather_kernel, count, items), out_sh...  64.5 us
    psum x1, blocking collectives, body(): gains = lax.psum(gains, ('ctx', 'tp'))  41 us
    convert_element_type x12, other arithmetic, halve(): total = total.astype(BF16)  27.3 us
    dynamic_slice x5, local copies, waits for them, and re-layouts, halve(): keep = lax.dynamic_index_in_dim(total, mine, axis, keepdims=False)  21.9 us
  transfers between devices with their start and end apart: 18, of which 8 were waited for; matrix products, arithmetic and copies ran while one was open for 17% of the time, Pallas kernels for 10%

profile of v1, /device:TPU:0, one launch (start us, length us, event | category | flops | bytes accessed | tf_op | source)
XLA Modules:
  0.0 1071.3 jit_solution(9267990027385206201)
XLA Ops:
  9.9 4.3 copy.136
  14.1 2.0 fusion.64
  16.1 21.6 %enter.1 = bf16[5,2,4,16,2304]{4,3,2,1,0:T(8,128)(2,1)S(1)} custom-call(bf16[5,2,16,2304]{3,2,1,0:T(8,128)(2,1)S(1)} %bitcast.310, bf16[1,2304]{1,0:T(2,128)(2,1)S(1)} %reshape.414.refs_1_.refs_3_), custom_call_target="tpu_custom_call" | custom-call | tf_op jit(solution)/shard_map/enter/pallas_call | solution.py:159
  42.0 64.5 %ctx_gather.1 = bf16[10,8,128,256]{3,2,1,0:T(8,128)(2,1)} custom-call(bf16[10,128,256]{2,1,0:T(8,128)(2,1)} %pad_maximum_fusion.3.block), custom_call_target="tpu_custom_call" | custom-call | tf_op jit(solution)/shard_map/ctx_gather/pallas_call | solution.py:221
  106.5 3.3 fusion.75
  113.6 3.3 fusion.77
  117.0 3.4 copy.92
  123.3 37.3 %middle.1 = (bf16[5,2,4,16,2304]{4,3,2,1,0:T(8,128)(2,1)S(1)}, f32[5,2,16,2304]{3,2,1,0:T(8,128)S(1)}, f32[5,2,16,2304]{3,2,1,0:T(8,128)S(1)}) custom-call(bf16[5,2,4,16,2304]{4,3,2,1,0:T(8,128)(2,1)S(1)} %bitcast.315, bf16[5,2,16,2304]{3,2,1,0:T(8,128)(2,1)S(1)} %bitcast.311, bf16[1,2304]{1,0:T(2,128)(2,1)S(1)} %reshape.422.refs_2_.refs_5_, ...), custom_call_target="tpu_custom_call" | custom-call | tf_op jit(solution)/shard_map/middle/pallas_call | solution.py:159
  160.6 13.2 %fusion.79 = f32[640,2304]{1,0:T(8,128)} fusion(bf16[640,2304]{1,0:T(8,128)(2,1)S(1)} %bitcast.325, bf16[2304,2304]{1,0:T(8,128)(2,1)} %param.23), kind=kOutput, calls=%fused_computation.193 | convolution fusion | flops 6794772480 | bytes 19464192 | tf_op jit(solution)/shard_map/dot_general | solution.py:497
  173.9 14.1 %multiply_convert_fusion.1 = (bf16[640,2304]{1,0:T(8,128)(2,1)}, f32[640,2304]{1,0:T(8,128)}) fusion(f32[640,2304]{1,0:T(8,128)} %fusion.79, bf16[640,2304]{1,0:T(8,128)(2,1)S(1)} %bitcast.326, bf16[2304,2304]{1,0:T(8,128)(2,1)} %param.24), kind=kOutput, calls=%fused_computation.18 | convolution fusion | flops 6809518080 | bytes 28311552 | tf_op jit(solution)/shard_map/dot_general | solution.py:498
  188.0 8.8 convolution_convert_fusion.4
  196.9 37.9 %turn.1 = (bf16[5,2,4,16,2304]{4,3,2,1,0:T(8,128)(2,1)S(1)}, bf16[5,2,16,2304]{3,2,1,0:T(8,128)(2,1)S(1)}, f32[1,2304]{1,0:T(1,128)S(1)}) custom-call(bf16[5,2,4,16,2304]{4,3,2,1,0:T(8,128)(2,1)S(1)} %bitcast.322, f32[5,2,16,2304]{3,2,1,0:T(8,128)S(1)} %get-tuple-element.26.refs_1_, bf16[5,2,16,2304]{3,2,1,0:T(8,128)(2,1)S(1)} %bitcast.313, ...), custom_call_target="tpu_custom_call" | custom-call | tf_op jit(solution)/shard_map/turn/pallas_call | solution.py:159
  235.6 18.5 %multiply_convert_fusion = (bf16[640,2304]{1,0:T(8,128)(2,1)}, bf16[640,2304]{1,0:T(8,128)(2,1)}) fusion(f32[640,2304]{1,0:T(8,128)} %fusion.79, f32[640,2304]{1,0:T(8,128)} %get-tuple-element.118, bf16[640,2304]{1,0:T(8,128)(2,1)S(1)} %bitcast.329, bf16[2304,2304]{1,0:T(8,128)(2,1)} %param.25), kind=kOutput, calls=%fused_computation.17 | convolution fusion | flops 6830161920 | bytes 31260672 | tf_op jit(solution)/shard_map/rd,fd->rf/dot_general | solution.py:513
  254.1 13.4 %fusion.80 = f32[640,2304]{1,0:T(8,128)} fusion(bf16[640,2304]{1,0:T(8,128)(2,1)} %get-tuple-element.81, bf16[2304,2304]{1,0:T(8,128)(2,1)} %param.23), kind=kOutput, calls=%fused_computation.194 | convolution fusion | flops 6794772480 | bytes 19464192 | tf_op jit(solution)/shard_map/rf,df->rd/dot_general | solution.py:525
  267.5 12.9 %add_convert_fusion = bf16[640,2304]{1,0:T(8,128)(2,1)S(1)} fusion(f32[640,2304]{1,0:T(8,128)} %fusion.80, bf16[640,2304]{1,0:T(8,128)(2,1)} %get-tuple-element.80, bf16[2304,2304]{1,0:T(8,128)(2,1)} %param.24), kind=kOutput, calls=%fused_computation.16 | convolution fusion | flops 6797721600 | bytes 22413312 | tf_op jit(solution)/shard_map/rf,df->rd/dot_general | solution.py:525
  280.4 39.5 %middle_back.1 = (bf16[5,2,4,16,2304]{4,3,2,1,0:T(8,128)(2,1)}, f32[5,2,16,2304]{3,2,1,0:T(8,128)S(1)}, f32[1,2304]{1,0:T(1,128)S(1)}, f32[1,2304]{1,0:T(1,128)S(1)}) custom-call(bf16[5,2,4,16,2304]{4,3,2,1,0:T(8,128)(2,1)S(1)} %bitcast.321, f32[5,2,16,2304]{3,2,1,0:T(8,128)S(1)} %get-tuple-element.26.refs_1_, ...), custom_call_target="tpu_custom_call" | custom-call | tf_op jit(solution)/shard_map/middle_back/pallas_call | solution.py:159
  321.0 5.3 convolution_convert_fusion.7
  326.3 2.9 constant_dynamic-slice_fusion.10
  330.3 4.6 fusion.81
  334.9 2.1 reshape.431
  337.0 3.0 reshape.430
  339.9 3.3 copy.94
  343.2 2.1 copy.96
  345.3 1.8 multiply_reduce_fusion
  347.2 6.4 fusion.28
  353.6 5.1 fusion.13
  359.9 2.4 fusion.27
  362.3 4.4 copy.103
  366.7 4.4 copy.105
  371.0 5.3 pad_maximum_fusion.part
  376.3 84.0 %ctx_scatter.1 = f32[10,128,256]{2,1,0:T(8,128)} custom-call(bf16[10,8,128,256]{3,2,1,0:T(8,128)(2,1)} %pad_maximum_fusion.part), custom_call_target="tpu_custom_call" | custom-call | tf_op jit(solution)/shard_map/ctx_scatter/pallas_call | solution.py:284
  466.9 6.3 convolution_convert_fusion.3
  473.2 1.9 constant_dynamic-slice_fusion.12
  478.0 11.0 %convolution_convert_fusion.1 = bf16[2304,2304]{1,0:T(8,128)(2,1)} fusion(bf16[640,2304]{1,0:T(8,128)(2,1)S(1)} %bitcast.327, bf16[640,2304]{1,0:T(8,128)(2,1)S(1)} %copy-done.62), kind=kOutput, calls=%fused_computation.1 | convolution fusion | flops 6800080896 | bytes 16515072 | tf_op jit(solution)/shard_map/rd,rf->df/dot_general | solution.py:519
  489.1 8.8 fusion.74
  497.9 4.6 constant_dynamic-slice_fusion.4
  505.0 1.9 constant_dynamic-slice_fusion.6
  509.9 9.0 convolution_convert_fusion
  519.0 10.9 %convolution_convert_fusion.2 = bf16[2304,2304]{1,0:T(8,128)(2,1)} fusion(bf16[640,2304]{1,0:T(8,128)(2,1)S(1)} %bitcast.328, bf16[640,2304]{1,0:T(8,128)(2,1)S(1)} %copy-done.61), kind=kOutput, calls=%fused_computation.2 | convolution fusion | flops 6800080896 | bytes 16515072 | tf_op jit(solution)/shard_map/rd,rf->df/dot_general | solution.py:517
  529.9 10.6 constant_dynamic-slice_fusion.2
  540.5 2.7 copy.174
  549.2 5.0 convolution_convert_fusion.6
  557.4 20.2 %leave.1 = (f32[5,2,16,2304]{3,2,1,0:T(8,128)S(1)}, f32[1,2304]{1,0:T(1,128)S(1)}) custom-call(bf16[5,2,4,16,2304]{4,3,2,1,0:T(8,128)(2,1)S(1)} %bitcast.320, bf16[5,2,16,2304]{3,2,1,0:T(8,128)(2,1)S(1)} %bitcast.312, f32[5,2,16,2304]{3,2,1,0:T(8,128)S(1)} %copy-done.6, bf16[1,2304]{1,0:T(2,128)(2,1)S(1)} %copy-done.10), custom_call_target="tpu_custom_call" | custom-call | tf_op jit(solution)/shard_map/leave/pallas_call | solution.py:159
  577.6 2.2 copy.119
  579.9 5.4 copy.173
  585.2 126.7 %collective-permute-done.4 = bf16[2,288,512]{2,1,0:T(8,128)(2,1)} collective-permute-done((bf16[2,288,512]{2,1,0:T(8,128)(2,1)}, bf16[2,288,512]{2,1,0:T(8,128)(2,1)}, u32[]{:S(2)}, u32[]{:S(2)}) %collective-permute-start.4) | collective-permute-done | bytes 589856 | tf_op jit(solution)/shard_map/ppermute | solution.py:314
  713.3 41.0 %psum.7 = f32[4,2304]{1,0:T(4,128)S(1)} all-reduce(f32[4,2304]{1,0:T(4,128)S(1)} %pad_maximum_fusion.10), channel_id=1, replica_groups=mesh['ctx'=8,'tp'=4] {'ctx','tp'}, use_global_device_ids=true, to_apply=%region_3.4 | all-reduce | flops 9216 | bytes 73728 | tf_op jit(solution)/shard_map/psum | solution.py:573
  755.0 2.3 collective-permute-start.15
  758.2 3.6 fusion.22
  762.0 2.4 fusion.10
  764.6 2.1 collective-permute-start.13
  766.6 2.6 fusion.11
  770.4 20.5 %collective-permute-done.1 = bf16[2,288,1024]{2,1,0:T(8,128)(2,1)S(1)} collective-permute-done((bf16[2,288,1024]{2,1,0:T(8,128)(2,1)S(1)}, bf16[2,288,1024]{2,1,0:T(8,128)(2,1)S(1)}, u32[]{:S(2)}, u32[]{:S(2)}) %collective-permute-start.1) | collective-permute-done | bytes 1179680 | tf_op jit(solution)/shard_map/ppermute | solution.py:314
  792.6 36.7 %collective-permute-done.13 = bf16[2,288,1152]{2,1,0:T(8,128)(2,1)S(1)} collective-permute-done((bf16[2,288,1152]{2,1,0:T(8,128)(2,1)S(1)}, bf16[2,288,1152]{2,1,0:T(8,128)(2,1)S(1)}, u32[]{:S(2)}, u32[]{:S(2)}) %collective-permute-start.13) | collective-permute-done | bytes 1327136 | tf_op jit(solution)/shard_map/ppermute | solution.py:314
  829.9 6.4 fusion.1
  836.3 3.4 dynamic-slice_bitcast_fusion.1
  839.7 1.9 collective-permute-start.7
  841.6 31.3 %collective-permute-done.15 = bf16[2,2,288,2304]{3,2,0,1:T(8,128)(2,1)} collective-permute-done((bf16[2,2,288,2304]{3,2,0,1:T(8,128)(2,1)}, bf16[2,2,288,2304]{3,2,0,1:T(8,128)(2,1)}, u32[]{:S(2)}, u32[]{:S(2)}) %collective-permute-start.15) | collective-permute-done | bytes 5308448 | tf_op jit(solution)/shard_map/ppermute | solution.py:314
  873.0 3.9 fusion
  877.1 22.2 %collective-permute-done.10 = bf16[2,288,1152]{2,1,0:T(8,128)(2,1)} collective-permute-done((bf16[2,288,1152]{2,1,0:T(8,128)(2,1)}, bf16[2,288,1152]{2,1,0:T(8,128)(2,1)}, u32[]{:S(2)}, u32[]{:S(2)}) %collective-permute-start.10) | collective-permute-done | bytes 1327136 | tf_op jit(solution)/shard_map/ppermute | solution.py:314
  905.5 22.7 %collective-permute-done.7 = bf16[2,288,2304]{2,1,0:T(8,128)(2,1)} collective-permute-done((bf16[2,288,2304]{2,1,0:T(8,128)(2,1)}, bf16[2,288,2304]{2,1,0:T(8,128)(2,1)}, u32[]{:S(2)}, u32[]{:S(2)}) %collective-permute-start.7) | collective-permute-done | bytes 2654240 | tf_op jit(solution)/shard_map/ppermute | solution.py:314
  928.2 2.4 fusion.12
  930.8 79.8 %collective-permute-done.16 = bf16[2,288,2304]{2,1,0:T(8,128)(2,1)S(1)} collective-permute-done((bf16[2,288,2304]{2,1,0:T(8,128)(2,1)S(1)}, bf16[2,288,2304]{2,1,0:T(8,128)(2,1)S(1)}, u32[]{:S(2)}, u32[]{:S(2)}) %collective-permute-start.16) | collective-permute-done | bytes 2654240 | tf_op jit(solution)/shard_map/ppermute | solution.py:314
  1015.3 53.7 %collective-permute-done.17 = bf16[288,2304]{1,0:T(8,128)(2,1)S(1)} collective-permute-done((bf16[288,2304]{1,0:T(8,128)(2,1)S(1)}, bf16[288,2304]{1,0:T(8,128)(2,1)S(1)}, u32[]{:S(2)}, u32[]{:S(2)}) %collective-permute-start.17) | collective-permute-done | bytes 1327136 | tf_op jit(solution)/shard_map/ppermute | solution.py:314
  (248 shorter events, 67.8 us)
Async XLA Ops:
  0.6 120.9 %copy-start = (bf16[512,2304]{1,0:T(8,128)(2,1)S(1)}, bf16[512,2304]{1,0:T(8,128)(2,1)}, u32[]{:S(2)}) copy-start(bf16[512,2304]{1,0:T(8,128)(2,1)} %param.20) | copy-start | bytes 7077892
  0.7 38.0 %copy-start.53 = (f32[128]{0:T(128)}, f32[128]{0:T(128)S(1)}, u32[]{:S(2)}) copy-start(f32[128]{0:T(128)S(1)} %multiply_power_fusion) | copy-start | bytes 1540
  3.2 5.7 copy-start.40
  4.0 12.1 %copy-start.9 = (bf16[1,2304]{1,0:T(2,128)(2,1)}, bf16[1,2304]{1,0:T(2,128)(2,1)S(1)}, u32[]{:S(2)}) copy-start(bf16[1,2304]{1,0:T(2,128)(2,1)S(1)} %reshape.414.refs_1_.refs_3_) | copy-start | bytes 13828
  6.1 32.6 %copy-start.51 = (f32[5,128]{1,0:T(8,128)}, f32[5,128]{1,0:T(8,128)S(1)}, u32[]{:S(2)}) copy-start(f32[5,128]{1,0:T(8,128)S(1)} %subtract_convert_fusion.2) | copy-start | bytes 7684
  14.1 23.6 %copy-start.57 = (bf16[2304,256]{1,0:T(8,128)(2,1)S(1)}, bf16[2304,256]{1,0:T(8,128)(2,1)}, u32[]{:S(2)}) copy-start(bf16[2304,256]{1,0:T(8,128)(2,1)} %param.18) | copy-start | bytes 3538948
  16.1 95.5 %copy-start.29 = (f32[5,128,128]{2,1,0:T(8,128)}, f32[5,128,128]{2,1,0:T(8,128)S(1)}, u32[]{:S(2)}) copy-start(f32[5,128,128]{2,1,0:T(8,128)S(1)} %get-tuple-element.112) | copy-start | bytes 983044
  37.7 72.2 %copy-start.3 = (bf16[5,2,4,16,2304]{4,3,2,1,0:T(8,128)(2,1)}, bf16[5,2,4,16,2304]{4,3,2,1,0:T(8,128)(2,1)S(1)}, u32[]{:S(2)}) copy-start(bf16[5,2,4,16,2304]{4,3,2,1,0:T(8,128)(2,1)S(1)} %enter.1) | copy-start | bytes 8847364
  160.6 13.3 %copy-start.11 = (bf16[5,2,4,16,2304]{4,3,2,1,0:T(8,128)(2,1)}, bf16[5,2,4,16,2304]{4,3,2,1,0:T(8,128)(2,1)S(1)}, u32[]{:S(2)}) copy-start(bf16[5,2,4,16,2304]{4,3,2,1,0:T(8,128)(2,1)S(1)} %get-tuple-element.25) | copy-start | bytes 8847364
  160.6 27.4 %slice-start.8 = ((s8[10616832]{0:T(1024)(128)(4,1)}), s8[4194304]{0:T(1024)(128)(4,1)S(1)}, s32[]{:S(2)}) async-start(s8[10616832]{0:T(1024)(128)(4,1)} %bitcast.370), calls=%async_computation.8 | async-start | bytes 8388608
  160.6 27.4 %slice-start.9 = ((s8[10616832]{0:T(1024)(128)(4,1)}), s8[4194304]{0:T(1024)(128)(4,1)S(1)}, s32[]{:S(2)}) async-start(s8[10616832]{0:T(1024)(128)(4,1)} %bitcast.370), calls=%async_computation.9 | async-start | bytes 8388608
  173.9 14.1 %slice-start.10 = ((s8[10616832]{0:T(1024)(128)(4,1)}), s8[2228224]{0:T(1024)(128)(4,1)S(1)}, s32[]{:S(2)}) async-start(s8[10616832]{0:T(1024)(128)(4,1)} %bitcast.370), calls=%async_computation.10 | async-start | bytes 4456448
  188.0 8.9 copy-start.2
  235.6 18.5 %copy-start.14 = (bf16[5,2,4,16,2304]{4,3,2,1,0:T(8,128)(2,1)}, bf16[5,2,4,16,2304]{4,3,2,1,0:T(8,128)(2,1)S(1)}, u32[]{:S(2)}) copy-start(bf16[5,2,4,16,2304]{4,3,2,1,0:T(8,128)(2,1)S(1)} %get-tuple-element.28) | copy-start | bytes 8847364
  280.4 40.6 %copy-start.46 = (bf16[80,8,2,256]{3,1,2,0:T(8,128)(2,1)S(1)}, bf16[80,8,2,256]{3,1,2,0:T(8,128)(2,1)}, u32[]{:S(2)}) copy-start(bf16[80,8,2,256]{3,1,2,0:T(8,128)(2,1)} %copy-done.45) | copy-start | bytes 1966084
  330.3 214.2 %collective-permute-start.3 = (bf16[2,2,288,512]{3,2,0,1:T(8,128)(2,1)}, bf16[2,2,288,512]{3,2,0,1:T(8,128)(2,1)}, u32[]{:S(2)}, u32[]{:S(2)}) collective-permute-start(bf16[2,2,288,512]{3,2,0,1:T(8,128)(2,1)} %bitcast.307), channel_id=1, source_target_pairs={{0,8},{4,12},{8,0},{12,4},{16,24},{20,28},{24,16},{28,20},{1,9},{5... | collective-permute-start | bytes 3538952 | tf_op jit(solution)/shard_map/ppermute | solution.py:314
  347.2 6.4 copy-start.32
  347.2 6.4 copy-start.39
  353.6 5.1 copy-start.21
  376.3 87.0 %copy-start.30 = (f32[5,128,128]{2,1,0:T(8,128)S(1)}, f32[5,128,128]{2,1,0:T(8,128)}, u32[]{:S(2)}) copy-start(f32[5,128,128]{2,1,0:T(8,128)} %copy-done.29) | copy-start | bytes 983044
  465.4 7.8 copy-start.43
  466.9 6.3 copy-start.49
  476.8 281.4 %collective-permute-start = (bf16[2,2,288,1024]{3,2,0,1:T(8,128)(2,1)}, bf16[2,2,288,1024]{3,2,0,1:T(8,128)(2,1)}, u32[]{:S(2)}, u32[]{:S(2)}) collective-permute-start(bf16[2,2,288,1024]{3,2,0,1:T(8,128)(2,1)} %bitcast.306), channel_id=1, source_target_pairs={{0,4},{4,0},{8,12},{12,8},{16,20},{20,16},{24,28},{28,24},{1,5},{5... | collective-permute-start | bytes 7077896 | tf_op jit(solution)/shard_map/ppermute | solution.py:314
  497.9 7.1 slice-start.6
  497.9 7.1 slice-start.7
  504.2 257.8 %collective-permute-start.12 = (bf16[2,2,288,1152]{3,2,0,1:T(8,128)(2,1)}, bf16[2,2,288,1152]{3,2,0,1:T(8,128)(2,1)}, u32[]{:S(2)}, u32[]{:S(2)}) collective-permute-start(bf16[2,2,288,1152]{3,2,0,1:T(8,128)(2,1)} %bitcast.304), channel_id=1, source_target_pairs={{0,4},{4,0},{8,12},{12,8},{16,20},{20,16},{24,28},{28,24},{1,5},{5... | collective-permute-start | bytes 7962632 | tf_op jit(solution)/shard_map/ppermute | solution.py:314
  508.6 10.3 copy-start.13
  508.6 10.4 copy-start.61
  508.6 258.0 %collective-permute-start.9 = (bf16[2,2,288,1152]{3,2,0,1:T(8,128)(2,1)}, bf16[2,2,288,1152]{3,2,0,1:T(8,128)(2,1)}, u32[]{:S(2)}, u32[]{:S(2)}) collective-permute-start(bf16[2,2,288,1152]{3,2,0,1:T(8,128)(2,1)} %bitcast.305), channel_id=1, source_target_pairs={{0,8},{4,12},{8,0},{12,4},{16,24},{20,28},{24,16},{28,20},{1,9},{5... | collective-permute-start | bytes 7962632 | tf_op jit(solution)/shard_map/ppermute | solution.py:314
  540.4 8.7 copy-start.58
  543.1 6.0 copy-start.33
  543.1 6.0 copy-start.44
  543.1 6.0 copy-start.48
  543.1 6.0 copy-start.50
  543.1 6.0 copy-start.56
  543.2 286.7 %collective-permute-start.6 = (bf16[2,2,288,2304]{3,2,0,1:T(8,128)(2,1)}, bf16[2,2,288,2304]{3,2,0,1:T(8,128)(2,1)}, u32[]{:S(2)}, u32[]{:S(2)}) collective-permute-start(bf16[2,2,288,2304]{3,2,0,1:T(8,128)(2,1)} %bitcast.303), channel_id=1, source_target_pairs={{0,4},{4,0},{8,12},{12,8},{16,20},{20,16},{24,28},{28,24},{1,5},{5... | collective-permute-start | bytes 15925256 | tf_op jit(solution)/shard_map/ppermute | solution.py:314
  548.0 6.1 copy-start.8
  548.0 7.6 copy-start.6
  548.0 7.6 copy-start.10
  548.0 163.9 %collective-permute-start.4 = (bf16[2,288,512]{2,1,0:T(8,128)(2,1)}, bf16[2,288,512]{2,1,0:T(8,128)(2,1)}, u32[]{:S(2)}, u32[]{:S(2)}) collective-permute-start(bf16[2,288,512]{2,1,0:T(8,128)(2,1)} %dynamic-slice_bitcast_fusion.9), channel_id=1, source_target_pairs={{0,4},{4,0},{8,12},{12,8},{16,20},{20,16},{24,28},{28,24},{1,5},{5... | collective-permute-start | bytes 1769480 | tf_op jit(solution)/shard_map/ppermute | solution.py:314
  579.9 132.0 %copy-start.26 = (bf16[2,2,288,512]{3,2,0,1:T(8,128)(2,1)S(1)}, bf16[2,2,288,512]{3,2,0,1:T(8,128)(2,1)}, u32[]{:S(2)}) copy-start(bf16[2,2,288,512]{3,2,0,1:T(8,128)(2,1)} %copy-done.25) | copy-start | bytes 3538948
  713.2 41.8 %collective-permute-start.5 = (bf16[288,512]{1,0:T(8,128)(2,1)S(1)}, bf16[288,512]{1,0:T(8,128)(2,1)S(1)}, u32[]{:S(2)}, u32[]{:S(2)}) collective-permute-start(bf16[288,512]{1,0:T(8,128)(2,1)S(1)} %dynamic-slice_bitcast_fusion.11), channel_id=1, source_target_pairs={{0,16},{4,20},{8,24},{12,28},{16,0},{20,4},{24,8},{28,12},{1,17},{... | collective-permute-start | bytes 884744 | tf_op jit(solution)/shard_map/ppermute | solution.py:314
  755.0 118.0 %collective-permute-start.15 = (bf16[2,2,288,2304]{3,2,0,1:T(8,128)(2,1)}, bf16[2,2,288,2304]{3,2,0,1:T(8,128)(2,1)}, u32[]{:S(2)}, u32[]{:S(2)}) collective-permute-start(bf16[2,2,288,2304]{3,2,0,1:T(8,128)(2,1)} %bitcast.347), channel_id=1, source_target_pairs={{0,4},{4,0},{8,12},{12,8},{16,20},{20,16},{24,28},{28,24},{1,5},{5... | collective-permute-start | bytes 15925256 | tf_op jit(solution)/shard_map/ppermute | solution.py:314
  761.9 29.0 %collective-permute-start.1 = (bf16[2,288,1024]{2,1,0:T(8,128)(2,1)S(1)}, bf16[2,288,1024]{2,1,0:T(8,128)(2,1)S(1)}, u32[]{:S(2)}, u32[]{:S(2)}) collective-permute-start(bf16[2,288,1024]{2,1,0:T(8,128)(2,1)S(1)} %dynamic-slice_bitcast_fusion.6), channel_id=1, source_target_pairs={{0,8},{4,12},{8,0},{12,4},{16,24},{20,28},{24,16},{28,20},{1,9},{5... | collective-permute-start | bytes 3538952 | tf_op jit(solution)/shard_map/ppermute | solution.py:314
  764.6 64.8 %collective-permute-start.13 = (bf16[2,288,1152]{2,1,0:T(8,128)(2,1)S(1)}, bf16[2,288,1152]{2,1,0:T(8,128)(2,1)S(1)}, u32[]{:S(2)}, u32[]{:S(2)}) collective-permute-start(bf16[2,288,1152]{2,1,0:T(8,128)(2,1)S(1)} %dynamic-slice_bitcast_fusion.3), channel_id=1, source_target_pairs={{0,8},{4,12},{8,0},{12,4},{16,24},{20,28},{24,16},{28,20},{1,9},{5... | collective-permute-start | bytes 3981320 | tf_op jit(solution)/shard_map/ppermute | solution.py:314
  766.6 63.2 %slice-start.2 = ((s8[5308416]{0:T(1024)(128)(4,1)}), s8[4194304]{0:T(1024)(128)(4,1)S(1)}, s32[]{:S(2)}) async-start(s8[5308416]{0:T(1024)(128)(4,1)} %bitcast.333), calls=%async_computation.2 | async-start | bytes 8388608
  769.2 22.2 %copy-start.18 = (bf16[2,2,288,1152]{3,2,0,1:T(8,128)(2,1)}, bf16[2,2,288,1152]{3,2,0,1:T(8,128)(2,1)S(1)}, u32[]{:S(2)}) copy-start(bf16[2,2,288,1152]{3,2,0,1:T(8,128)(2,1)S(1)} %fusion.11) | copy-start | bytes 7962628
  769.2 60.7 %slice-start.3 = ((s8[5308416]{0:T(1024)(128)(4,1)}), s8[1114112]{0:T(1024)(128)(4,1)S(1)}, s32[]{:S(2)}) async-start(s8[5308416]{0:T(1024)(128)(4,1)} %bitcast.333), calls=%async_computation.3 | async-start | bytes 2228224
  770.4 128.9 %collective-permute-start.10 = (bf16[2,288,1152]{2,1,0:T(8,128)(2,1)}, bf16[2,288,1152]{2,1,0:T(8,128)(2,1)}, u32[]{:S(2)}, u32[]{:S(2)}) collective-permute-start(bf16[2,288,1152]{2,1,0:T(8,128)(2,1)} %dynamic-slice_bitcast_fusion.4), channel_id=1, source_target_pairs={{0,4},{4,0},{8,12},{12,8},{16,20},{20,16},{24,28},{28,24},{1,5},{5... | collective-permute-start | bytes 3981320 | tf_op jit(solution)/shard_map/ppermute | solution.py:314
  792.3 108.9 %collective-permute-start.2 = (bf16[288,1024]{1,0:T(8,128)(2,1)}, bf16[288,1024]{1,0:T(8,128)(2,1)}, u32[]{:S(2)}, u32[]{:S(2)}) collective-permute-start(bf16[288,1024]{1,0:T(8,128)(2,1)} %dynamic-slice_bitcast_fusion.10), channel_id=1, source_target_pairs={{0,16},{4,20},{8,24},{12,28},{16,0},{20,4},{24,8},{28,12},{1,17},{... | collective-permute-start | bytes 1769480 | tf_op jit(solution)/shard_map/ppermute | solution.py:314
  829.7 6.6 copy-start.22
  829.7 74.5 %collective-permute-start.14 = (bf16[288,1152]{1,0:T(8,128)(2,1)S(1)}, bf16[288,1152]{1,0:T(8,128)(2,1)}, u32[]{:S(2)}, u32[]{:S(2)}) collective-permute-start(bf16[288,1152]{1,0:T(8,128)(2,1)S(1)} %dynamic-slice_bitcast_fusion.7), channel_id=1, source_target_pairs={{0,16},{4,20},{8,24},{12,28},{16,0},{20,4},{24,8},{28,12},{1,17},{... | collective-permute-start | bytes 1990664 | tf_op jit(solution)/shard_map/ppermute | solution.py:314
  829.8 43.1 %slice-start = ((s8[5308416]{0:T(1024)(128)(4,1)}), s8[4194304]{0:T(1024)(128)(4,1)S(1)}, s32[]{:S(2)}) async-start(s8[5308416]{0:T(1024)(128)(4,1)} %bitcast.331), calls=%async_computation | async-start | bytes 8388608
  829.9 43.1 %slice-start.1 = ((s8[5308416]{0:T(1024)(128)(4,1)}), s8[1114112]{0:T(1024)(128)(4,1)S(1)}, s32[]{:S(2)}) async-start(s8[5308416]{0:T(1024)(128)(4,1)} %bitcast.331), calls=%async_computation.1 | async-start | bytes 2228224
  839.7 88.5 %collective-permute-start.7 = (bf16[2,288,2304]{2,1,0:T(8,128)(2,1)}, bf16[2,288,2304]{2,1,0:T(8,128)(2,1)}, u32[]{:S(2)}, u32[]{:S(2)}) collective-permute-start(bf16[2,288,2304]{2,1,0:T(8,128)(2,1)} %dynamic-slice_bitcast_fusion.1), channel_id=1, source_target_pairs={{0,8},{4,12},{8,0},{12,4},{16,24},{20,28},{24,16},{28,20},{1,9},{5... | collective-permute-start | bytes 7962632 | tf_op jit(solution)/shard_map/ppermute | solution.py:314
  873.0 26.4 %copy-start.19 = (bf16[2,2,288,1152]{3,2,0,1:T(8,128)(2,1)S(1)}, bf16[2,2,288,1152]{3,2,0,1:T(8,128)(2,1)}, u32[]{:S(2)}) copy-start(bf16[2,2,288,1152]{3,2,0,1:T(8,128)(2,1)} %copy-done.18) | copy-start | bytes 7962628
  876.8 51.4 %slice-start.4 = ((s8[5308416]{0:T(1024)(128)(4,1)}), s8[4194304]{0:T(1024)(128)(4,1)S(1)}, s32[]{:S(2)}) async-start(s8[5308416]{0:T(1024)(128)(4,1)} %bitcast.335), calls=%async_computation.4 | async-start | bytes 8388608
  877.0 24.2 %copy-start.28 = (bf16[2,288,1024]{2,1,0:T(8,128)(2,1)S(1)}, bf16[2,288,1024]{2,1,0:T(8,128)(2,1)}, u32[]{:S(2)}) copy-start(bf16[2,288,1024]{2,1,0:T(8,128)(2,1)} %copy-done.27) | copy-start | bytes 3538948
  877.1 51.2 %slice-start.5 = ((s8[5308416]{0:T(1024)(128)(4,1)}), s8[1114112]{0:T(1024)(128)(4,1)S(1)}, s32[]{:S(2)}) async-start(s8[5308416]{0:T(1024)(128)(4,1)} %bitcast.335), calls=%async_computation.5 | async-start | bytes 2228224
  877.1 133.6 %collective-permute-start.16 = (bf16[2,288,2304]{2,1,0:T(8,128)(2,1)S(1)}, bf16[2,288,2304]{2,1,0:T(8,128)(2,1)S(1)}, u32[]{:S(2)}, u32[]{:S(2)}) collective-permute-start(bf16[2,288,2304]{2,1,0:T(8,128)(2,1)S(1)} %dynamic-slice_bitcast_fusion), channel_id=1, source_target_pairs={{0,8},{4,12},{8,0},{12,4},{16,24},{20,28},{24,16},{28,20},{1,9},{5... | collective-permute-start | bytes 7962632 | tf_op jit(solution)/shard_map/ppermute | solution.py:314
  901.0 110.7 %collective-permute-start.11 = (bf16[288,1152]{1,0:T(8,128)(2,1)S(1)}, bf16[288,1152]{1,0:T(8,128)(2,1)S(1)}, u32[]{:S(2)}, u32[]{:S(2)}) collective-permute-start(bf16[288,1152]{1,0:T(8,128)(2,1)S(1)} %dynamic-slice_bitcast_fusion.8), channel_id=1, source_target_pairs={{0,16},{4,20},{8,24},{12,28},{16,0},{20,4},{24,8},{28,12},{1,17},{... | collective-permute-start | bytes 1990664 | tf_op jit(solution)/shard_map/ppermute | solution.py:314
  930.8 82.8 %collective-permute-start.8 = (bf16[288,2304]{1,0:T(8,128)(2,1)S(1)}, bf16[288,2304]{1,0:T(8,128)(2,1)S(1)}, u32[]{:S(2)}, u32[]{:S(2)}) collective-permute-start(bf16[288,2304]{1,0:T(8,128)(2,1)S(1)} %dynamic-slice_bitcast_fusion.5), channel_id=1, source_target_pairs={{0,16},{4,20},{8,24},{12,28},{16,0},{20,4},{24,8},{28,12},{1,17},{... | collective-permute-start | bytes 3981320 | tf_op jit(solution)/shard_map/ppermute | solution.py:314
  1011.4 57.6 %collective-permute-start.17 = (bf16[288,2304]{1,0:T(8,128)(2,1)S(1)}, bf16[288,2304]{1,0:T(8,128)(2,1)S(1)}, u32[]{:S(2)}, u32[]{:S(2)}) collective-permute-start(bf16[288,2304]{1,0:T(8,128)(2,1)S(1)} %dynamic-slice_bitcast_fusion.2), channel_id=1, source_target_pairs={{0,16},{4,20},{8,24},{12,28},{16,0},{20,4},{24,8},{28,12},{1,17},{... | collective-permute-start | bytes 3981320 | tf_op jit(solution)/shard_map/ppermute | solution.py:314
  1013.6 57.3 %copy-start.1 = (bf16[512,2304]{1,0:T(8,128)(2,1)S(1)}, bf16[512,2304]{1,0:T(8,128)(2,1)}, u32[]{:S(2)}) copy-start(bf16[512,2304]{1,0:T(8,128)(2,1)} %param.20) | copy-start | bytes 7077892
  (28 other events, 67.9 us)

commit v2 on v1

--- a/solution.py
+++ b/solution.py
@@ -141,6 +141,10 @@
                     rs_copy(item, step, sub).wait_send()
 
 
+def takes(us):
+    return pl.CostEstimate(flops=int(us * 1.1e9), bytes_accessed=0, transcendentals=0)
+
+
 def tp_exchange(name, cid, fn, ins, outs, part=None, gather=True):
     count = lax.axis_size("tp")
     rows_shape = ins[0].shape
@@ -167,6 +171,7 @@
         compiler_params=pltpu.CompilerParams(
             collective_id=cid, has_side_effects=True, vmem_limit_bytes=40 * MIB
         ),
+        cost_estimate=takes(18 * (scatter + gather)),
         name=name,
     )(*args)
 
@@ -227,6 +232,7 @@
         compiler_params=pltpu.CompilerParams(
             collective_id=cid, has_side_effects=True, vmem_limit_bytes=56 * MIB
         ),
+        cost_estimate=takes(55),
         name="ctx_gather",
     )(block)
 
@@ -295,27 +301,171 @@
         compiler_params=pltpu.CompilerParams(
             collective_id=cid, has_side_effects=True, vmem_limit_bytes=56 * MIB
         ),
+        cost_estimate=takes(60),
         name="ctx_scatter",
     )(part)
 
 
-def halve(part, order):
-    count = lax.axis_size("ctx")
+class Halving:
+    def __init__(self, part, order):
+        count = lax.axis_size("ctx")
+        steps = count.bit_length() - 1
+        self.order = list(order)
+        self.left = list(range(steps))[::-1]
+        self.total = part.reshape((2,) * steps + (part.shape[0] // count, part.shape[1]))
+
+    def send(self):
+        b = self.order.pop(0)
+        axis = self.left.index(b)
+        self.left.remove(b)
+        mine = (lax.axis_index("ctx") >> b) & 1
+        pick = functools.partial(lax.dynamic_index_in_dim, axis=axis, keepdims=False)
+        pairs = [(i, i ^ (1 << b)) for i in range(lax.axis_size("ctx"))]
+        self.got = lax.ppermute(pick(self.total, 1 - mine), "ctx", pairs)
+        self.keep = pick(self.total, mine)
+
+    def add(self):
+        self.total = self.keep.astype(F32) + self.got.astype(F32)
+        if self.order:
+            self.total = self.total.astype(BF16)
+
+    def finish(self):
+        self.add()
+        while self.order:
+            self.send()
+            self.add()
+        return self.total
+
+
+def pin(value, *halvings):
+    value, gots = lax.optimization_barrier((value, [h.got for h in halvings]))
+    for h, got in zip(halvings, gots):
+        h.got = got
+    return value
+
+
+def cube_order(steps, turn):
+    usual = list(range(steps))
+    return usual if turn == 0 or steps < 2 else [1, 0] + usual[2:]
+
+
+def weights_scatter_kernel(count, tp_count, plan, n_parts, *refs):
+    refs = list(refs)
+    parts = [refs.pop(0) for _ in range(n_parts)]
+    gains = refs.pop(0)
+    outs = [refs.pop(0) for _ in range(n_parts)]
+    gains_out = refs.pop(0)
+    landed = [refs.pop(0) for _ in range(n_parts)]
+    sendbuf = [refs.pop(0) for _ in range(n_parts)]
+    gains_landed, gains_send = refs.pop(0), refs.pop(0)
+    sems = (refs.pop(0), refs.pop(0))
+    gain_sems = (refs.pop(0), refs.pop(0))
+    me = lax.axis_index("ctx")
+    me_tp = lax.axis_index("tp")
     steps = count.bit_length() - 1
-    me = lax.axis_index("ctx")
-    left = list(range(steps))[::-1]
-    total = part.reshape((2,) * steps + (part.shape[0] // count, part.shape[1]))
-    for at, b in enumerate(order):
-        axis = left.index(b)
-        left.remove(b)
-        mine = (me >> b) & 1
-        give = lax.dynamic_index_in_dim(total, 1 - mine, axis, keepdims=False)
-        keep = lax.dynamic_index_in_dim(total, mine, axis, keepdims=False)
-        got = lax.ppermute(give, "ctx", [(i, i ^ (1 << b)) for i in range(count)])
-        total = keep.astype(F32) + got.astype(F32)
-        if at < steps - 1:
-            total = total.astype(BF16)
-    return total
+    tp_steps = tp_count.bit_length() - 1
+    barrier = pltpu.get_barrier_semaphore()
+    for b in range(steps):
+        pl.semaphore_signal(
+            barrier, inc=1, device_id={"ctx": flipped(me, 1 << b)}, device_id_type=MESH
+        )
+    for b in range(tp_steps):
+        pl.semaphore_signal(
+            barrier, inc=1, device_id={"tp": flipped(me_tp, 1 << b)}, device_id_type=MESH
+        )
+    pl.semaphore_wait(barrier, steps + tp_steps)
+
+    def subs(order, step):
+        return submasks(order[step + 1 :])
+
+    def copy(n, step, sub):
+        p, item, order = plan[n]
+        bit = 1 << order[step]
+        mask = bit | sub
+        if step == 0:
+            src = parts[p].at[flipped(me, mask), item]
+        else:
+            src = sendbuf[p].at[without(mask, order[0]), item]
+        return remote(
+            "ctx", src, landed[p].at[mask, item], sems, (n, mask), flipped(me, bit)
+        )
+
+    def total_of(n, mask, upto):
+        p, item, order = plan[n]
+        total = parts[p][flipped(me, mask), item].astype(F32)
+        for step in range(upto):
+            total = total + landed[p][1 << order[step] | mask, item].astype(F32)
+        return total
+
+    for n, (_, _, order) in enumerate(plan):
+        for sub in subs(order, 0):
+            copy(n, 0, sub).start()
+
+    gains_send[0] = gains[...]
+    for step in range(tp_steps + steps):
+        axis, bit, at = ("tp", step, me_tp) if step < tp_steps else ("ctx", step - tp_steps, me)
+        go = remote(
+            axis,
+            gains_send.at[step],
+            gains_landed.at[step],
+            gain_sems,
+            step,
+            flipped(at, 1 << bit),
+        )
+        go.start()
+        go.wait_recv()
+        both = gains_send[step] + gains_landed[step]
+        if step + 1 < tp_steps + steps:
+            gains_send[step + 1] = both
+        else:
+            gains_out[...] = both
+        go.wait_send()
+
+    for step in range(1, steps):
+        for n, (p, item, order) in enumerate(plan):
+            for sub in subs(order, step - 1):
+                copy(n, step - 1, sub).wait_recv()
+            for sub in subs(order, step):
+                mask = 1 << order[step] | sub
+                sendbuf[p][without(mask, order[0]), item] = total_of(n, mask, step).astype(BF16)
+                copy(n, step, sub).start()
+    for n, (p, item, order) in enumerate(plan):
+        for sub in subs(order, steps - 1):
+            copy(n, steps - 1, sub).wait_recv()
+        outs[p][item] = total_of(n, 0, steps)
+    for step in range(steps):
+        for n, (_, _, order) in enumerate(plan):
+            for sub in subs(order, step):
+                copy(n, step, sub).wait_send()
+
+
+def weights_scatter(parts, gains, cid):
+    count, tp_count = lax.axis_size("ctx"), lax.axis_size("tp")
+    steps = count.bit_length() - 1
+    rows = parts[0].shape[0] // count
+    cut = max(c for c in range(1, 7) if rows % (16 * c) == 0) if rows % 16 == 0 else 1
+    blocks = [p.reshape(count, cut, rows // cut, p.shape[1]) for p in parts]
+    pairs = [(p, item) for item in range(cut) for p in range(len(parts))]
+    plan = [(p, item, cube_order(steps, int(n % 4 == 3))) for n, (p, item) in enumerate(pairs)]
+    hops = steps + tp_count.bit_length() - 1
+    dma = pltpu.SemaphoreType.DMA((len(plan), count))
+    out = pl.pallas_call(
+        functools.partial(weights_scatter_kernel, count, tp_count, plan, len(parts)),
+        out_shape=[jax.ShapeDtypeStruct(b.shape[1:], F32) for b in blocks]
+        + [jax.ShapeDtypeStruct(gains.shape, F32)],
+        in_specs=[pl.BlockSpec(memory_space=VMEM)] * (len(parts) + 1),
+        out_specs=[pl.BlockSpec(memory_space=VMEM)] * (len(parts) + 1),
+        scratch_shapes=[VMEM(b.shape, BF16) for b in blocks]
+        + [VMEM((max(count // 2, 1),) + b.shape[1:], BF16) for b in blocks]
+        + [VMEM((hops,) + gains.shape, F32)] * 2
+        + [dma, dma, pltpu.SemaphoreType.DMA((hops,)), pltpu.SemaphoreType.DMA((hops,))],
+        compiler_params=pltpu.CompilerParams(
+            collective_id=cid, has_side_effects=True, vmem_limit_bytes=56 * MIB
+        ),
+        cost_estimate=takes(180),
+        name="weights_scatter",
+    )(*blocks, gains)
+    return [o.reshape(rows, o.shape[-1]) for o in out[:-1]], out[-1]
 
 
 def inv_rms(v):
@@ -419,8 +569,7 @@
     scale = HD ** (-0.5)
     own = (seqs, slots, stretch_rows, width)
     steps = ctx_count.bit_length() - 1
-    usual = list(range(steps))
-    other = usual if steps < 2 else [1, 0] + usual[2:]
+    usual, other = cube_order(steps, 0), cube_order(steps, 1)
 
     slot_stretch = jnp.stack([ctx_rank, 2 * ctx_count - 1 - ctx_rank])
     iota = jnp.arange(stretch, dtype=jnp.int32)
@@ -509,18 +658,19 @@
     )
     ffw_grad_all = ffw_grad_all.reshape(all_rows, width)
     down_part = ein("rd,rf->df", ffw_grad_all, mixed).astype(BF16)
-    down_sum = halve(down_part, usual)
+    ff_cut = down_part.shape[1] * 2 // 3
+    down = [Halving(down_part[:, :ff_cut], usual), Halving(down_part[:, ff_cut:], other)]
+    for h in down:
+        h.send()
     mixed_grad = ein("rd,fd->rf", ffw_grad_all, down_weight)
     gate_grad, up_grad = mixed_back(mixed_grad)
     gate_grad = gate_grad.astype(BF16)
     up_grad = up_grad.astype(BF16)
     gate_part = ein("rd,rf->df", ffw_all, gate_grad).astype(BF16)
-    gate_sum = halve(gate_part, usual)
+    gates = [Halving(gate_part[:, :ff_cut], usual), Halving(gate_part[:, ff_cut:], other)]
+    for h in gates:
+        h.send()
     up_part = ein("rd,rf->df", ffw_all, up_grad).astype(BF16)
-    cut = up_part.shape[1] // 2
-    up_sum = jnp.concatenate(
-        [halve(up_part[:, :cut], other), halve(up_part[:, cut:], usual)], 1
-    )
     part = (
         ein("rf,df->rd", gate_grad, gate_weight) + ein("rf,df->rd", up_grad, up_weight)
     ).astype(BF16)
@@ -532,9 +682,11 @@
         [f32_rows, gain_shape, gain_shape],
         by_owner(part),
     )
-    branch_grad_all = branch_grad_all.reshape(all_rows, width)
+    branch_grad_all = pin(branch_grad_all.reshape(all_rows, width), *down)
+    for h in down:
+        h.add()
+        h.send()
     output_part = ein("rd,rh->dh", branch_grad_all, attn_rows).astype(BF16)
-    output_sum = halve(output_part, other)
     attn_grad = ein("rd,hd->rh", branch_grad_all, output_weight).reshape(attn.shape)
     row_dot = jnp.sum(attn_grad * attn, axis=-1)
     scaled = (attn_grad / total_rows).astype(BF16)
@@ -548,6 +700,10 @@
     value_acc = ein("skgru,srkgd->sukd", exps_low, scaled)
     kv_acc = jnp.concatenate([key_acc, value_acc], 0).astype(BF16)
     kv_sum = ctx_scatter(kv_acc.reshape(2 * seqs, ctx_count, rows, local_kv * HD), 6)
+    kv_sum = pin(kv_sum, *down, *gates)
+    for h in down + gates:
+        h.add()
+        h.send()
     key_grad = rotate(kv_sum[:seqs].reshape(seqs, rows, local_kv, HD), cosine, -sine)
     key_grad = key_grad.astype(BF16).reshape(all_rows, local_kv * HD)
     value_grad = kv_sum[seqs:].astype(BF16).reshape(all_rows, local_kv * HD)
@@ -557,7 +713,6 @@
     qkv_weight = jnp.concatenate([query_weight, key_weight, value_weight], 1)
     part = ein("rh,dh->rd", qkv_grad, qkv_weight).astype(BF16)
     qkv_part = ein("rd,rh->dh", normed_all, qkv_grad).astype(BF16)
-    qkv_sum = halve(qkv_part, usual)
     tokens_grad, attn_in_gain_part = tp_exchange(
         "leave",
         7,
@@ -570,7 +725,15 @@
     gains = jnp.concatenate(
         [attn_in_gain_part, attn_out_gain_part, ffw_in_gain_part, ffw_out_gain_part], 0
     )
-    gains = lax.psum(gains, ("ctx", "tp"))
+    gains = pin(gains, *gates)
+    for h in gates:
+        h.add()
+        h.send()
+    (up_sum, output_sum, qkv_sum), gains = weights_scatter(
+        [up_part, output_part, qkv_part], gains, 8
+    )
+    down_sum = jnp.concatenate([h.finish() for h in down], 1)
+    gate_sum = jnp.concatenate([h.finish() for h in gates], 1)
     share = width // ctx_count
     gains = lax.dynamic_slice_in_dim(gains, ctx_rank * share, share, 1)
     heads_end = local_heads * HD

time: 1080 us -> 954 us (0.88)
  waiting for transfers between devices: 394 us -> 38.3 us
  Pallas kernels: 305 us -> 590 us
  blocking collectives: 41 us -> 0 us
  other arithmetic: 53.6 us -> 36.3 us
    ppermute x18 -> x12, waiting for transfers between devices: 394 us -> 38.3 us  [send(): self.got = lax.ppermute(pick(self.total, 1 - mine), 'ctx', pairs)]
    pallas_call x0 -> x1, Pallas kernels: none -> 281 us  [weights_scatter(): pl.pallas_call(functools.partial(weights_scatter_kernel, count, tp_count,...]
    psum x1 -> x0, blocking collectives: 41 us -> none  [body(): gains = lax.psum(gains, ('ctx', 'tp'))]
    dynamic_slice x11 -> x8, local copies, waits for them, and re-layouts: 36 us -> 20.3 us  [the longest x4 13 us: send(): self.keep = pick(self.total, mine)]
    unnamed x154 -> x162, local copies, waits for them, and re-layouts: 14.2 us -> 27 us
    convert_element_type x12 -> x8, other arithmetic: 27.3 us -> 15.6 us  [add(): self.total = self.total.astype(BF16)]
  transfers between devices with their start and end apart: 18 -> 12, of which waited for: 8 -> 3; matrix products, arithmetic and copies ran while one was open for 17% -> 18% of each run, Pallas kernels for 10% -> 45%
where the time goes in v2:
time: 954 us; the launch traced here: 945 us
  Pallas kernels  590 us (62%)
  matrix products  159 us (17%)
  local copies, waits for them, and re-layouts  105 us (11%)
  waiting for transfers between devices  38.3 us (4%)
  other arithmetic  36.3 us (4%)
  starting transfers between devices  14.6 us (2%)
    pallas_call x1, Pallas kernels, weights_scatter(): pl.pallas_call(functools.partial(weights_scatter_kernel, count, tp_count,...  281 us
    pallas_call x5, Pallas kernels, tp_exchange(): pl.pallas_call(functools.partial(tp_kernel, fn, count, items, len(ins), l...  155 us
    pallas_call x1, Pallas kernels, ctx_scatter(): pl.pallas_call(functools.partial(ctx_scatter_kernel, count, items), out_s...  89 us
    pallas_call x1, Pallas kernels, ctx_gather(): pl.pallas_call(functools.partial(ctx_gather_kernel, count, items), out_sh...  64.5 us
    ppermute x12, waiting for transfers between devices, send(): self.got = lax.ppermute(pick(self.total, 1 - mine), 'ctx', pairs)  38.3 us
    unnamed x162, local copies, waits for them, and re-layouts  27 us
  transfers between devices with their start and end apart: 12, of which 3 were waited for; matrix products, arithmetic and copies ran while one was open for 18% of the time, Pallas kernels for 45%

profile of v2, /device:TPU:0, one launch (start us, length us, event | category | flops | bytes accessed | tf_op | source)
XLA Modules:
  0.0 944.7 jit_solution(7166188737578239576)
XLA Ops:
  9.9 4.3 copy.124
  14.2 2.0 fusion.58
  16.1 21.6 %enter.1 = bf16[5,2,4,16,2304]{4,3,2,1,0:T(8,128)(2,1)S(1)} custom-call(bf16[5,2,16,2304]{3,2,1,0:T(8,128)(2,1)S(1)} %bitcast.279, bf16[1,2304]{1,0:T(2,128)(2,1)S(1)} %reshape.414.refs_1_.refs_3_), custom_call_target="tpu_custom_call" | custom-call | flops 19800000512 | tf_op jit(solution)/shard_map/enter/pallas_call | solution.py:163
  42.0 64.5 %ctx_gather.1 = bf16[10,8,128,256]{3,2,1,0:T(8,128)(2,1)} custom-call(bf16[10,128,256]{2,1,0:T(8,128)(2,1)} %pad_maximum_fusion.3.block), custom_call_target="tpu_custom_call" | custom-call | flops 60500000768 | tf_op jit(solution)/shard_map/ctx_gather/pallas_call | solution.py:226
  106.6 3.3 fusion.68
  113.6 3.4 fusion.70
  117.0 3.1 copy.84
  123.1 37.3 %middle.1 = (bf16[5,2,4,16,2304]{4,3,2,1,0:T(8,128)(2,1)S(1)}, f32[5,2,16,2304]{3,2,1,0:T(8,128)S(1)}, f32[5,2,16,2304]{3,2,1,0:T(8,128)S(1)}) custom-call(bf16[5,2,4,16,2304]{4,3,2,1,0:T(8,128)(2,1)S(1)} %bitcast.300, bf16[5,2,16,2304]{3,2,1,0:T(8,128)(2,1)S(1)} %bitcast.280, bf16[1,2304]{1,0:T(2,128)(2,1)S(1)} %reshape.422.refs_2_.refs_5_, ...), custom_call_target="tpu_custom_call" | custom-call | flops 39600001024 | tf_op jit(solution)/shard_map/middle/pallas_call | solution.py:163
  160.5 14.2 %fusion.72 = f32[640,2304]{1,0:T(8,128)} fusion(bf16[640,2304]{1,0:T(8,128)(2,1)S(1)} %bitcast.289, bf16[2304,2304]{1,0:T(8,128)(2,1)} %param.23), kind=kOutput, calls=%fused_computation.169 | convolution fusion | flops 6794772480 | bytes 19464192 | tf_op jit(solution)/shard_map/dot_general | solution.py:646
  174.7 14.1 %multiply_convert_fusion.1 = (bf16[640,2304]{1,0:T(8,128)(2,1)}, f32[640,2304]{1,0:T(8,128)}) fusion(f32[640,2304]{1,0:T(8,128)} %fusion.72, bf16[640,2304]{1,0:T(8,128)(2,1)S(1)} %bitcast.290, bf16[2304,2304]{1,0:T(8,128)(2,1)} %param.24), kind=kOutput, calls=%fused_computation.18 | convolution fusion | flops 6809518080 | bytes 28311552 | tf_op jit(solution)/shard_map/dot_general | solution.py:647
  188.9 8.9 convolution_convert_fusion.4
  197.8 37.9 %turn.1 = (bf16[5,2,4,16,2304]{4,3,2,1,0:T(8,128)(2,1)S(1)}, bf16[5,2,16,2304]{3,2,1,0:T(8,128)(2,1)S(1)}, f32[1,2304]{1,0:T(1,128)S(1)}) custom-call(bf16[5,2,4,16,2304]{4,3,2,1,0:T(8,128)(2,1)S(1)} %bitcast.299, f32[5,2,16,2304]{3,2,1,0:T(8,128)S(1)} %get-tuple-element.41.refs_1_, bf16[5,2,16,2304]{3,2,1,0:T(8,128)(2,1)S(1)} %bitcast.282, ...), custom_call_target="tpu_custom_call" | custom-call | flops 39600001024 | tf_op jit(solution)/shard_map/turn/pallas_call | solution.py:163
  235.7 12.1 %convolution_convert_fusion.2 = bf16[2304,2304]{1,0:T(8,128)(2,1)S(1)} fusion(bf16[640,2304]{1,0:T(8,128)(2,1)S(1)} %bitcast.295, bf16[640,2304]{1,0:T(8,128)(2,1)} %get-tuple-element.141), kind=kOutput, calls=%fused_computation.2 | convolution fusion | flops 6800080896 | bytes 16515072 | tf_op jit(solution)/shard_map/rd,rf->df/dot_general | solution.py:660
  247.8 4.0 copy-done.32
  251.8 2.0 slice.100
  253.9 3.4 constant_dynamic-slice_fusion.5
  258.6 6.3 slice.99
  265.0 5.3 constant_dynamic-slice_fusion.6
  270.3 2.0 copy.152
  273.4 17.6 %multiply_convert_fusion = (bf16[640,2304]{1,0:T(8,128)(2,1)}, bf16[640,2304]{1,0:T(8,128)(2,1)}) fusion(f32[640,2304]{1,0:T(8,128)} %fusion.72, f32[640,2304]{1,0:T(8,128)} %get-tuple-element.142, bf16[640,2304]{1,0:T(8,128)(2,1)S(1)} %bitcast.296, bf16[2304,2304]{1,0:T(8,128)(2,1)} %param.25), kind=kOutput, calls=%fused_computation.17 | convolution fusion | flops 6830161920 | bytes 31260672 | tf_op jit(solution)/shard_map/rd,fd->rf/dot_general | solution.py:665
  291.0 11.2 %convolution_convert_fusion.1 = bf16[2304,2304]{1,0:T(8,128)(2,1)S(1)} fusion(bf16[640,2304]{1,0:T(8,128)(2,1)S(1)} %bitcast.292, bf16[640,2304]{1,0:T(8,128)(2,1)} %get-tuple-element.111), kind=kOutput, calls=%fused_computation.1 | convolution fusion | flops 6800080896 | bytes 16515072 | tf_op jit(solution)/shard_map/rd,rf->df/dot_general | solution.py:669
  304.3 1.9 copy.153
  307.2 2.0 collective-permute-start.5
  309.3 3.0 slice-done
  312.3 2.4 constant_dynamic-slice_fusion.2
  314.7 2.1 copy.151
  317.8 12.2 %fusion.73 = f32[640,2304]{1,0:T(8,128)} fusion(bf16[640,2304]{1,0:T(8,128)(2,1)S(1)} %copy-done.73, bf16[2304,2304]{1,0:T(8,128)(2,1)} %param.23), kind=kOutput, calls=%fused_computation.170 | convolution fusion | flops 6794772480 | bytes 19464192 | tf_op jit(solution)/shard_map/rf,df->rd/dot_general | solution.py:675
  330.0 13.0 %add_convert_fusion = bf16[640,2304]{1,0:T(8,128)(2,1)S(1)} fusion(f32[640,2304]{1,0:T(8,128)} %fusion.73, bf16[640,2304]{1,0:T(8,128)(2,1)} %get-tuple-element.110, bf16[2304,2304]{1,0:T(8,128)(2,1)} %param.24), kind=kOutput, calls=%fused_computation.16 | convolution fusion | flops 6797721600 | bytes 22413312 | tf_op jit(solution)/shard_map/rf,df->rd/dot_general | solution.py:675
  344.4 37.6 %middle_back.1 = (bf16[5,2,4,16,2304]{4,3,2,1,0:T(8,128)(2,1)S(1)}, f32[5,2,16,2304]{3,2,1,0:T(8,128)S(1)}, f32[1,2304]{1,0:T(1,128)S(1)}, f32[1,2304]{1,0:T(1,128)S(1)}) custom-call(bf16[5,2,4,16,2304]{4,3,2,1,0:T(8,128)(2,1)S(1)} %bitcast.298, f32[5,2,16,2304]{3,2,1,0:T(8,128)S(1)} %copy-done.25, f32[5,2,16,2304]{3,2,1,0:T(8,128)S(1)} %copy-done.23, ...), custom_call_target="tpu_custom_call" | custom-call | flops 39600001024 | tf_op jit(solution)/shard_map/middle_back/pallas_call | solution.py:163
  384.7 2.5 copy.106
  387.3 13.5 %convolution_convert_fusion = bf16[2304,2304]{1,0:T(8,128)(2,1)} fusion(bf16[640,2304]{1,0:T(8,128)(2,1)} %bitcast.291, bf16[640,2304]{1,0:T(8,128)(2,1)} %get-tuple-element.110), kind=kOutput, calls=%fused_computation | convolution fusion | flops 6800080896 | bytes 16515072 | tf_op jit(solution)/shard_map/rd,rf->df/dot_general | solution.py:673
  400.8 2.8 fusion.74
  403.6 3.1 reshape.433
  406.6 1.9 reshape.432
  408.5 2.4 fusion.21
  412.8 3.3 copy.88
  416.0 3.7 copy.90
  419.7 1.9 multiply_reduce_fusion
  421.6 6.5 fusion.24
  428.1 4.6 fusion.9
  434.3 2.4 fusion.23
  436.7 4.4 copy.97
  441.1 4.4 copy.99
  445.5 4.2 fusion.1
  453.9 2.7 pad_maximum_fusion.part
  456.6 89.0 %ctx_scatter.1 = f32[10,128,256]{2,1,0:T(8,128)} custom-call(bf16[10,8,128,256]{3,2,1,0:T(8,128)(2,1)} %pad_maximum_fusion.part), custom_call_target="tpu_custom_call" | custom-call | flops 65999998976 | tf_op jit(solution)/shard_map/ctx_scatter/pallas_call | solution.py:290
  545.6 2.8 fusion.33
  550.4 3.5 convolution_convert_fusion.7
  555.7 6.0 convolution_convert_fusion.3
  561.8 3.2 convolution_convert_fusion.6
  566.5 2.1 fusion.18
  568.6 3.5 collective-permute-start.11
  572.0 1.9 fusion.20
  575.9 3.0 fusion
  579.1 2.3 collective-permute-start.6
  581.4 20.3 %leave.1 = (f32[5,2,16,2304]{3,2,1,0:T(8,128)S(1)}, f32[1,2304]{1,0:T(1,128)S(1)}) custom-call(bf16[5,2,4,16,2304]{4,3,2,1,0:T(8,128)(2,1)S(1)} %bitcast.297, bf16[5,2,16,2304]{3,2,1,0:T(8,128)(2,1)S(1)} %bitcast.281, f32[5,2,16,2304]{3,2,1,0:T(8,128)S(1)} %copy-done.21, bf16[1,2304]{1,0:T(2,128)(2,1)S(1)} %copy-done.6), custom_call_target="tpu_custom_call" | custom-call | flops 19800000512 | tf_op jit(solution)/shard_map/leave/pallas_call | solution.py:163
  601.8 2.2 copy.107
  604.7 7.0 collective-permute-done.11
  611.7 17.1 %collective-permute-done.10 = bf16[288,1536]{1,0:T(8,128)(2,1)S(1)} collective-permute-done((bf16[288,1536]{1,0:T(8,128)(2,1)S(1)}, bf16[288,1536]{1,0:T(8,128)(2,1)S(1)}, u32[]{:S(2)}, u32[]{:S(2)}) %collective-permute-start.10) | collective-permute-done | bytes 884768 | tf_op jit(solution)/shard_map/ppermute | solution.py:324
  630.8 14.2 %collective-permute-done.6 = bf16[2,288,1536]{2,1,0:T(8,128)(2,1)S(1)} collective-permute-done((bf16[2,288,1536]{2,1,0:T(8,128)(2,1)S(1)}, bf16[2,288,1536]{2,1,0:T(8,128)(2,1)S(1)}, u32[]{:S(2)}, u32[]{:S(2)}) %collective-permute-start.6) | collective-permute-done | bytes 1769504 | tf_op jit(solution)/shard_map/ppermute | solution.py:324
  647.8 2.7 collective-permute-start.8
  650.6 281.2 %weights_scatter.1 = (f32[6,48,2304]{2,1,0:T(8,128)}, f32[6,48,512]{2,1,0:T(8,128)}, f32[6,48,1024]{2,1,0:T(8,128)}, f32[4,2304]{1,0:T(4,128)}) custom-call(bf16[8,6,48,2304]{3,2,1,0:T(8,128)(2,1)} %bitcast.335, bf16[8,6,48,512]{3,2,1,0:T(8,128)(2,1)} %bitcast.337, bf16[8,6,48,1024]{3,2,1,0:T(8,128)(2,1)} %bitcast.336, f32[4,2304]{1,0:T(4,128)} %pad_maximum_fusion.10.refs_3_), custom_call_target="tpu_custom_call" | custom-call | flops 198000001024 | tf_op jit(solution)/shard_map/weights_scatter/pallas_call | solution.py:452
  931.8 2.0 slice.108
  935.4 1.9 fusion.69
  (232 shorter events, 59.5 us)
Async XLA Ops:
  0.6 120.7 %copy-start = (bf16[512,2304]{1,0:T(8,128)(2,1)S(1)}, bf16[512,2304]{1,0:T(8,128)(2,1)}, u32[]{:S(2)}) copy-start(bf16[512,2304]{1,0:T(8,128)(2,1)} %param.20) | copy-start | bytes 7077892
  0.7 38.0 %copy-start.66 = (f32[128]{0:T(128)}, f32[128]{0:T(128)S(1)}, u32[]{:S(2)}) copy-start(f32[128]{0:T(128)S(1)} %multiply_power_fusion) | copy-start | bytes 1540
  3.2 5.7 copy-start.56
  4.0 12.1 %copy-start.5 = (bf16[1,2304]{1,0:T(2,128)(2,1)}, bf16[1,2304]{1,0:T(2,128)(2,1)S(1)}, u32[]{:S(2)}) copy-start(bf16[1,2304]{1,0:T(2,128)(2,1)S(1)} %reshape.414.refs_1_.refs_3_) | copy-start | bytes 13828
  4.7 118.3 %copy-start.7 = (bf16[1,2304]{1,0:T(2,128)(2,1)}, bf16[1,2304]{1,0:T(2,128)(2,1)S(1)}, u32[]{:S(2)}) copy-start(bf16[1,2304]{1,0:T(2,128)(2,1)S(1)} %reshape.422.refs_2_.refs_5_) | copy-start | bytes 13828
  5.4 117.6 %copy-start.9 = (bf16[1,2304]{1,0:T(2,128)(2,1)}, bf16[1,2304]{1,0:T(2,128)(2,1)S(1)}, u32[]{:S(2)}) copy-start(bf16[1,2304]{1,0:T(2,128)(2,1)S(1)} %reshape.423.refs_3_.refs_4_) | copy-start | bytes 13828
  6.2 32.6 %copy-start.62 = (f32[5,128]{1,0:T(8,128)}, f32[5,128]{1,0:T(8,128)S(1)}, u32[]{:S(2)}) copy-start(f32[5,128]{1,0:T(8,128)S(1)} %subtract_convert_fusion.2) | copy-start | bytes 7684
  16.1 95.5 %copy-start.42 = (f32[5,128,128]{2,1,0:T(8,128)}, f32[5,128,128]{2,1,0:T(8,128)S(1)}, u32[]{:S(2)}) copy-start(f32[5,128,128]{2,1,0:T(8,128)S(1)} %get-tuple-element.136) | copy-start | bytes 983044
  16.1 21.6 %copy-start.70 = (bf16[2304,256]{1,0:T(8,128)(2,1)S(1)}, bf16[2304,256]{1,0:T(8,128)(2,1)}, u32[]{:S(2)}) copy-start(bf16[2304,256]{1,0:T(8,128)(2,1)} %param.18) | copy-start | bytes 3538948
  37.7 72.2 %copy-start.11 = (bf16[5,2,4,16,2304]{4,3,2,1,0:T(8,128)(2,1)}, bf16[5,2,4,16,2304]{4,3,2,1,0:T(8,128)(2,1)S(1)}, u32[]{:S(2)}) copy-start(bf16[5,2,4,16,2304]{4,3,2,1,0:T(8,128)(2,1)S(1)} %enter.1) | copy-start | bytes 8847364
  106.6 3.4 copy-start.48
  109.9 3.7 copy-start.45
  113.6 3.4 copy-start.64
  113.6 3.4 copy-start.72
  160.4 14.3 %copy-start.13 = (bf16[5,2,4,16,2304]{4,3,2,1,0:T(8,128)(2,1)}, bf16[5,2,4,16,2304]{4,3,2,1,0:T(8,128)(2,1)S(1)}, u32[]{:S(2)}) copy-start(bf16[5,2,4,16,2304]{4,3,2,1,0:T(8,128)(2,1)S(1)} %get-tuple-element.40) | copy-start | bytes 8847364
  160.4 14.3 %copy-start.22 = (f32[5,2,16,2304]{3,2,1,0:T(8,128)}, f32[5,2,16,2304]{3,2,1,0:T(8,128)S(1)}, u32[]{:S(2)}) copy-start(f32[5,2,16,2304]{3,2,1,0:T(8,128)S(1)} %get-tuple-element.44.refs_2_) | copy-start | bytes 4423684
  160.4 37.3 %copy-start.24 = (f32[5,2,16,2304]{3,2,1,0:T(8,128)}, f32[5,2,16,2304]{3,2,1,0:T(8,128)S(1)}, u32[]{:S(2)}) copy-start(f32[5,2,16,2304]{3,2,1,0:T(8,128)S(1)} %get-tuple-element.41.refs_1_) | copy-start | bytes 4423684
  160.5 28.4 %slice-start.1 = ((s8[10616832]{0:T(1024)(128)(4,1)}), s8[4194304]{0:T(1024)(128)(4,1)S(1)}, s32[]{:S(2)}) async-start(s8[10616832]{0:T(1024)(128)(4,1)} %bitcast.333), calls=%async_computation.1 | async-start | bytes 8388608
  160.5 28.4 %slice-start.2 = ((s8[10616832]{0:T(1024)(128)(4,1)}), s8[4194304]{0:T(1024)(128)(4,1)S(1)}, s32[]{:S(2)}) async-start(s8[10616832]{0:T(1024)(128)(4,1)} %bitcast.333), calls=%async_computation.2 | async-start | bytes 8388608
  174.7 14.1 %slice-start.3 = ((s8[10616832]{0:T(1024)(128)(4,1)}), s8[2228224]{0:T(1024)(128)(4,1)S(1)}, s32[]{:S(2)}) async-start(s8[10616832]{0:T(1024)(128)(4,1)} %bitcast.333), calls=%async_computation.3 | async-start | bytes 4456448
  188.8 8.9 copy-start.2
  235.7 12.1 %copy-start.4 = (bf16[5,2,16,2304]{3,2,1,0:T(8,128)(2,1)}, bf16[5,2,16,2304]{3,2,1,0:T(8,128)(2,1)S(1)}, u32[]{:S(2)}) copy-start(bf16[5,2,16,2304]{3,2,1,0:T(8,128)(2,1)S(1)} %get-tuple-element.42) | copy-start | bytes 2211844
  235.7 12.1 %copy-start.18 = (bf16[5,2,4,16,2304]{4,3,2,1,0:T(8,128)(2,1)}, bf16[5,2,4,16,2304]{4,3,2,1,0:T(8,128)(2,1)S(1)}, u32[]{:S(2)}) copy-start(bf16[5,2,4,16,2304]{4,3,2,1,0:T(8,128)(2,1)S(1)} %get-tuple-element.43) | copy-start | bytes 8847364
  247.8 4.0 copy-start.32
  258.6 142.1 %collective-permute-start.1 = (bf16[2,2,288,768]{3,2,0,1:T(8,128)(2,1)}, bf16[2,2,288,768]{3,2,0,1:T(8,128)(2,1)}, u32[]{:S(2)}, u32[]{:S(2)}) collective-permute-start(bf16[2,2,288,768]{3,2,0,1:T(8,128)(2,1)} %bitcast.275), channel_id=1, source_target_pairs={{0,8},{4,12},{8,0},{12,4},{16,24},{20,28},{24,16},{28,20},{1,9},{5... | collective-permute-start | bytes 5308424 | tf_op jit(solution)/shard_map/ppermute | solution.py:324
  270.3 3.1 copy-start.19
  272.3 128.5 %collective-permute-start = (bf16[2,2,288,1536]{3,2,0,1:T(8,128)(2,1)}, bf16[2,2,288,1536]{3,2,0,1:T(8,128)(2,1)}, u32[]{:S(2)}, u32[]{:S(2)}) collective-permute-start(bf16[2,2,288,1536]{3,2,0,1:T(8,128)(2,1)} %bitcast.273), channel_id=1, source_target_pairs={{0,4},{4,0},{8,12},{12,8},{16,20},{20,16},{24,28},{28,24},{1,5},{5... | collective-permute-start | bytes 10616840 | tf_op jit(solution)/shard_map/ppermute | solution.py:324
  273.4 17.6 %copy-start.14 = (bf16[5,2,4,16,2304]{4,3,2,1,0:T(8,128)(2,1)S(1)}, bf16[5,2,4,16,2304]{4,3,2,1,0:T(8,128)(2,1)}, u32[]{:S(2)}) copy-start(bf16[5,2,4,16,2304]{4,3,2,1,0:T(8,128)(2,1)} %copy-done.13) | copy-start | bytes 8847364
  302.2 5.0 copy-start.26
  307.2 246.7 %collective-permute-start.5 = (bf16[2,2,288,768]{3,2,0,1:T(8,128)(2,1)}, bf16[2,2,288,768]{3,2,0,1:T(8,128)(2,1)}, u32[]{:S(2)}, u32[]{:S(2)}) collective-permute-start(bf16[2,2,288,768]{3,2,0,1:T(8,128)(2,1)} %bitcast.274), channel_id=1, source_target_pairs={{0,8},{4,12},{8,0},{12,4},{16,24},{20,28},{24,16},{28,20},{1,9},{5... | collective-permute-start | bytes 5308424 | tf_op jit(solution)/shard_map/ppermute | solution.py:324
  316.8 237.1 %collective-permute-start.4 = (bf16[2,2,288,1536]{3,2,0,1:T(8,128)(2,1)}, bf16[2,2,288,1536]{3,2,0,1:T(8,128)(2,1)}, u32[]{:S(2)}, u32[]{:S(2)}) collective-permute-start(bf16[2,2,288,1536]{3,2,0,1:T(8,128)(2,1)} %bitcast.272), channel_id=1, source_target_pairs={{0,4},{4,0},{8,12},{12,8},{16,20},{20,16},{24,28},{28,24},{1,5},{5... | collective-permute-start | bytes 10616840 | tf_op jit(solution)/shard_map/ppermute | solution.py:324
  330.0 13.0 %copy-start.3 = (bf16[16,5,2,2304]{3,0,2,1:T(8,128)(2,1)S(1)}, bf16[16,5,2,2304]{3,0,2,1:T(8,128)(2,1)}, u32[]{:S(2)}) copy-start(bf16[16,5,2,2304]{3,0,2,1:T(8,128)(2,1)} %copy.155) | copy-start | bytes 2211844
  330.0 13.0 %copy-start.8 = (bf16[1,2304]{1,0:T(2,128)(2,1)S(1)}, bf16[1,2304]{1,0:T(2,128)(2,1)}, u32[]{:S(2)}) copy-start(bf16[1,2304]{1,0:T(2,128)(2,1)} %copy-done.7) | copy-start | bytes 13828
  330.0 13.0 %copy-start.10 = (bf16[1,2304]{1,0:T(2,128)(2,1)S(1)}, bf16[1,2304]{1,0:T(2,128)(2,1)}, u32[]{:S(2)}) copy-start(bf16[1,2304]{1,0:T(2,128)(2,1)} %copy-done.9) | copy-start | bytes 13828
  330.0 13.0 %copy-start.23 = (f32[5,2,16,2304]{3,2,1,0:T(8,128)S(1)}, f32[5,2,16,2304]{3,2,1,0:T(8,128)}, u32[]{:S(2)}) copy-start(f32[5,2,16,2304]{3,2,1,0:T(8,128)} %copy-done.22) | copy-start | bytes 4423684
  387.3 13.5 %copy-start.16 = (bf16[5,2,4,16,2304]{4,3,2,1,0:T(8,128)(2,1)S(1)}, bf16[5,2,4,16,2304]{4,3,2,1,0:T(8,128)(2,1)}, u32[]{:S(2)}) copy-start(bf16[5,2,4,16,2304]{4,3,2,1,0:T(8,128)(2,1)} %copy-done.15) | copy-start | bytes 8847364
  411.9 142.0 %collective-permute-start.3 = (bf16[2,288,768]{2,1,0:T(8,128)(2,1)}, bf16[2,288,768]{2,1,0:T(8,128)(2,1)}, u32[]{:S(2)}, u32[]{:S(2)}) collective-permute-start(bf16[2,288,768]{2,1,0:T(8,128)(2,1)} %dynamic-slice_bitcast_fusion.5), channel_id=1, source_target_pairs={{0,4},{4,0},{8,12},{12,8},{16,20},{20,16},{24,28},{28,24},{1,5},{5... | collective-permute-start | bytes 2654216 | tf_op jit(solution)/shard_map/ppermute | solution.py:324
  416.0 5.5 copy-start.65
  421.6 6.5 copy-start.46
  421.6 6.5 copy-start.54
  421.6 6.5 copy-start.58
  428.1 6.2 copy-start.50
  428.1 6.2 copy-start.52
  445.5 7.5 copy-start.35
  452.8 101.1 %collective-permute-start.2 = (bf16[2,288,1536]{2,1,0:T(8,128)(2,1)}, bf16[2,288,1536]{2,1,0:T(8,128)(2,1)}, u32[]{:S(2)}, u32[]{:S(2)}) collective-permute-start(bf16[2,288,1536]{2,1,0:T(8,128)(2,1)} %dynamic-slice_bitcast_fusion.1), channel_id=1, source_target_pairs={{0,8},{4,12},{8,0},{12,4},{16,24},{20,28},{24,16},{28,20},{1,9},{5... | collective-permute-start | bytes 5308424 | tf_op jit(solution)/shard_map/ppermute | solution.py:324
  456.6 89.0 %copy-start.28 = (bf16[5,1,2,128,1024]{3,4,2,0,1:T(8,128)(2,1)S(1)}, bf16[5,1,2,128,1024]{3,4,2,0,1:T(8,128)(2,1)}, u32[]{:S(2)}) copy-start(bf16[5,1,2,128,1024]{3,4,2,0,1:T(8,128)(2,1)} %copy-done.27) | copy-start | bytes 7864324
  550.4 3.5 copy-start.55
  550.4 3.6 copy-start.63
  550.4 3.6 copy-start.67
  555.7 6.0 copy-start.47
  555.7 6.0 copy-start.69
  555.7 6.0 copy-start.71
  561.8 4.6 copy-start.31
  566.4 5.6 copy-start.38
  568.6 43.1 %collective-permute-start.11 = (bf16[288,768]{1,0:T(8,128)(2,1)S(1)}, bf16[288,768]{1,0:T(8,128)(2,1)S(1)}, u32[]{:S(2)}, u32[]{:S(2)}) collective-permute-start(bf16[288,768]{1,0:T(8,128)(2,1)S(1)} %dynamic-slice_bitcast_fusion.6), channel_id=1, source_target_pairs={{0,16},{4,20},{8,24},{12,28},{16,0},{20,4},{24,8},{28,12},{1,17},{... | collective-permute-start | bytes 1327112 | tf_op jit(solution)/shard_map/ppermute | solution.py:324
  574.1 54.7 %collective-permute-start.10 = (bf16[288,1536]{1,0:T(8,128)(2,1)S(1)}, bf16[288,1536]{1,0:T(8,128)(2,1)S(1)}, u32[]{:S(2)}, u32[]{:S(2)}) collective-permute-start(bf16[288,1536]{1,0:T(8,128)(2,1)S(1)} %dynamic-slice_bitcast_fusion.2), channel_id=1, source_target_pairs={{0,16},{4,20},{8,24},{12,28},{16,0},{20,4},{24,8},{28,12},{1,17},{... | collective-permute-start | bytes 2654216 | tf_op jit(solution)/shard_map/ppermute | solution.py:324
  574.2 56.6 %collective-permute-start.7 = (bf16[2,288,768]{2,1,0:T(8,128)(2,1)S(1)}, bf16[2,288,768]{2,1,0:T(8,128)(2,1)S(1)}, u32[]{:S(2)}, u32[]{:S(2)}) collective-permute-start(bf16[2,288,768]{2,1,0:T(8,128)(2,1)S(1)} %dynamic-slice_bitcast_fusion.4), channel_id=1, source_target_pairs={{0,4},{4,0},{8,12},{12,8},{16,20},{20,16},{24,28},{28,24},{1,5},{5... | collective-permute-start | bytes 2654216 | tf_op jit(solution)/shard_map/ppermute | solution.py:324
  579.1 65.9 %collective-permute-start.6 = (bf16[2,288,1536]{2,1,0:T(8,128)(2,1)S(1)}, bf16[2,288,1536]{2,1,0:T(8,128)(2,1)S(1)}, u32[]{:S(2)}, u32[]{:S(2)}) collective-permute-start(bf16[2,288,1536]{2,1,0:T(8,128)(2,1)S(1)} %dynamic-slice_bitcast_fusion), channel_id=1, source_target_pairs={{0,8},{4,12},{8,0},{12,4},{16,24},{20,28},{24,16},{28,20},{1,9},{5... | collective-permute-start | bytes 5308424 | tf_op jit(solution)/shard_map/ppermute | solution.py:324
  645.7 286.1 %copy-start.36 = (bf16[2,288,1536]{2,1,0:T(8,128)(2,1)}, bf16[2,288,1536]{2,1,0:T(8,128)(2,1)S(1)}, u32[]{:S(2)}) copy-start(bf16[2,288,1536]{2,1,0:T(8,128)(2,1)S(1)} %fusion.19) | copy-start | bytes 5308420
  646.6 290.7 %collective-permute-start.9 = (bf16[288,768]{1,0:T(8,128)(2,1)}, bf16[288,768]{1,0:T(8,128)(2,1)}, u32[]{:S(2)}, u32[]{:S(2)}) collective-permute-start(bf16[288,768]{1,0:T(8,128)(2,1)} %dynamic-slice_bitcast_fusion.7), channel_id=1, source_target_pairs={{0,16},{4,20},{8,24},{12,28},{16,0},{20,4},{24,8},{28,12},{1,17},{... | collective-permute-start | bytes 1327112 | tf_op jit(solution)/shard_map/ppermute | solution.py:324
  647.8 290.6 %collective-permute-start.8 = (bf16[288,1536]{1,0:T(8,128)(2,1)}, bf16[288,1536]{1,0:T(8,128)(2,1)}, u32[]{:S(2)}, u32[]{:S(2)}) collective-permute-start(bf16[288,1536]{1,0:T(8,128)(2,1)} %dynamic-slice_bitcast_fusion.3), channel_id=1, source_target_pairs={{0,16},{4,20},{8,24},{12,28},{16,0},{20,4},{24,8},{28,12},{1,17},{... | collective-permute-start | bytes 2654216 | tf_op jit(solution)/shard_map/ppermute | solution.py:324
  650.6 286.7 %copy-start.41 = (bf16[2,288,768]{2,1,0:T(8,128)(2,1)S(1)}, bf16[2,288,768]{2,1,0:T(8,128)(2,1)}, u32[]{:S(2)}) copy-start(bf16[2,288,768]{2,1,0:T(8,128)(2,1)} %copy-done.40) | copy-start | bytes 2654212
  931.8 6.6 copy-start.37
  939.8 3.1 copy-start.44
  (26 other events, 54.8 us)

commit v3 on v2

--- a/solution.py
+++ b/solution.py
@@ -37,6 +37,13 @@
     for b in bits:
         masks = masks + [m | 1 << b for m in masks]
     return masks
+
+
+def wavefront(items, stages, lag=2):
+    for t in range(items + (stages - 1) * lag):
+        for stage in range(stages):
+            if 0 <= t - stage * lag < items:
+                yield t - stage * lag, stage
 
 
 def greet(axis, count):
@@ -142,7 +149,7 @@
 
 
 def takes(us):
-    return pl.CostEstimate(flops=int(us * 1.1e9), bytes_accessed=0, transcendentals=0)
+    return pl.CostEstimate(flops=int(us * 1e7), bytes_accessed=0, transcendentals=0)
 
 
 def tp_exchange(name, cid, fn, ins, outs, part=None, gather=True):
@@ -206,12 +213,11 @@
     for step in range(steps):
         for item in range(items):
             copy(item, step, 0).start()
-    for got in range(steps):
-        for item in range(items):
-            for mask in masks(item, got):
-                copy(item, got, mask).wait_recv()
-                for step in range(got + 1, steps):
-                    copy(item, step, mask | 1 << orders[item][got]).start()
+    for item, got in wavefront(items, steps):
+        for mask in masks(item, got):
+            copy(item, got, mask).wait_recv()
+            for step in range(got + 1, steps):
+                copy(item, step, mask | 1 << orders[item][got]).start()
     for step in range(steps):
         for item in range(items):
             for mask in masks(item, step):
@@ -264,19 +270,18 @@
     for item in range(items):
         for sub in subs(item, 0):
             copy(item, 0, sub).start()
-    for step in range(1, steps):
-        for item in range(items):
-            for sub in subs(item, step - 1):
-                copy(item, step - 1, sub).wait_recv()
-            for sub in subs(item, step):
-                mask = 1 << orders[item][step] | sub
-                slot = without(mask, orders[item][0])
-                sendbuf[item, slot] = total_of(item, mask, step).astype(BF16)
-                copy(item, step, sub).start()
-    for item in range(items):
-        for sub in subs(item, steps - 1):
-            copy(item, steps - 1, sub).wait_recv()
-        out[item] = total_of(item, 0, steps)
+    for item, got in wavefront(items, steps):
+        for sub in subs(item, got):
+            copy(item, got, sub).wait_recv()
+        step = got + 1
+        if step == steps:
+            out[item] = total_of(item, 0, steps)
+            continue
+        for sub in subs(item, step):
+            mask = 1 << orders[item][step] | sub
+            slot = without(mask, orders[item][0])
+            sendbuf[item, slot] = total_of(item, mask, step).astype(BF16)
+            copy(item, step, sub).start()
     for step in range(steps):
         for item in range(items):
             for sub in subs(item, step):
@@ -306,13 +311,16 @@
     )(part)
 
 
+def pairs_of(b):
+    return [(i, i ^ (1 << b)) for i in range(lax.axis_size("ctx"))]
+
+
 class Halving:
     def __init__(self, part, order):
-        count = lax.axis_size("ctx")
-        steps = count.bit_length() - 1
         self.order = list(order)
-        self.left = list(range(steps))[::-1]
-        self.total = part.reshape((2,) * steps + (part.shape[0] // count, part.shape[1]))
+        self.left = sorted(order, reverse=True)
+        owners = 1 << len(self.order)
+        self.total = part.reshape((2,) * len(self.order) + (part.shape[0] // owners, part.shape[1]))
 
     def send(self):
         b = self.order.pop(0)
@@ -320,8 +328,7 @@
         self.left.remove(b)
         mine = (lax.axis_index("ctx") >> b) & 1
         pick = functools.partial(lax.dynamic_index_in_dim, axis=axis, keepdims=False)
-        pairs = [(i, i ^ (1 << b)) for i in range(lax.axis_size("ctx"))]
-        self.got = lax.ppermute(pick(self.total, 1 - mine), "ctx", pairs)
+        self.got = lax.ppermute(pick(self.total, 1 - mine), "ctx", pairs_of(b))
         self.keep = pick(self.total, mine)
 
     def add(self):
@@ -335,6 +342,18 @@
             self.send()
             self.add()
         return self.total
+
+
+class Swap:
+    def __init__(self, value, b):
+        self.got = lax.ppermute(value, "ctx", pairs_of(b))
+
+
+def owner_half(rows_of_owners, b, which):
+    total, cols = rows_of_owners.shape
+    low = (total // lax.axis_size("ctx")) << b
+    cut = rows_of_owners.reshape(total // (2 * low), 2, low, cols)
+    return lax.dynamic_index_in_dim(cut, which, 1, keepdims=False).reshape(total // 2, cols)
 
 
 def pin(value, *halvings):
@@ -421,18 +440,18 @@
             gains_out[...] = both
         go.wait_send()
 
-    for step in range(1, steps):
-        for n, (p, item, order) in enumerate(plan):
-            for sub in subs(order, step - 1):
-                copy(n, step - 1, sub).wait_recv()
-            for sub in subs(order, step):
-                mask = 1 << order[step] | sub
-                sendbuf[p][without(mask, order[0]), item] = total_of(n, mask, step).astype(BF16)
-                copy(n, step, sub).start()
-    for n, (p, item, order) in enumerate(plan):
-        for sub in subs(order, steps - 1):
-            copy(n, steps - 1, sub).wait_recv()
-        outs[p][item] = total_of(n, 0, steps)
+    for n, got in wavefront(len(plan), steps):
+        p, item, order = plan[n]
+        for sub in subs(order, got):
+            copy(n, got, sub).wait_recv()
+        step = got + 1
+        if step == steps:
+            outs[p][item] = total_of(n, 0, steps)
+            continue
+        for sub in subs(order, step):
+            mask = 1 << order[step] | sub
+            sendbuf[p][without(mask, order[0]), item] = total_of(n, mask, step).astype(BF16)
+            copy(n, step, sub).start()
     for step in range(steps):
         for n, (_, _, order) in enumerate(plan):
             for sub in subs(order, step):
@@ -462,7 +481,7 @@
         compiler_params=pltpu.CompilerParams(
             collective_id=cid, has_side_effects=True, vmem_limit_bytes=56 * MIB
         ),
-        cost_estimate=takes(180),
+        cost_estimate=takes(80),
         name="weights_scatter",
     )(*blocks, gains)
     return [o.reshape(rows, o.shape[-1]) for o in out[:-1]], out[-1]
@@ -643,11 +662,18 @@
         by_owner(part),
     )
     ffw_all = ffw_all.reshape(all_rows, width)
+    pair = min(1, steps - 1)
+    others = [b for b in usual if b != pair]
+    pair_bit = (ctx_rank >> pair) & 1
+    ffw_turned = ffw_all.T
+    ffw_mine = owner_half(ffw_turned, pair, pair_bit)
+    ffw_swap = Swap(owner_half(ffw_turned, pair, 1 - pair_bit), pair)
     gate = dot(ffw_all, gate_weight)
     up = dot(ffw_all, up_weight)
     mixed, mixed_back = jax.vjp(gelu_times, gate, up)
     mixed = mixed.astype(BF16)
-    part = dot(mixed, down_weight).astype(BF16)
+    mixed_swap = Swap(mixed, pair)
+    part = pin(dot(mixed, down_weight).astype(BF16), ffw_swap)
     ffw_grad_all, layer_out, ffw_out_gain_part = tp_exchange(
         "turn",
         4,
@@ -657,20 +683,15 @@
         by_owner(part),
     )
     ffw_grad_all = ffw_grad_all.reshape(all_rows, width)
-    down_part = ein("rd,rf->df", ffw_grad_all, mixed).astype(BF16)
-    ff_cut = down_part.shape[1] * 2 // 3
-    down = [Halving(down_part[:, :ff_cut], usual), Halving(down_part[:, ff_cut:], other)]
-    for h in down:
-        h.send()
+    grad_turned = ffw_grad_all.T
+    grad_mine = owner_half(grad_turned, pair, pair_bit)
+    grad_swap = Swap(owner_half(grad_turned, pair, 1 - pair_bit), pair)
     mixed_grad = ein("rd,fd->rf", ffw_grad_all, down_weight)
     gate_grad, up_grad = mixed_back(mixed_grad)
     gate_grad = gate_grad.astype(BF16)
     up_grad = up_grad.astype(BF16)
-    gate_part = ein("rd,rf->df", ffw_all, gate_grad).astype(BF16)
-    gates = [Halving(gate_part[:, :ff_cut], usual), Halving(gate_part[:, ff_cut:], other)]
-    for h in gates:
-        h.send()
-    up_part = ein("rd,rf->df", ffw_all, up_grad).astype(BF16)
+    gate_swap = Swap(gate_grad, pair)
+    up_swap = Swap(up_grad, pair)
     part = (
         ein("rf,df->rd", gate_grad, gate_weight) + ein("rf,df->rd", up_grad, up_weight)
     ).astype(BF16)
@@ -682,10 +703,9 @@
         [f32_rows, gain_shape, gain_shape],
         by_owner(part),
     )
-    branch_grad_all = pin(branch_grad_all.reshape(all_rows, width), *down)
-    for h in down:
-        h.add()
-        h.send()
+    branch_grad_all = pin(branch_grad_all.reshape(all_rows, width), ffw_swap, mixed_swap, grad_swap)
+    down = Halving((dot(grad_mine, mixed) + dot(grad_swap.got, mixed_swap.got)).astype(BF16), others)
+    down.send()
     output_part = ein("rd,rh->dh", branch_grad_all, attn_rows).astype(BF16)
     attn_grad = ein("rd,hd->rh", branch_grad_all, output_weight).reshape(attn.shape)
     row_dot = jnp.sum(attn_grad * attn, axis=-1)
@@ -699,11 +719,18 @@
     key_acc = ein("skgru,srkgd->sukd", score_grad, grouped)
     value_acc = ein("skgru,srkgd->sukd", exps_low, scaled)
     kv_acc = jnp.concatenate([key_acc, value_acc], 0).astype(BF16)
+    kv_acc = pin(kv_acc, gate_swap, down)
+    down.add()
+    down.send()
+    gates = Halving((dot(ffw_mine, gate_grad) + dot(ffw_swap.got, gate_swap.got)).astype(BF16), others)
+    gates.send()
     kv_sum = ctx_scatter(kv_acc.reshape(2 * seqs, ctx_count, rows, local_kv * HD), 6)
-    kv_sum = pin(kv_sum, *down, *gates)
-    for h in down + gates:
-        h.add()
-        h.send()
+    kv_sum = pin(kv_sum, up_swap, gates, down)
+    down_sum = down.finish()
+    gates.add()
+    gates.send()
+    ups = Halving((dot(ffw_mine, up_grad) + dot(ffw_swap.got, up_swap.got)).astype(BF16), others)
+    ups.send()
     key_grad = rotate(kv_sum[:seqs].reshape(seqs, rows, local_kv, HD), cosine, -sine)
     key_grad = key_grad.astype(BF16).reshape(all_rows, local_kv * HD)
     value_grad = kv_sum[seqs:].astype(BF16).reshape(all_rows, local_kv * HD)
@@ -725,15 +752,11 @@
     gains = jnp.concatenate(
         [attn_in_gain_part, attn_out_gain_part, ffw_in_gain_part, ffw_out_gain_part], 0
     )
-    gains = pin(gains, *gates)
-    for h in gates:
-        h.add()
-        h.send()
-    (up_sum, output_sum, qkv_sum), gains = weights_scatter(
-        [up_part, output_part, qkv_part], gains, 8
-    )
-    down_sum = jnp.concatenate([h.finish() for h in down], 1)
-    gate_sum = jnp.concatenate([h.finish() for h in gates], 1)
+    gains = pin(gains, ups)
+    ups.add()
+    ups.send()
+    (output_sum, qkv_sum), gains = weights_scatter([output_part, qkv_part], gains, 8)
+    gate_sum, up_sum = gates.finish(), ups.finish()
     share = width // ctx_count
     gains = lax.dynamic_slice_in_dim(gains, ctx_rank * share, share, 1)
     heads_end = local_heads * HD

time: 954 us -> 836 us (0.88)
  Pallas kernels: 590 us -> 435 us
  waiting for transfers between devices: 38.3 us -> 88.2 us
  local copies, waits for them, and re-layouts: 105 us -> 86.2 us
  matrix products: 159 us -> 174 us
    pallas_call x1, Pallas kernels: 281 us -> 112 us  [weights_scatter(): pl.pallas_call(functools.partial(weights_scatter_kernel, count, tp_count,...]
    ppermute x12 -> x11, waiting for transfers between devices: 38.3 us -> 88.2 us  [the longest x6 63.4 us: send(): self.got = lax.ppermute(pick(self.total, 1 - mine), 'ctx', pairs_of(b))]
    dot_general x4 -> x7, matrix products: 45.7 us -> 68.6 us  [the longest x1 11.8 us: body(): part = pin(dot(mixed, down_weight).astype(BF16), ffw_swap)]
    dynamic_slice x8 -> x2, local copies, waits for them, and re-layouts: 20.3 us -> 5.71 us  [owner_half(): lax.dynamic_index_in_dim(cut, which, 1, keepdims=False)]
    slice x5 -> x0, local copies, waits for them, and re-layouts: 11.6 us -> none  [the longest x1 6.33 us: body(): down_part[:, :ff_cut]]
    reshape x0 -> x2, local copies, waits for them, and re-layouts: none -> 11.1 us  [the longest x1 5.68 us: body(): ffw_all = ffw_all.reshape(all_rows, width)]
    unnamed x162 -> x151, local copies, waits for them, and re-layouts: 27 us -> 20.9 us
  transfers between devices with their start and end apart: 12 -> 11, of which waited for: 3 -> 4; matrix products, arithmetic and copies ran while one was open for 18% -> 26% of each run, Pallas kernels for 45% -> 37%
where the time goes in v3:
time: 836 us; the launch traced here: 832 us
  Pallas kernels  435 us (52%)
  matrix products  174 us (21%)
  waiting for transfers between devices  88.2 us (11%)
  local copies, waits for them, and re-layouts  86.2 us (10%)
  other arithmetic  31.3 us (4%)
  starting transfers between devices  14.5 us (2%)
    pallas_call x5, Pallas kernels, tp_exchange(): pl.pallas_call(functools.partial(tp_kernel, fn, count, items, len(ins), l...  155 us
    pallas_call x1, Pallas kernels, weights_scatter(): pl.pallas_call(functools.partial(weights_scatter_kernel, count, tp_count,...  112 us
    pallas_call x1, Pallas kernels, ctx_scatter(): pl.pallas_call(functools.partial(ctx_scatter_kernel, count, items), out_s...  95.2 us
    pallas_call x1, Pallas kernels, ctx_gather(): pl.pallas_call(functools.partial(ctx_gather_kernel, count, items), out_sh...  72.6 us
    ppermute x6, waiting for transfers between devices, send(): self.got = lax.ppermute(pick(self.total, 1 - mine), 'ctx', pairs_of(b))  63.4 us
    ppermute x5, waiting for transfers between devices, __init__(): self.got = lax.ppermute(value, 'ctx', pairs_of(b))  24.8 us
    unnamed x151, local copies, waits for them, and re-layouts  20.9 us
    dot_general x1, matrix products, body(): mixed_grad = ein('rd,fd->rf', ffw_grad_all, down_weight)  19.2 us
  transfers between devices with their start and end apart: 11, of which 4 were waited for; matrix products, arithmetic and copies ran while one was open for 26% of the time, Pallas kernels for 37%

profile of v3, /device:TPU:0, one launch (start us, length us, event | category | flops | bytes accessed | tf_op | source)
XLA Modules:
  0.0 831.9 jit_solution(8496445106283335174)
XLA Ops:
  6.8 21.6 %enter.1 = bf16[5,2,4,16,2304]{4,3,2,1,0:T(8,128)(2,1)S(1)} custom-call(bf16[5,2,16,2304]{3,2,1,0:T(8,128)(2,1)S(1)} %bitcast.254, bf16[1,2304]{1,0:T(2,128)(2,1)S(1)} %reshape.434.refs_1_.refs_3_), custom_call_target="tpu_custom_call" | custom-call | flops 180000000 | tf_op jit(solution)/shard_map/enter/pallas_call | solution.py:170
  29.4 2.3 fusion.57
  35.0 72.6 %ctx_gather.1 = bf16[10,8,128,256]{3,2,1,0:T(8,128)(2,1)} custom-call(bf16[10,128,256]{2,1,0:T(8,128)(2,1)} %pad_maximum_fusion.2.block), custom_call_target="tpu_custom_call" | custom-call | flops 550000000 | tf_op jit(solution)/shard_map/ctx_gather/pallas_call | solution.py:232
  107.6 5.5 fusion.67
  113.1 4.3 copy.110
  117.4 4.4 fusion.70
  124.0 3.3 fusion.69
  127.3 3.0 copy.74
  133.2 37.3 %middle.1 = (bf16[5,2,4,16,2304]{4,3,2,1,0:T(8,128)(2,1)S(1)}, f32[5,2,16,2304]{3,2,1,0:T(8,128)S(1)}, f32[5,2,16,2304]{3,2,1,0:T(8,128)S(1)}) custom-call(bf16[5,2,4,16,2304]{4,3,2,1,0:T(8,128)(2,1)S(1)} %bitcast.259, bf16[5,2,16,2304]{3,2,1,0:T(8,128)(2,1)S(1)} %bitcast.255, bf16[1,2304]{1,0:T(2,128)(2,1)S(1)} %reshape.442.refs_2_.refs_5_, ...), custom_call_target="tpu_custom_call" | custom-call | flops 360000000 | tf_op jit(solution)/shard_map/middle/pallas_call | solution.py:170
  174.4 5.7 copy.75
  180.1 3.8 constant_dynamic-slice_fusion.1
  184.4 9.6 %fusion.71 = f32[640,2304]{1,0:T(8,128)S(1)} fusion(bf16[640,2304]{1,0:T(8,128)(2,1)S(1)} %bitcast.265, bf16[2304,2304]{1,0:T(8,128)(2,1)} %param.23), kind=kOutput, calls=%fused_computation.146 | convolution fusion | flops 6794772480 | bytes 19464192 | tf_op jit(solution)/shard_map/dot_general | solution.py:671
  194.1 9.4 %multiply_convert_fusion.1 = (bf16[640,2304]{1,0:T(8,128)(2,1)}, f32[640,2304]{1,0:T(8,128)}) fusion(f32[640,2304]{1,0:T(8,128)S(1)} %fusion.71, bf16[640,2304]{1,0:T(8,128)(2,1)S(1)} %bitcast.266, bf16[2304,2304]{1,0:T(8,128)(2,1)S(1)} %bitcast.320), kind=kOutput, calls=%fused_computation.17 | convolution fusion | flops 6809518080 | bytes 28311552 | tf_op jit(solution)/shard_map/dot_general | solution.py:672
  203.5 2.1 collective-permute-start.1
  205.6 2.1 copy.120
  207.7 11.8 %convolution_convert_fusion.1 = bf16[640,2304]{1,0:T(8,128)(2,1)S(1)} fusion(bf16[640,2304]{1,0:T(8,128)(2,1)} %get-tuple-element.143, bf16[2304,2304]{1,0:T(8,128)(2,1)} %param.25), kind=kOutput, calls=%fused_computation.37 | convolution fusion | flops 6796247040 | bytes 16515072 | tf_op jit(solution)/shard_map/dot_general | solution.py:676
  219.6 37.5 %turn.1 = (bf16[5,2,4,16,2304]{4,3,2,1,0:T(8,128)(2,1)S(1)}, bf16[5,2,16,2304]{3,2,1,0:T(8,128)(2,1)S(1)}, f32[1,2304]{1,0:T(1,128)S(1)}) custom-call(bf16[5,2,4,16,2304]{4,3,2,1,0:T(8,128)(2,1)S(1)} %bitcast.270, f32[5,2,16,2304]{3,2,1,0:T(8,128)S(1)} %copy-done.4, bf16[5,2,16,2304]{3,2,1,0:T(8,128)(2,1)S(1)} %bitcast.257, bf16[1,2304]{1,0:T(2,128)(2,1)S(1)} %reshape.448.refs_3_), custom_call_target="tpu_custom_call" | custom-call | flops 360000000 | tf_op jit(solution)/shard_map/turn/pallas_call | solution.py:170
  259.6 5.5 copy.77
  265.0 19.2 %multiply_convert_fusion = (bf16[640,2304]{1,0:T(8,128)(2,1)}, bf16[640,2304]{1,0:T(8,128)(2,1)}) fusion(f32[640,2304]{1,0:T(8,128)} %copy-done.64, f32[640,2304]{1,0:T(8,128)} %get-tuple-element.144, bf16[640,2304]{1,0:T(8,128)(2,1)} %bitcast.268, bf16[2304,2304]{1,0:T(8,128)(2,1)} %param.25), kind=kOutput, calls=%fused_computation.16 | convolution fusion | flops 6830161920 | bytes 31260672 | tf_op jit(solution)/shard_map/rd,fd->rf/dot_general | solution.py:689
  284.2 13.5 %fusion.72 = f32[640,2304]{1,0:T(8,128)} fusion(bf16[640,2304]{1,0:T(8,128)(2,1)} %get-tuple-element.117, bf16[2304,2304]{1,0:T(8,128)(2,1)} %param.23), kind=kOutput, calls=%fused_computation.147 | convolution fusion | flops 6794772480 | bytes 19464192 | tf_op jit(solution)/shard_map/rf,df->rd/dot_general | solution.py:696
  298.0 1.9 constant_dynamic-slice_fusion.2
  299.9 1.7 collective-permute-start.2
  301.9 13.0 %add_convert_fusion = bf16[640,2304]{1,0:T(8,128)(2,1)S(1)} fusion(f32[640,2304]{1,0:T(8,128)} %fusion.72, bf16[640,2304]{1,0:T(8,128)(2,1)} %get-tuple-element.116, bf16[2304,2304]{1,0:T(8,128)(2,1)} %param.24), kind=kOutput, calls=%fused_computation.15 | convolution fusion | flops 6797721600 | bytes 22413312 | tf_op jit(solution)/shard_map/rf,df->rd/dot_general | solution.py:696
  314.9 37.6 %middle_back.1 = (bf16[5,2,4,16,2304]{4,3,2,1,0:T(8,128)(2,1)S(1)}, f32[5,2,16,2304]{3,2,1,0:T(8,128)S(1)}, f32[1,2304]{1,0:T(1,128)S(1)}, f32[1,2304]{1,0:T(1,128)S(1)}) custom-call(bf16[5,2,4,16,2304]{4,3,2,1,0:T(8,128)(2,1)S(1)} %bitcast.269, f32[5,2,16,2304]{3,2,1,0:T(8,128)S(1)} %copy-done.5, f32[5,2,16,2304]{3,2,1,0:T(8,128)S(1)} %copy-done.14, ...), custom_call_target="tpu_custom_call" | custom-call | flops 360000000 | tf_op jit(solution)/shard_map/middle_back/pallas_call | solution.py:170
  352.6 10.3 %fusion.74 = f32[1152,2304]{1,0:T(8,128)} fusion(bf16[1152,640]{1,0:T(8,128)(2,1)S(1)} %bitcast.301, bf16[640,2304]{1,0:T(8,128)(2,1)} %get-tuple-element.143), kind=kOutput, calls=%fused_computation.149 | convolution fusion | flops 3397386240 | bytes 15040512 | tf_op jit(solution)/shard_map/dot_general | solution.py:707
  362.9 8.7 %fusion.75 = f32[1152,2304]{1,0:T(8,128)} fusion(bf16[1152,640]{1,0:T(8,128)(2,1)S(1)} %bitcast.299, bf16[640,2304]{1,0:T(8,128)(2,1)} %get-tuple-element.117), kind=kOutput, calls=%fused_computation.150 | convolution fusion | flops 3397386240 | bytes 15040512 | tf_op jit(solution)/shard_map/dot_general | solution.py:725
  371.6 24.8 %collective-permute-done.2 = bf16[1152,640]{1,0:T(8,128)(2,1)} collective-permute-done((bf16[1152,640]{1,0:T(8,128)(2,1)}, bf16[1152,640]{1,0:T(8,128)(2,1)}, u32[]{:S(2)}, u32[]{:S(2)}) %collective-permute-start.2) | collective-permute-done | bytes 1474592 | tf_op jit(solution)/shard_map/ppermute | solution.py:349
  396.4 9.7 %fusion = bf16[1152,2304]{1,0:T(8,128)(2,1)S(1)} fusion(f32[1152,2304]{1,0:T(8,128)} %fusion.74, bf16[1152,640]{1,0:T(8,128)(2,1)} %collective-permute-done.2, bf16[640,2304]{1,0:T(8,128)(2,1)} %collective-permute-done.1), kind=kOutput, calls=%fused_computation.3 | convolution fusion | flops 3402694656 | bytes 20348928 | tf_op jit(solution)/shard_map/dot_general | solution.py:707
  406.0 2.3 copy-done.27
  411.1 2.8 fusion.73
  413.9 2.9 reshape.454
  416.8 3.3 reshape.455
  420.1 3.3 copy.78
  423.4 3.3 copy.80
  426.7 1.8 multiply_reduce_fusion
  428.6 6.4 fusion.13
  436.5 4.3 fusion.25
  440.8 3.1 pad_maximum_fusion
  444.0 24.3 %collective-permute-done.4 = bf16[2,288,2304]{2,1,0:T(8,128)(2,1)} collective-permute-done((bf16[2,288,2304]{2,1,0:T(8,128)(2,1)}, bf16[2,288,2304]{2,1,0:T(8,128)(2,1)}, u32[]{:S(2)}, u32[]{:S(2)}) %collective-permute-start.4) | collective-permute-done | bytes 2654240 | tf_op jit(solution)/shard_map/ppermute | solution.py:331
  468.3 9.7 %fusion.1 = bf16[1152,2304]{1,0:T(8,128)(2,1)S(1)} fusion(f32[1152,2304]{1,0:T(8,128)} %fusion.75, bf16[1152,640]{1,0:T(8,128)(2,1)} %collective-permute-done, bf16[640,2304]{1,0:T(8,128)(2,1)} %collective-permute-done.3), kind=kOutput, calls=%fused_computation.4 | convolution fusion | flops 3402694656 | bytes 20348928 | tf_op jit(solution)/shard_map/dot_general | solution.py:725
  478.0 1.8 dynamic-slice_bitcast_fusion.1
  482.1 2.4 fusion.12
  487.0 8.7 %fusion.76 = f32[1152,2304]{1,0:T(8,128)} fusion(bf16[1152,640]{1,0:T(8,128)(2,1)S(1)} %bitcast.300, bf16[640,2304]{1,0:T(8,128)(2,1)} %get-tuple-element.116), kind=kOutput, calls=%fused_computation.151 | convolution fusion | flops 3397386240 | bytes 15040512 | tf_op jit(solution)/shard_map/dot_general | solution.py:732
  500.2 3.5 convolution_convert_fusion.4
  503.7 8.0 copy.88
  511.8 95.2 %ctx_scatter.1 = f32[10,128,256]{2,1,0:T(8,128)} custom-call(bf16[10,8,128,256]{3,2,1,0:T(8,128)(2,1)} %bitcast.276), custom_call_target="tpu_custom_call" | custom-call | flops 600000000 | tf_op jit(solution)/shard_map/ctx_scatter/pallas_call | solution.py:295
  607.1 9.8 %fusion.2 = bf16[1152,2304]{1,0:T(8,128)(2,1)S(1)} fusion(f32[1152,2304]{1,0:T(8,128)} %fusion.76, bf16[1152,640]{1,0:T(8,128)(2,1)} %collective-permute-done, bf16[640,2304]{1,0:T(8,128)(2,1)} %collective-permute-done.5), kind=kOutput, calls=%fused_computation.5 | convolution fusion | flops 3402694656 | bytes 20348928 | tf_op jit(solution)/shard_map/dot_general | solution.py:732
  616.9 1.8 dynamic-slice_bitcast_fusion
  618.7 2.4 collective-permute-start.8
  621.1 2.4 fusion.11
  626.1 3.2 convolution_convert_fusion.3
  629.4 21.0 %leave.1 = (f32[5,2,16,2304]{3,2,1,0:T(8,128)S(1)}, f32[1,2304]{1,0:T(1,128)S(1)}) custom-call(bf16[5,2,4,16,2304]{4,3,2,1,0:T(8,128)(2,1)S(1)} %bitcast.271, bf16[5,2,16,2304]{3,2,1,0:T(8,128)(2,1)S(1)} %bitcast.256, f32[5,2,16,2304]{3,2,1,0:T(8,128)S(1)} %copy-done.12, bf16[1,2304]{1,0:T(2,128)(2,1)S(1)} %copy-done.18), custom_call_target="tpu_custom_call" | custom-call | flops 180000000 | tf_op jit(solution)/shard_map/leave/pallas_call | solution.py:170
  651.1 3.1 fusion.22
  654.2 18.9 %collective-permute-done.8 = bf16[2,288,2304]{2,1,0:T(8,128)(2,1)} collective-permute-done((bf16[2,288,2304]{2,1,0:T(8,128)(2,1)}, bf16[2,288,2304]{2,1,0:T(8,128)(2,1)}, u32[]{:S(2)}, u32[]{:S(2)}) %collective-permute-start.8) | collective-permute-done | bytes 2654240 | tf_op jit(solution)/shard_map/ppermute | solution.py:331
  673.1 3.2 fusion.10
  676.4 3.3 collective-permute-start.10
  679.7 6.1 convolution_convert_fusion
  685.8 2.2 copy.93
  688.0 20.1 %collective-permute-done.9 = bf16[288,2304]{1,0:T(8,128)(2,1)S(1)} collective-permute-done((bf16[288,2304]{1,0:T(8,128)(2,1)S(1)}, bf16[288,2304]{1,0:T(8,128)(2,1)S(1)}, u32[]{:S(2)}, u32[]{:S(2)}) %collective-permute-start.9) | collective-permute-done | bytes 1327136 | tf_op jit(solution)/shard_map/ppermute | solution.py:331
  708.1 1.8 convert_add_fusion.5
  709.9 112.4 %weights_scatter.1 = (f32[6,48,512]{2,1,0:T(8,128)}, f32[6,48,1024]{2,1,0:T(8,128)}, f32[4,2304]{1,0:T(4,128)}) custom-call(bf16[8,6,48,512]{3,2,1,0:T(8,128)(2,1)} %bitcast.296, bf16[8,6,48,1024]{3,2,1,0:T(8,128)(2,1)} %bitcast.291, f32[4,2304]{1,0:T(4,128)} %pad_maximum_fusion.9.refs_2_), custom_call_target="tpu_custom_call" | custom-call | flops 800000000 | tf_op jit(solution)/shard_map/weights_scatter/pallas_call | solution.py:471
  822.3 1.9 slice.88
  825.8 1.9 fusion.68
  827.7 3.1 convert_add_fusion.4
  (204 shorter events, 41.7 us)
Async XLA Ops:
  0.6 130.9 %copy-start = (bf16[512,2304]{1,0:T(8,128)(2,1)S(1)}, bf16[512,2304]{1,0:T(8,128)(2,1)}, u32[]{:S(2)}) copy-start(bf16[512,2304]{1,0:T(8,128)(2,1)} %param.20) | copy-start | bytes 7077892
  0.7 31.0 %copy-start.57 = (f32[128]{0:T(128)}, f32[128]{0:T(128)S(1)}, u32[]{:S(2)}) copy-start(f32[128]{0:T(128)S(1)} %multiply_power_fusion) | copy-start | bytes 1540
  3.5 28.2 %copy-start.50 = (f32[5,128]{1,0:T(8,128)}, f32[5,128]{1,0:T(8,128)S(1)}, u32[]{:S(2)}) copy-start(f32[5,128]{1,0:T(8,128)S(1)} %subtract_convert_fusion.2) | copy-start | bytes 7684
  3.5 24.9 %copy-start.61 = (bf16[2304,256]{1,0:T(8,128)(2,1)S(1)}, bf16[2304,256]{1,0:T(8,128)(2,1)}, u32[]{:S(2)}) copy-start(bf16[2304,256]{1,0:T(8,128)(2,1)} %param.18) | copy-start | bytes 3538948
  6.8 22.6 %copy-start.17 = (bf16[1,2304]{1,0:T(2,128)(2,1)}, bf16[1,2304]{1,0:T(2,128)(2,1)S(1)}, u32[]{:S(2)}) copy-start(bf16[1,2304]{1,0:T(2,128)(2,1)S(1)} %reshape.434.refs_1_.refs_3_) | copy-start | bytes 13828
  28.4 4.7 copy-start.6
  28.4 4.7 copy-start.59
  31.7 90.1 %copy-start.30 = (f32[5,128,128]{2,1,0:T(8,128)}, f32[5,128,128]{2,1,0:T(8,128)S(1)}, u32[]{:S(2)}) copy-start(f32[5,128,128]{2,1,0:T(8,128)S(1)} %get-tuple-element.138) | copy-start | bytes 983044
  117.4 4.4 copy-start.42
  117.4 4.7 copy-start.24
  117.4 4.7 copy-start.46
  123.7 3.5 copy-start.55
  123.8 3.5 copy-start.63
  124.0 7.5 copy-start.52
  124.0 7.5 copy-start.53
  180.1 4.3 copy-start.9
  183.9 10.2 %slice-start.4 = ((s8[10616832]{0:T(1024)(128)(4,1)}), s8[4194304]{0:T(1024)(128)(4,1)S(1)}, s32[]{:S(2)}) async-start(s8[10616832]{0:T(1024)(128)(4,1)} %bitcast.319), calls=%async_computation.4 | async-start | bytes 8388608
  183.9 10.2 %slice-start.5 = ((s8[10616832]{0:T(1024)(128)(4,1)}), s8[4194304]{0:T(1024)(128)(4,1)S(1)}, s32[]{:S(2)}) async-start(s8[10616832]{0:T(1024)(128)(4,1)} %bitcast.319), calls=%async_computation.5 | async-start | bytes 8388608
  183.9 10.2 %slice-start.6 = ((s8[10616832]{0:T(1024)(128)(4,1)}), s8[2228224]{0:T(1024)(128)(4,1)S(1)}, s32[]{:S(2)}) async-start(s8[10616832]{0:T(1024)(128)(4,1)} %bitcast.319), calls=%async_computation.6 | async-start | bytes 4456448
  183.9 35.7 %collective-permute-start = (bf16[1152,640]{1,0:T(8,128)(2,1)}, bf16[1152,640]{1,0:T(8,128)(2,1)}, u32[]{:S(2)}, u32[]{:S(2)}) collective-permute-start(bf16[1152,640]{1,0:T(8,128)(2,1)} %bitcast.32), channel_id=1, source_target_pairs={{0,8},{4,12},{8,0},{12,4},{16,24},{20,28},{24,16},{28,20},{1,9},{5... | collective-permute-start | bytes 4423688 | tf_op jit(solution)/shard_map/ppermute | solution.py:349
  194.1 9.4 %copy-start.64 = (f32[640,2304]{1,0:T(8,128)}, f32[640,2304]{1,0:T(8,128)S(1)}, u32[]{:S(2)}) copy-start(f32[640,2304]{1,0:T(8,128)S(1)} %fusion.71) | copy-start | bytes 17694724
  194.1 13.6 %copy-start.54 = (bf16[2304]{0:T(1024)(128)(2,1)S(1)}, bf16[2304]{0:T(1024)(128)(2,1)}, u32[]{:S(2)}) copy-start(bf16[2304]{0:T(1024)(128)(2,1)} %param.26) | copy-start | bytes 13828
  203.5 168.1 %collective-permute-start.1 = (bf16[640,2304]{1,0:T(8,128)(2,1)}, bf16[640,2304]{1,0:T(8,128)(2,1)}, u32[]{:S(2)}, u32[]{:S(2)}) collective-permute-start(bf16[640,2304]{1,0:T(8,128)(2,1)} %get-tuple-element.143), channel_id=1, source_target_pairs={{0,8},{4,12},{8,0},{12,4},{16,24},{20,28},{24,16},{28,20},{1,9},{5... | collective-permute-start | bytes 8847368 | tf_op jit(solution)/shard_map/ppermute | solution.py:349
  207.7 11.9 %copy-start.1 = (bf16[16,5,2,2304]{3,0,2,1:T(8,128)(2,1)S(1)}, bf16[16,5,2,2304]{3,0,2,1:T(8,128)(2,1)}, u32[]{:S(2)}) copy-start(bf16[16,5,2,2304]{3,0,2,1:T(8,128)(2,1)} %copy.120) | copy-start | bytes 2211844
  207.7 11.9 %copy-start.4 = (f32[5,2,16,2304]{3,2,1,0:T(8,128)S(1)}, f32[5,2,16,2304]{3,2,1,0:T(8,128)}, u32[]{:S(2)}) copy-start(f32[5,2,16,2304]{3,2,1,0:T(8,128)} %copy-done.3) | copy-start | bytes 4423684
  284.2 13.8 %copy-start.21 = (bf16[640,2304]{0,1:T(8,128)(2,1)S(1)}, bf16[640,2304]{0,1:T(8,128)(2,1)}, u32[]{:S(2)}) copy-start(bf16[640,2304]{0,1:T(8,128)(2,1)} %copy.77) | copy-start | bytes 8847364
  297.7 146.3 %collective-permute-start.3 = (bf16[640,2304]{1,0:T(8,128)(2,1)}, bf16[640,2304]{1,0:T(8,128)(2,1)}, u32[]{:S(2)}, u32[]{:S(2)}) collective-permute-start(bf16[640,2304]{1,0:T(8,128)(2,1)} %get-tuple-element.117), channel_id=1, source_target_pairs={{0,8},{4,12},{8,0},{12,4},{16,24},{20,28},{24,16},{28,20},{1,9},{5... | collective-permute-start | bytes 8847368 | tf_op jit(solution)/shard_map/ppermute | solution.py:349
  299.9 96.5 %collective-permute-start.2 = (bf16[1152,640]{1,0:T(8,128)(2,1)}, bf16[1152,640]{1,0:T(8,128)(2,1)}, u32[]{:S(2)}, u32[]{:S(2)}) collective-permute-start(bf16[1152,640]{1,0:T(8,128)(2,1)} %bitcast.44), channel_id=1, source_target_pairs={{0,8},{4,12},{8,0},{12,4},{16,24},{20,28},{24,16},{28,20},{1,9},{5... | collective-permute-start | bytes 4423688 | tf_op jit(solution)/shard_map/ppermute | solution.py:349
  301.6 13.3 %copy-start.2 = (bf16[16,5,2,2304]{3,0,2,1:T(8,128)(2,1)S(1)}, bf16[16,5,2,2304]{3,0,2,1:T(8,128)(2,1)}, u32[]{:S(2)}) copy-start(bf16[16,5,2,2304]{3,0,2,1:T(8,128)(2,1)} %copy.120) | copy-start | bytes 2211844
  301.6 13.3 %copy-start.5 = (f32[5,2,16,2304]{3,2,1,0:T(8,128)S(1)}, f32[5,2,16,2304]{3,2,1,0:T(8,128)}, u32[]{:S(2)}) copy-start(f32[5,2,16,2304]{3,2,1,0:T(8,128)} %copy-done.3) | copy-start | bytes 4423684
  301.6 13.3 %copy-start.14 = (f32[5,2,16,2304]{3,2,1,0:T(8,128)S(1)}, f32[5,2,16,2304]{3,2,1,0:T(8,128)}, u32[]{:S(2)}) copy-start(f32[5,2,16,2304]{3,2,1,0:T(8,128)} %copy-done.13) | copy-start | bytes 4423684
  301.6 305.4 %collective-permute-start.5 = (bf16[640,2304]{1,0:T(8,128)(2,1)}, bf16[640,2304]{1,0:T(8,128)(2,1)}, u32[]{:S(2)}, u32[]{:S(2)}) collective-permute-start(bf16[640,2304]{1,0:T(8,128)(2,1)} %get-tuple-element.116), channel_id=1, source_target_pairs={{0,8},{4,12},{8,0},{12,4},{16,24},{20,28},{24,16},{28,20},{1,9},{5... | collective-permute-start | bytes 8847368 | tf_op jit(solution)/shard_map/ppermute | solution.py:349
  314.9 37.7 %copy-start.36 = (bf16[2,1,576,640]{3,2,1,0:T(8,128)(2,1)S(1)}, bf16[2,1,576,640]{3,2,1,0:T(8,128)(2,1)}, u32[]{:S(2)}) copy-start(bf16[2,1,576,640]{3,2,1,0:T(8,128)(2,1)} %get-tuple-element.122) | copy-start | bytes 4423684
  352.6 10.3 %copy-start.11 = (f32[5,2,16,2304]{3,2,1,0:T(8,128)}, f32[5,2,16,2304]{3,2,1,0:T(8,128)S(1)}, u32[]{:S(2)}) copy-start(f32[5,2,16,2304]{3,2,1,0:T(8,128)S(1)} %get-tuple-element.59.refs_2_) | copy-start | bytes 4423684
  352.6 58.5 %copy-start.19 = (bf16[5,2,4,16,2304]{4,3,2,1,0:T(8,128)(2,1)}, bf16[5,2,4,16,2304]{4,3,2,1,0:T(8,128)(2,1)S(1)}, u32[]{:S(2)}) copy-start(bf16[5,2,4,16,2304]{4,3,2,1,0:T(8,128)(2,1)S(1)} %get-tuple-element.49) | copy-start | bytes 8847364
  352.6 10.3 %copy-start.34 = (bf16[2,1,576,640]{3,2,1,0:T(8,128)(2,1)S(1)}, bf16[2,1,576,640]{3,2,1,0:T(8,128)(2,1)}, u32[]{:S(2)}) copy-start(bf16[2,1,576,640]{3,2,1,0:T(8,128)(2,1)} %get-tuple-element.120) | copy-start | bytes 4423684
  410.0 58.3 %collective-permute-start.4 = (bf16[2,288,2304]{2,1,0:T(8,128)(2,1)}, bf16[2,288,2304]{2,1,0:T(8,128)(2,1)}, u32[]{:S(2)}, u32[]{:S(2)}) collective-permute-start(bf16[2,288,2304]{2,1,0:T(8,128)(2,1)} %dynamic-slice_bitcast_fusion.2), channel_id=1, source_target_pairs={{0,4},{4,0},{8,12},{12,8},{16,20},{20,16},{24,28},{28,24},{1,5},{5... | collective-permute-start | bytes 7962632 | tf_op jit(solution)/shard_map/ppermute | solution.py:331
  423.4 5.1 copy-start.56
  428.6 6.4 copy-start.38
  428.6 6.4 copy-start.40
  440.8 41.3 %slice-start.2 = ((s8[5308416]{0:T(1024)(128)(4,1)}), s8[4194304]{0:T(1024)(128)(4,1)S(1)}, s32[]{:S(2)}) async-start(s8[5308416]{0:T(1024)(128)(4,1)} %bitcast.286), calls=%async_computation.2 | async-start | bytes 8388608
  444.0 38.2 %slice-start.3 = ((s8[5308416]{0:T(1024)(128)(4,1)}), s8[1114112]{0:T(1024)(128)(4,1)S(1)}, s32[]{:S(2)}) async-start(s8[5308416]{0:T(1024)(128)(4,1)} %bitcast.286), calls=%async_computation.3 | async-start | bytes 2228224
  478.0 3.1 copy-start.26
  481.1 5.9 copy-start.35
  481.1 126.0 %collective-permute-start.6 = (bf16[2,288,2304]{2,1,0:T(8,128)(2,1)}, bf16[2,288,2304]{2,1,0:T(8,128)(2,1)}, u32[]{:S(2)}, u32[]{:S(2)}) collective-permute-start(bf16[2,288,2304]{2,1,0:T(8,128)(2,1)} %dynamic-slice_bitcast_fusion.1), channel_id=1, source_target_pairs={{0,4},{4,0},{8,12},{12,8},{16,20},{20,16},{24,28},{28,24},{1,5},{5... | collective-permute-start | bytes 7962632 | tf_op jit(solution)/shard_map/ppermute | solution.py:331
  484.6 11.1 %copy-start.22 = (bf16[2,288,2304]{2,1,0:T(8,128)(2,1)}, bf16[2,288,2304]{2,1,0:T(8,128)(2,1)S(1)}, u32[]{:S(2)}) copy-start(bf16[2,288,2304]{2,1,0:T(8,128)(2,1)S(1)} %fusion.12) | copy-start | bytes 7962628
  486.0 9.8 %copy-start.16 = (bf16[5,2,16,2304]{3,2,1,0:T(8,128)(2,1)S(1)}, bf16[5,2,16,2304]{3,2,1,0:T(8,128)(2,1)}, u32[]{:S(2)}) copy-start(bf16[5,2,16,2304]{3,2,1,0:T(8,128)(2,1)} %copy-done.15) | copy-start | bytes 2211844
  486.0 11.2 %copy-start.25 = (bf16[5,8,128,256]{3,2,1,0:T(8,128)(2,1)S(1)}, bf16[5,8,128,256]{3,2,1,0:T(8,128)(2,1)}, u32[]{:S(2)}) copy-start(bf16[5,8,128,256]{3,2,1,0:T(8,128)(2,1)} %get-tuple-element.118) | copy-start | bytes 7864324
  486.0 121.1 %collective-permute-start.7 = (bf16[288,2304]{1,0:T(8,128)(2,1)}, bf16[288,2304]{1,0:T(8,128)(2,1)}, u32[]{:S(2)}, u32[]{:S(2)}) collective-permute-start(bf16[288,2304]{1,0:T(8,128)(2,1)} %dynamic-slice_bitcast_fusion.5), channel_id=1, source_target_pairs={{0,16},{4,20},{8,24},{12,28},{16,0},{20,4},{24,8},{28,12},{1,17},{... | collective-permute-start | bytes 3981320 | tf_op jit(solution)/shard_map/ppermute | solution.py:331
  511.8 109.3 %slice-start = ((s8[5308416]{0:T(1024)(128)(4,1)}), s8[1114112]{0:T(1024)(128)(4,1)S(1)}, s32[]{:S(2)}) async-start(s8[5308416]{0:T(1024)(128)(4,1)} %bitcast.282), calls=%async_computation | async-start | bytes 2228224
  607.0 14.1 %slice-start.1 = ((s8[5308416]{0:T(1024)(128)(4,1)}), s8[4194304]{0:T(1024)(128)(4,1)S(1)}, s32[]{:S(2)}) async-start(s8[5308416]{0:T(1024)(128)(4,1)} %bitcast.282), calls=%async_computation.1 | async-start | bytes 8388608
  616.9 6.7 copy-start.28
  618.7 5.1 copy-start.29
  618.7 54.4 %collective-permute-start.8 = (bf16[2,288,2304]{2,1,0:T(8,128)(2,1)}, bf16[2,288,2304]{2,1,0:T(8,128)(2,1)}, u32[]{:S(2)}, u32[]{:S(2)}) collective-permute-start(bf16[2,288,2304]{2,1,0:T(8,128)(2,1)} %dynamic-slice_bitcast_fusion), channel_id=1, source_target_pairs={{0,4},{4,0},{8,12},{12,8},{16,20},{20,16},{24,28},{28,24},{1,5},{5... | collective-permute-start | bytes 7962632 | tf_op jit(solution)/shard_map/ppermute | solution.py:331
  623.6 2.4 copy-start.33
  623.6 2.4 copy-start.48
  623.6 2.5 copy-start.62
  623.8 84.3 %collective-permute-start.9 = (bf16[288,2304]{1,0:T(8,128)(2,1)S(1)}, bf16[288,2304]{1,0:T(8,128)(2,1)S(1)}, u32[]{:S(2)}, u32[]{:S(2)}) collective-permute-start(bf16[288,2304]{1,0:T(8,128)(2,1)S(1)} %dynamic-slice_bitcast_fusion.4), channel_id=1, source_target_pairs={{0,16},{4,20},{8,24},{12,28},{16,0},{20,4},{24,8},{28,12},{1,17},{... | collective-permute-start | bytes 3981320 | tf_op jit(solution)/shard_map/ppermute | solution.py:331
  626.1 3.3 copy-start.12
  626.1 3.3 copy-start.18
  629.4 21.7 %copy-start.23 = (bf16[2,288,2304]{2,1,0:T(8,128)(2,1)S(1)}, bf16[2,288,2304]{2,1,0:T(8,128)(2,1)}, u32[]{:S(2)}) copy-start(bf16[2,288,2304]{2,1,0:T(8,128)(2,1)} %copy-done.22) | copy-start | bytes 7962628
  654.2 25.5 %copy-start.7 = (bf16[5,2,4,16,2304]{4,3,2,1,0:T(8,128)(2,1)S(1)}, bf16[5,2,4,16,2304]{4,3,2,1,0:T(8,128)(2,1)}, u32[]{:S(2)}) copy-start(bf16[5,2,4,16,2304]{4,3,2,1,0:T(8,128)(2,1)} %copy-done.6) | copy-start | bytes 8847364
  676.4 151.3 %collective-permute-start.10 = (bf16[288,2304]{1,0:T(8,128)(2,1)S(1)}, bf16[288,2304]{1,0:T(8,128)(2,1)}, u32[]{:S(2)}, u32[]{:S(2)}) collective-permute-start(bf16[288,2304]{1,0:T(8,128)(2,1)S(1)} %dynamic-slice_bitcast_fusion.3), channel_id=1, source_target_pairs={{0,16},{4,20},{8,24},{12,28},{16,0},{20,4},{24,8},{28,12},{1,17},{... | collective-permute-start | bytes 3981320 | tf_op jit(solution)/shard_map/ppermute | solution.py:331
  827.7 3.2 copy-start.49
  (19 other events, 28.9 us)

commit v4 on v3

--- a/solution.py
+++ b/solution.py
@@ -39,11 +39,19 @@
     return masks
 
 
-def wavefront(items, stages, lag=2):
-    for t in range(items + (stages - 1) * lag):
-        for stage in range(stages):
-            if 0 <= t - stage * lag < items:
-                yield t - stage * lag, stage
+def scatter_events(orders):
+    steps = len(orders[0])
+    usual = [i for i, order in enumerate(orders) if order[0] == 0]
+    other = [i for i, order in enumerate(orders) if order[0] != 0]
+    events = []
+    for t in range(len(usual) + steps - 1):
+        events += [(usual[t - s], s) for s in range(steps) if 0 <= t - s < len(usual)]
+        if 1 <= t <= len(other):
+            events.append((other[t - 1], 0))
+    events += [(i, 0) for i in other[max(0, len(usual) + steps - 2) :]]
+    for t in range(len(other) + steps - 2):
+        events += [(other[t - s + 1], s) for s in range(1, steps) if 0 <= t - s + 1 < len(other)]
+    return events
 
 
 def greet(axis, count):
@@ -183,77 +191,132 @@
     )(*args)
 
 
+def cube_order(steps, turned):
+    usual = list(range(steps))
+    return [1, 0] + usual[2:] if turned and steps > 1 else usual
+
+
 def ctx_orders(items, steps):
-    usual = list(range(steps))[::-1]
-    if steps < 2:
-        return [usual] * items
-    other = usual[:-2] + [usual[-1], usual[-2]]
-    return [other if i % 4 == 3 else usual for i in range(items)]
-
-
-def ctx_gather_kernel(count, items, block, whole, send_sem, recv_sem, local_sem):
+    return [cube_order(steps, i >= items - 3 * items // 10) for i in range(items)]
+
+
+def rotated(values, cosine, sine):
+    low, high = values[:, : HD // 2], values[:, HD // 2 :]
+    return jnp.concatenate([low * cosine - high * sine, high * cosine + low * sine], 1)
+
+
+def attend_kernel(count, seqs, heads, q, k, v, cosine, sine, start, tok, key_tok, *refs):
+    whole, attn, attn_low, sums, queries, send_sem, recv_sem = refs
     me = lax.axis_index("ctx")
     steps = count.bit_length() - 1
-    orders = ctx_orders(items, steps)
-    own = pltpu.make_async_copy(block, whole.at[:, me], local_sem)
-    own.start()
-    greet("ctx", count)
+    items = 2 * seqs
+    orders = [order[::-1] for order in ctx_orders(items, steps)]
+    rows = q.shape[1]
+    scale = HD ** (-0.5)
 
     def copy(item, step, mask):
         bit = 1 << orders[item][step]
-        dst = whole.at[item, flipped(me, mask)]
-        src = block.at[item] if mask == 0 else dst
+        block = whole.at[item, flipped(me, mask)]
         return remote(
-            "ctx", src, dst, (send_sem, recv_sem), (item, mask | bit), flipped(me, bit)
+            "ctx", block, block, (send_sem, recv_sem), (item, mask | bit), flipped(me, bit)
         )
 
     def masks(item, step):
         return submasks(orders[item][:step])
 
-    for step in range(steps):
+    def send_own(item):
+        for step in range(steps):
+            copy(item, step, 0).start()
+
+    for s in range(seqs):
+        whole[2 * s, me] = rotated(k[s], cosine[s], sine[s]).astype(BF16)
+        whole[2 * s + 1, me] = v[s].astype(BF16)
+        if s == 0:
+            greet("ctx", count)
+        send_own(2 * s)
+        send_own(2 * s + 1)
+    for s in range(seqs):
+        for h in range(heads):
+            at = slice(h * HD, (h + 1) * HD)
+            queries[s, :, at] = rotated(q[s, :, at], cosine[s], sine[s]).astype(BF16)
+
+    def attend(s):
+        keys = whole[2 * s].reshape(count * rows, HD)
+        values = whole[2 * s + 1].reshape(count * rows, HD)
+        allowed = (key_tok[...] <= tok[...]) & (key_tok[...] >= start[s])
+        for h in range(heads):
+            at = slice(h * HD, (h + 1) * HD)
+            raw = lax.dot_general(
+                queries[s, :, at], keys, (((1,), (1,)), ((), ())), preferred_element_type=F32
+            )
+            exps = jnp.where(allowed, jnp.exp(CAP * jnp.tanh(raw * (scale / CAP))), 0.0)
+            total = jnp.sum(exps, axis=-1, keepdims=True)
+            out = jnp.dot(exps.astype(BF16), values, preferred_element_type=F32) / total
+            sums[s, h] = total
+            attn[s, :, at] = out
+            attn_low[s, :, at] = out.astype(BF16)
+
+    for got in range(steps):
         for item in range(items):
-            copy(item, step, 0).start()
-    for item, got in wavefront(items, steps):
-        for mask in masks(item, got):
-            copy(item, got, mask).wait_recv()
-            for step in range(got + 1, steps):
-                copy(item, step, mask | 1 << orders[item][got]).start()
+            for mask in masks(item, got):
+                copy(item, got, mask).wait_recv()
+                for step in range(got + 1, steps):
+                    copy(item, step, mask | 1 << orders[item][got]).start()
+            if got == steps - 1 and item % 2 == 1:
+                attend(item // 2)
     for step in range(steps):
         for item in range(items):
             for mask in masks(item, step):
                 copy(item, step, mask).wait_send()
-    own.wait()
-
-
-def ctx_gather(block, cid):
+
+
+def attend_all(q, k, v, cosine, sine, start, tok, key_tok, cid):
     count = lax.axis_size("ctx")
-    items, rows, cols = block.shape
-    dma = pltpu.SemaphoreType.DMA((items, count))
+    seqs, rows, cols = q.shape
+    heads = cols // HD
+    dma = pltpu.SemaphoreType.DMA((2 * seqs, count))
+    shape = jax.ShapeDtypeStruct
+    args = (q, k, v, cosine, sine, start, tok, key_tok)
+    outs = [
+        shape((2 * seqs, count, rows, HD), BF16),
+        shape(q.shape, F32),
+        shape(q.shape, BF16),
+        shape((seqs, heads, rows, 1), F32),
+        shape(q.shape, BF16),
+    ]
     return pl.pallas_call(
-        functools.partial(ctx_gather_kernel, count, items),
-        out_shape=jax.ShapeDtypeStruct((items, count, rows, cols), block.dtype),
-        in_specs=[pl.BlockSpec(memory_space=VMEM)],
-        out_specs=pl.BlockSpec(memory_space=VMEM),
-        scratch_shapes=[dma, dma, pltpu.SemaphoreType.DMA],
+        functools.partial(attend_kernel, count, seqs, heads),
+        out_shape=outs,
+        in_specs=[pl.BlockSpec(memory_space=VMEM)] * len(args),
+        out_specs=[pl.BlockSpec(memory_space=VMEM)] * len(outs),
+        scratch_shapes=[dma, dma],
         compiler_params=pltpu.CompilerParams(
             collective_id=cid, has_side_effects=True, vmem_limit_bytes=56 * MIB
         ),
-        cost_estimate=takes(55),
-        name="ctx_gather",
-    )(block)
-
-
-def ctx_scatter_kernel(count, items, part, out, landed, sendbuf, send_sem, recv_sem):
+        cost_estimate=takes(60),
+        name="attend",
+    )(*args)
+
+
+def attend_back_kernel(count, seqs, heads, *refs):
+    queries, whole, out_grad, attn, sums, cosine, sine, start, tok, key_tok = refs[:10]
+    grads, part, landed, sendbuf, query_grad, send_sem, recv_sem = refs[10:]
     me = lax.axis_index("ctx")
     steps = count.bit_length() - 1
-    orders = [order[::-1] for order in ctx_orders(items, steps)]
+    items = 2 * seqs
+    orders = ctx_orders(items, steps)
+    rows = queries.shape[1]
+    scale = HD ** (-0.5)
     greet("ctx", count)
 
     def copy(item, step, sub):
-        bit = 1 << orders[item][step]
+        order = orders[item]
+        bit = 1 << order[step]
         mask = bit | sub
-        first = orders[item][0]
-        src = part.at[item, flipped(me, mask)] if step == 0 else sendbuf.at[item, without(mask, first)]
+        if step == 0:
+            src = part.at[item, flipped(me, mask)]
+        else:
+            src = sendbuf.at[item, without(mask, order[0])]
         return remote(
             "ctx", src, landed.at[item, mask], (send_sem, recv_sem), (item, mask), flipped(me, bit)
         )
@@ -267,39 +330,83 @@
     def subs(item, step):
         return submasks(orders[item][step + 1 :])
 
-    for item in range(items):
-        for sub in subs(item, 0):
-            copy(item, 0, sub).start()
-    for item, got in wavefront(items, steps):
+    def backward(s):
+        keys = whole[2 * s].reshape(count * rows, HD)
+        values = whole[2 * s + 1].reshape(count * rows, HD)
+        allowed = (key_tok[...] <= tok[...]) & (key_tok[...] >= start[s])
+        key_grad, value_grad = None, None
+        for h in range(heads):
+            at = slice(h * HD, (h + 1) * HD)
+            query, total = queries[s, :, at], sums[s, h]
+            raw = lax.dot_general(query, keys, (((1,), (1,)), ((), ())), preferred_element_type=F32)
+            tanh = jnp.tanh(raw * (scale / CAP))
+            exps = jnp.where(allowed, jnp.exp(CAP * tanh), 0.0)
+            og = out_grad[s, :, at]
+            low = (og / total).astype(BF16)
+            shift = jnp.sum(og * attn[s, :, at], axis=-1, keepdims=True) / total
+            toward = lax.dot_general(
+                low, values, (((1,), (1,)), ((), ())), preferred_element_type=F32
+            )
+            score = (exps * (toward - shift) * (scale * (1.0 - tanh * tanh))).astype(BF16)
+            grad = jnp.dot(score, keys, preferred_element_type=F32)
+            query_grad[s, :, at] = grad
+            across = (((0,), (0,)), ((), ()))
+            k_term = lax.dot_general(score, query, across, preferred_element_type=F32)
+            v_term = lax.dot_general(exps.astype(BF16), low, across, preferred_element_type=F32)
+            key_grad = k_term if h == 0 else key_grad + k_term
+            value_grad = v_term if h == 0 else value_grad + v_term
+        part[2 * s] = key_grad.astype(BF16).reshape(count, rows, HD)
+        part[2 * s + 1] = value_grad.astype(BF16).reshape(count, rows, HD)
+
+    def advance(item, got):
         for sub in subs(item, got):
             copy(item, got, sub).wait_recv()
         step = got + 1
         if step == steps:
-            out[item] = total_of(item, 0, steps)
-            continue
+            s, total = item // 2, total_of(item, 0, steps)
+            if item % 2 == 0:
+                total = rotated(total, cosine[s], -sine[s])
+            lane = heads * HD + (item % 2) * HD
+            grads[s, :, lane : lane + HD] = total.astype(BF16)
+            return
         for sub in subs(item, step):
             mask = 1 << orders[item][step] | sub
-            slot = without(mask, orders[item][0])
-            sendbuf[item, slot] = total_of(item, mask, step).astype(BF16)
+            sendbuf[item, without(mask, orders[item][0])] = total_of(item, mask, step).astype(BF16)
             copy(item, step, sub).start()
+
+    for s in range(seqs):
+        backward(s)
+        for item in (2 * s, 2 * s + 1):
+            for sub in subs(item, 0):
+                copy(item, 0, sub).start()
+    for s in range(seqs):
+        for h in range(heads):
+            at = slice(h * HD, (h + 1) * HD)
+            grads[s, :, at] = rotated(query_grad[s, :, at], cosine[s], -sine[s]).astype(BF16)
+    for item, got in scatter_events(orders):
+        advance(item, got)
     for step in range(steps):
         for item in range(items):
             for sub in subs(item, step):
                 copy(item, step, sub).wait_send()
 
 
-def ctx_scatter(part, cid):
+def attend_back_some(queries, whole, out_grad, attn, sums, cosine, sine, start, tok, key_tok, cid):
     count = lax.axis_size("ctx")
-    items, _, rows, cols = part.shape
-    dma = pltpu.SemaphoreType.DMA((items, count))
+    seqs, rows, cols = queries.shape
+    heads = cols // HD
+    dma = pltpu.SemaphoreType.DMA((2 * seqs, count))
+    args = (queries, whole, out_grad, attn, sums, cosine, sine, start, tok, key_tok)
     return pl.pallas_call(
-        functools.partial(ctx_scatter_kernel, count, items),
-        out_shape=jax.ShapeDtypeStruct((items, rows, cols), F32),
-        in_specs=[pl.BlockSpec(memory_space=VMEM)],
+        functools.partial(attend_back_kernel, count, seqs, heads),
+        out_shape=jax.ShapeDtypeStruct((seqs, rows, cols + 2 * HD), BF16),
+        in_specs=[pl.BlockSpec(memory_space=VMEM)] * len(args),
         out_specs=pl.BlockSpec(memory_space=VMEM),
         scratch_shapes=[
-            VMEM(part.shape, BF16),
-            VMEM((items, count // 2, rows, cols), BF16),
+            VMEM(whole.shape, BF16),
+            VMEM(whole.shape, BF16),
+            VMEM((2 * seqs, max(count // 2, 1), rows, HD), BF16),
+            VMEM(queries.shape, F32),
             dma,
             dma,
         ],
@@ -307,20 +414,37 @@
             collective_id=cid, has_side_effects=True, vmem_limit_bytes=56 * MIB
         ),
         cost_estimate=takes(60),
-        name="ctx_scatter",
-    )(part)
-
-
-def pairs_of(b):
-    return [(i, i ^ (1 << b)) for i in range(lax.axis_size("ctx"))]
+        name="attend_back",
+    )(*args)
+
+
+def attend_back(queries, whole, out_grad, attn, sums, cosine, sine, start, tok, key_tok, cid):
+    seqs = queries.shape[0]
+    size = max(1, min(seqs, 8 * seqs // whole.shape[1]))
+    grads = []
+    for i, s in enumerate(range(0, seqs, size)):
+        e = min(s + size, seqs)
+        some = (queries[s:e], whole[2 * s : 2 * e], out_grad[s:e], attn[s:e], sums[s:e])
+        near = (cosine[s:e], sine[s:e], start[s:e], tok, key_tok)
+        grads.append(attend_back_some(*some, *near, cid + i))
+    return grads[0] if len(grads) == 1 else jnp.concatenate(grads, 0)
+
+
+def send_ctx(value, mask):
+    return lax.ppermute(value, "ctx", [(i, i ^ mask) for i in range(lax.axis_size("ctx"))])
+
+
+def send_core(value):
+    return lax.ppermute(value, "tp", [(i, i ^ 1) for i in range(lax.axis_size("tp"))])
 
 
 class Halving:
-    def __init__(self, part, order):
+    def __init__(self, part, order, but=None):
+        steps = lax.axis_size("ctx").bit_length() - 1
         self.order = list(order)
-        self.left = sorted(order, reverse=True)
-        owners = 1 << len(self.order)
-        self.total = part.reshape((2,) * len(self.order) + (part.shape[0] // owners, part.shape[1]))
+        self.left = [b for b in range(steps)[::-1] if b != but]
+        owners = 1 << len(self.left)
+        self.total = part.reshape((2,) * len(self.left) + (part.shape[0] // owners, part.shape[1]))
 
     def send(self):
         b = self.order.pop(0)
@@ -328,44 +452,84 @@
         self.left.remove(b)
         mine = (lax.axis_index("ctx") >> b) & 1
         pick = functools.partial(lax.dynamic_index_in_dim, axis=axis, keepdims=False)
-        self.got = lax.ppermute(pick(self.total, 1 - mine), "ctx", pairs_of(b))
+        self.gots = [send_ctx(pick(self.total, 1 - mine), 1 << b)]
         self.keep = pick(self.total, mine)
 
     def add(self):
-        self.total = self.keep.astype(F32) + self.got.astype(F32)
+        self.total = (self.keep.astype(F32) + self.gots[0].astype(F32)).astype(BF16)
+
+    def step(self):
+        self.add()
         if self.order:
-            self.total = self.total.astype(BF16)
+            self.send()
+        else:
+            del self.gots
 
     def finish(self):
-        self.add()
-        while self.order:
+        if self.order and not hasattr(self, "gots"):
             self.send()
+        while hasattr(self, "gots"):
             self.add()
+            del self.gots
+            if self.order:
+                self.send()
         return self.total
 
 
-class Swap:
+class Sent:
     def __init__(self, value, b):
-        self.got = lax.ppermute(value, "ctx", pairs_of(b))
-
-
-def owner_half(rows_of_owners, b, which):
-    total, cols = rows_of_owners.shape
-    low = (total // lax.axis_size("ctx")) << b
-    cut = rows_of_owners.reshape(total // (2 * low), 2, low, cols)
-    return lax.dynamic_index_in_dim(cut, which, 1, keepdims=False).reshape(total // 2, cols)
-
-
-def pin(value, *halvings):
-    value, gots = lax.optimization_barrier((value, [h.got for h in halvings]))
-    for h, got in zip(halvings, gots):
-        h.got = got
+        self.gots = [send_ctx(value, 1 << b)]
+
+
+class CoreSent(Sent):
+    def __init__(self, value):
+        self.gots = [send_core(value)]
+
+
+def pin(value, *sent):
+    value, gots = lax.optimization_barrier((value, [s.gots for s in sent]))
+    for s, got in zip(sent, gots):
+        s.gots = got
     return value
 
 
-def cube_order(steps, turn):
-    usual = list(range(steps))
-    return usual if turn == 0 or steps < 2 else [1, 0] + usual[2:]
+def product_kernel(own, far, near, mine, got, out):
+    core = lax.axis_index("tp") % 2
+    cols = mine.shape[-1]
+
+    def times(left, right):
+        return lax.dot_general(
+            left, right.reshape(-1, cols), (((0,), (0,)), ((), ())), preferred_element_type=F32
+        )
+
+    total = times(own[...], mine[...])
+    total = total + times(far[...], got[:, :, :, core])
+    total = total + times(near[...], got[:, :, :, 1 - core])
+    out[...] = total.astype(BF16)
+
+
+def product(own, far, near, mine, got, name):
+    rows, width = own.shape
+    cols, tile = mine.shape[-1], 256 if width % 256 == 0 else 384
+    whole = pl.BlockSpec(mine.shape, lambda i: (0,) * mine.ndim)
+    return pl.pallas_call(
+        product_kernel,
+        grid=(width // tile,),
+        out_shape=jax.ShapeDtypeStruct((width, cols), BF16),
+        in_specs=[
+            pl.BlockSpec((rows, tile), lambda i: (0, i)),
+            pl.BlockSpec((rows // 2, tile), lambda i: (0, i)),
+            pl.BlockSpec((rows // 2, tile), lambda i: (0, i)),
+            whole,
+            whole,
+        ],
+        out_specs=pl.BlockSpec((tile, cols), lambda i: (i, 0)),
+        compiler_params=pltpu.CompilerParams(vmem_limit_bytes=40 * MIB),
+        cost_estimate=pl.CostEstimate(
+            flops=4 * rows * width * cols, bytes_accessed=0, transcendentals=0
+        ),
+        name=name,
+    )(own, far, near, mine, got)
 
 
 def weights_scatter_kernel(count, tp_count, plan, n_parts, *refs):
@@ -440,7 +604,7 @@
             gains_out[...] = both
         go.wait_send()
 
-    for n, got in wavefront(len(plan), steps):
+    for n, got in scatter_events([order for _, _, order in plan]):
         p, item, order = plan[n]
         for sub in subs(order, got):
             copy(n, got, sub).wait_recv()
@@ -465,7 +629,8 @@
     cut = max(c for c in range(1, 7) if rows % (16 * c) == 0) if rows % 16 == 0 else 1
     blocks = [p.reshape(count, cut, rows // cut, p.shape[1]) for p in parts]
     pairs = [(p, item) for item in range(cut) for p in range(len(parts))]
-    plan = [(p, item, cube_order(steps, int(n % 4 == 3))) for n, (p, item) in enumerate(pairs)]
+    orders = ctx_orders(len(pairs), steps)
+    plan = [(p, item, order) for (p, item), order in zip(pairs, orders)]
     hops = steps + tp_count.bit_length() - 1
     dma = pltpu.SemaphoreType.DMA((len(plan), count))
     out = pl.pallas_call(
@@ -546,12 +711,6 @@
     dv, dg = rms_back(normed_grad, tokens[item].astype(F32), gain[...].astype(F32))
     add_to(gain_grad, item, dg)
     tokens_grad[item] = resid_grad[item] + dv
-
-
-def rotate(values, cosine, sine):
-    half_dim = values.shape[-1] // 2
-    low, high = values[..., :half_dim], values[..., half_dim:]
-    return jnp.concatenate([low * cosine - high * sine, high * cosine + low * sine], -1)
 
 
 def gelu_times(gate, up_val):
@@ -583,12 +742,9 @@
     rows = stretch * slots
     all_rows = seqs * rows
     local_heads = query_weight.shape[1] // HD
-    local_kv = key_weight.shape[1] // HD
-    group = local_heads // local_kv
-    scale = HD ** (-0.5)
+    assert key_weight.shape[1] == value_weight.shape[1] == HD
     own = (seqs, slots, stretch_rows, width)
     steps = ctx_count.bit_length() - 1
-    usual, other = cube_order(steps, 0), cube_order(steps, 1)
 
     slot_stretch = jnp.stack([ctx_rank, 2 * ctx_count - 1 - ctx_rank])
     iota = jnp.arange(stretch, dtype=jnp.int32)
@@ -604,14 +760,11 @@
     row_pos = row_tok[None] - row_start
     frequency = BASE ** (-jnp.arange(HD // 2).astype(F32) / (HD // 2))
     angles = row_pos.astype(F32)[..., None] * frequency
-    cosine = jnp.cos(angles)[:, :, None, :]
-    sine = jnp.sin(angles)[:, :, None, :]
+    cosine, sine = jnp.cos(angles), jnp.sin(angles)
     key_slot = jnp.arange(2 * ctx_count, dtype=jnp.int32)
     key_stretch = jnp.where(key_slot % 2 == 0, key_slot // 2, 2 * ctx_count - 1 - key_slot // 2)
     key_tok = (key_stretch[:, None] * stretch + iota[None, :]).reshape(length)
-    allowed = (key_tok[None, None, :] <= row_tok[None, :, None]) & (
-        key_tok[None, None, :] >= row_start[:, :, None]
-    )
+    where = (row_start[..., None], row_tok[:, None], key_tok[None, :])
 
     def wide(gain):
         return gain.reshape(1, width)
@@ -625,29 +778,13 @@
     normed_all = normed_all.reshape(all_rows, width)
     dot = functools.partial(jnp.dot, preferred_element_type=F32)
     ein = functools.partial(jnp.einsum, preferred_element_type=F32)
-    keys = rotate(
-        dot(normed_all, key_weight).reshape(seqs, rows, local_kv, HD), cosine, sine
-    ).astype(BF16)
-    values = dot(normed_all, value_weight).astype(BF16)
-    queries = rotate(
-        dot(normed_all, query_weight).reshape(seqs, rows, local_heads, HD), cosine, sine
-    ).astype(BF16)
-    kv = jnp.concatenate(
-        [keys.reshape(seqs, rows, local_kv * HD), values.reshape(seqs, rows, local_kv * HD)], 0
-    )
-    kv_all = ctx_gather(kv, 2).reshape(2, seqs, length, local_kv, HD)
-    keys_all, values_all = kv_all[0], kv_all[1]
-    grouped = queries.reshape(seqs, rows, local_kv, group, HD)
-
-    raw = ein("srkgd,sukd->skgru", grouped, keys_all)
-    tanh = jnp.tanh(raw * (scale / CAP))
-    exps = jnp.where(allowed[:, None, None], jnp.exp(CAP * tanh), 0.0)
-    total = jnp.sum(exps, axis=-1)
-    exps_low = exps.astype(BF16)
-    attn = ein("skgru,sukd->srkgd", exps_low, values_all)
-    total_rows = jnp.transpose(total, (0, 3, 1, 2))[..., None]
-    attn = attn / total_rows
-    attn_rows = attn.astype(BF16).reshape(all_rows, local_heads * HD)
+    queries = dot(normed_all, query_weight).reshape(seqs, rows, local_heads * HD)
+    keys = dot(normed_all, key_weight).reshape(seqs, rows, HD)
+    values = dot(normed_all, value_weight).reshape(seqs, rows, HD)
+    kv_all, attn, attn_low, sums, queries = attend_all(
+        queries, keys, values, cosine, sine, *where, 2
+    )
+    attn_rows = attn_low.reshape(all_rows, local_heads * HD)
     part = dot(attn_rows, output_weight).astype(BF16)
 
     def by_owner(value):
@@ -662,18 +799,51 @@
         by_owner(part),
     )
     ffw_all = ffw_all.reshape(all_rows, width)
-    pair = min(1, steps - 1)
-    others = [b for b in usual if b != pair]
-    pair_bit = (ctx_rank >> pair) & 1
-    ffw_turned = ffw_all.T
-    ffw_mine = owner_half(ffw_turned, pair, pair_bit)
-    ffw_swap = Swap(owner_half(ffw_turned, pair, 1 - pair_bit), pair)
+    low_bit, next_bit, far_bit = 0, min(1, steps - 1), steps - 1
+    high = list(range(2, steps))
+    core = lax.axis_index("tp") % 2
+    pick = functools.partial(lax.dynamic_index_in_dim, keepdims=False)
+
+    def by_core(value):
+        return value.reshape((seqs, slots, tp_count // 2, 2, stretch_rows, value.shape[-1]))
+
+    def core_rows(value):
+        return pick(by_core(value), core, 3).reshape(all_rows // 2, value.shape[-1])
+
+    def halves(value, b):
+        bit = (ctx_rank >> b) & 1
+        cut = value.shape[1] // 2
+        return [
+            by_core(lax.dynamic_slice_in_dim(value, at * cut, cut, 1)) for at in (bit, 1 - bit)
+        ]
+
+    def owner_cols(value):
+        bit = (ctx_rank >> far_bit) & 1
+        cut = value.shape[1] // 2
+        return [lax.dynamic_slice_in_dim(value, at * cut, cut, 1) for at in (bit, 1 - bit)]
+
+    def owner_pieces(total, b):
+        bit = (ctx_rank >> b) & 1
+        cut = total.reshape(2, -1, total.shape[-1])
+        return pick(cut, bit, 0), pick(cut, 1 - bit, 0)
+
+    def whole_cols(own_half, got_half, b):
+        bit = (ctx_rank >> b) & 1
+        first = jnp.where(bit == 0, own_half, got_half)
+        second = jnp.where(bit == 0, got_half, own_half)
+        return jnp.concatenate([first, second], 1).astype(F32)
+
+    ffw_send = core_rows(ffw_all)
+    ffw_all, ffw_send = lax.optimization_barrier((ffw_all, ffw_send))
+    ffw_far, ffw_far_low = Sent(ffw_send, next_bit), Sent(ffw_send, low_bit)
     gate = dot(ffw_all, gate_weight)
     up = dot(ffw_all, up_weight)
     mixed, mixed_back = jax.vjp(gelu_times, gate, up)
     mixed = mixed.astype(BF16)
-    mixed_swap = Swap(mixed, pair)
-    part = pin(dot(mixed, down_weight).astype(BF16), ffw_swap)
+    mixed_sent = Sent(by_core(mixed), far_bit)
+    part = dot(mixed, down_weight).astype(BF16)
+    part = pin(part, ffw_far, ffw_far_low)
+    ffw_near, ffw_near_low = CoreSent(ffw_far.gots[0]), CoreSent(ffw_far_low.gots[0])
     ffw_grad_all, layer_out, ffw_out_gain_part = tp_exchange(
         "turn",
         4,
@@ -683,18 +853,50 @@
         by_owner(part),
     )
     ffw_grad_all = ffw_grad_all.reshape(all_rows, width)
-    grad_turned = ffw_grad_all.T
-    grad_mine = owner_half(grad_turned, pair, pair_bit)
-    grad_swap = Swap(owner_half(grad_turned, pair, 1 - pair_bit), pair)
+    grad_half, grad_give = owner_cols(ffw_grad_all)
+    grad_send = core_rows(grad_give)
+    ffw_grad_all, grad_send = lax.optimization_barrier((ffw_grad_all, grad_send))
+    grad_far = Sent(grad_send, far_bit)
     mixed_grad = ein("rd,fd->rf", ffw_grad_all, down_weight)
     gate_grad, up_grad = mixed_back(mixed_grad)
     gate_grad = gate_grad.astype(BF16)
     up_grad = up_grad.astype(BF16)
-    gate_swap = Swap(gate_grad, pair)
-    up_swap = Swap(up_grad, pair)
+    gate_half, gate_give = halves(gate_grad, low_bit)
+    up_half, up_give = halves(up_grad, next_bit)
+    gate_grad, up_grad, gate_give, up_give = lax.optimization_barrier(
+        (gate_grad, up_grad, gate_give, up_give)
+    )
+    gate_sent, up_sent = Sent(gate_give, low_bit), Sent(up_give, next_bit)
     part = (
         ein("rf,df->rd", gate_grad, gate_weight) + ein("rf,df->rd", up_grad, up_weight)
     ).astype(BF16)
+    part = pin(part, gate_sent, ffw_near, ffw_near_low)
+    gate_part = product(
+        ffw_all, ffw_far_low.gots[0], ffw_near_low.gots[0], gate_half, gate_sent.gots[0], "gate_product"
+    )
+    gates = Halving(gate_part, [next_bit] + high)
+    gates.send()
+    part, gate_part = lax.optimization_barrier((part, gate_part))
+    part = pin(part, up_sent)
+    up_part = product(
+        ffw_all, ffw_far.gots[0], ffw_near.gots[0], up_half, up_sent.gots[0], "up_product"
+    )
+    ups = Halving(up_part, [low_bit] + high)
+    ups.send()
+    part, up_part = lax.optimization_barrier((part, up_part))
+    part = pin(part, grad_far, mixed_sent)
+    grad_near = CoreSent(grad_far.gots[0])
+    down_part = product(
+        grad_half,
+        grad_far.gots[0],
+        grad_near.gots[0],
+        by_core(mixed),
+        mixed_sent.gots[0],
+        "down_product",
+    )
+    down = Halving(down_part, [b for b in range(steps) if b != far_bit], far_bit)
+    down.send()
+    part, down_part = lax.optimization_barrier((part, down_part))
     branch_grad_all, resid_grad, ffw_in_gain_part, attn_out_gain_part = tp_exchange(
         "middle_back",
         5,
@@ -703,40 +905,15 @@
         [f32_rows, gain_shape, gain_shape],
         by_owner(part),
     )
-    branch_grad_all = pin(branch_grad_all.reshape(all_rows, width), ffw_swap, mixed_swap, grad_swap)
-    down = Halving((dot(grad_mine, mixed) + dot(grad_swap.got, mixed_swap.got)).astype(BF16), others)
-    down.send()
+    branch_grad_all = branch_grad_all.reshape(all_rows, width)
     output_part = ein("rd,rh->dh", branch_grad_all, attn_rows).astype(BF16)
     attn_grad = ein("rd,hd->rh", branch_grad_all, output_weight).reshape(attn.shape)
-    row_dot = jnp.sum(attn_grad * attn, axis=-1)
-    scaled = (attn_grad / total_rows).astype(BF16)
-    shift = jnp.transpose(row_dot, (0, 2, 3, 1)) / total
-    weight_grad = ein("srkgd,sukd->skgru", scaled, values_all)
-    score_grad = (
-        exps * (weight_grad - shift[..., None]) * (scale * (1.0 - tanh * tanh))
-    ).astype(BF16)
-    query_acc = ein("skgru,sukd->srkgd", score_grad, keys_all)
-    key_acc = ein("skgru,srkgd->sukd", score_grad, grouped)
-    value_acc = ein("skgru,srkgd->sukd", exps_low, scaled)
-    kv_acc = jnp.concatenate([key_acc, value_acc], 0).astype(BF16)
-    kv_acc = pin(kv_acc, gate_swap, down)
-    down.add()
-    down.send()
-    gates = Halving((dot(ffw_mine, gate_grad) + dot(ffw_swap.got, gate_swap.got)).astype(BF16), others)
-    gates.send()
-    kv_sum = ctx_scatter(kv_acc.reshape(2 * seqs, ctx_count, rows, local_kv * HD), 6)
-    kv_sum = pin(kv_sum, up_swap, gates, down)
-    down_sum = down.finish()
-    gates.add()
-    gates.send()
-    ups = Halving((dot(ffw_mine, up_grad) + dot(ffw_swap.got, up_swap.got)).astype(BF16), others)
-    ups.send()
-    key_grad = rotate(kv_sum[:seqs].reshape(seqs, rows, local_kv, HD), cosine, -sine)
-    key_grad = key_grad.astype(BF16).reshape(all_rows, local_kv * HD)
-    value_grad = kv_sum[seqs:].astype(BF16).reshape(all_rows, local_kv * HD)
-    query_grad = rotate(query_acc.reshape(seqs, rows, local_heads, HD), cosine, -sine)
-    query_grad = query_grad.astype(BF16).reshape(all_rows, local_heads * HD)
-    qkv_grad = jnp.concatenate([query_grad, key_grad, value_grad], 1)
+    attn_grad = pin(attn_grad, gates)
+    gates.step()
+    qkv_grad = attend_back(queries, kv_all, attn_grad, attn, sums, cosine, sine, *where, 16)
+    qkv_grad = pin(qkv_grad, down, ups).reshape(all_rows, -1)
+    ups.step()
+    down.step()
     qkv_weight = jnp.concatenate([query_weight, key_weight, value_weight], 1)
     part = ein("rh,dh->rd", qkv_grad, qkv_weight).astype(BF16)
     qkv_part = ein("rd,rh->dh", normed_all, qkv_grad).astype(BF16)
@@ -752,15 +929,19 @@
     gains = jnp.concatenate(
         [attn_in_gain_part, attn_out_gain_part, ffw_in_gain_part, ffw_out_gain_part], 0
     )
-    gains = pin(gains, ups)
-    ups.add()
-    ups.send()
     (output_sum, qkv_sum), gains = weights_scatter([output_part, qkv_part], gains, 8)
-    gate_sum, up_sum = gates.finish(), ups.finish()
+    gains = pin(gains, gates, ups, down)
+    gate_own, gate_give = owner_pieces(gates.finish(), low_bit)
+    gate_sent = Sent(gate_give, low_bit)
+    up_own, up_give = owner_pieces(ups.finish(), next_bit)
+    up_sent = Sent(up_give, next_bit)
+    down_sum = down.finish().astype(F32)
+    gate_sum = whole_cols(gate_own, gate_sent.gots[0], low_bit)
+    up_sum = whole_cols(up_own, up_sent.gots[0], next_bit)
     share = width // ctx_count
     gains = lax.dynamic_slice_in_dim(gains, ctx_rank * share, share, 1)
     heads_end = local_heads * HD
-    keys_end = heads_end + local_kv * HD
+    keys_end = heads_end + HD
     return (
         jnp.transpose(layer_out, (2, 0, 1, 3)),
         jnp.transpose(tokens_grad, (2, 0, 1, 3)),

time: 836 us -> 752 us (0.90)
  matrix products: 174 us -> 107 us
  Pallas kernels: 435 us -> 492 us
  local copies, waits for them, and re-layouts: 86.2 us -> 52.6 us
  waiting for transfers between devices: 88.2 us -> 57.5 us
    dot_general x16 -> x4, matrix products: 92.5 us -> 18.1 us  [the longest x1 11.8 us: body(): part = dot(mixed, down_weight).astype(BF16)]
    pallas_call x2 -> x5, Pallas kernels: 168 us -> 210 us  [the longest x1 103 us: attend_back_some(): pl.pallas_call(functools.partial(attend_back_kernel, count, seqs, heads),...]
    ppermute x11 -> x17, waiting for transfers between devices: 88.2 us -> 57.5 us  [the longest x14 57.5 us: send_ctx(): lax.ppermute(value, 'ctx', [(i, i ^ mask) for i in range(lax.axis_size('c...]
    reshape x7 -> x0, local copies, waits for them, and re-layouts: 24 us -> none  [the longest x4 12.8 us: body(): ein('rd,hd->rh', branch_grad_all, output_weight).reshape(attn.shape)]
    pallas_call x1, Pallas kernels: 112 us -> 127 us  [weights_scatter(): pl.pallas_call(functools.partial(weights_scatter_kernel, count, tp_count,...]
    unnamed x151 -> x101, local copies, waits for them, and re-layouts: 20.9 us -> 25.7 us
  transfers between devices with their start and end apart: 11 -> 17, of which waited for: 4 -> 4; matrix products, arithmetic and copies ran while one was open for 26% -> 19% of each run, Pallas kernels for 37% -> 49%
where the time goes in v4:
time: 752 us; the launch traced here: 748 us
  Pallas kernels  492 us (65%)
  matrix products  107 us (14%)
  waiting for transfers between devices  57.5 us (8%)
  local copies, waits for them, and re-layouts  52.6 us (7%)
  other arithmetic  23.7 us (3%)
  starting transfers between devices  14.3 us (2%)
    pallas_call x5, Pallas kernels, tp_exchange(): pl.pallas_call(functools.partial(tp_kernel, fn, count, items, len(ins), l...  154 us
    pallas_call x1, Pallas kernels, weights_scatter(): pl.pallas_call(functools.partial(weights_scatter_kernel, count, tp_count,...  127 us
    pallas_call x1, Pallas kernels, attend_back_some(): pl.pallas_call(functools.partial(attend_back_kernel, count, seqs, heads),...  103 us
    pallas_call x1, Pallas kernels, attend_all(): pl.pallas_call(functools.partial(attend_kernel, count, seqs, heads), out_...  65.2 us
    ppermute x14, waiting for transfers between devices, send_ctx(): lax.ppermute(value, 'ctx', [(i, i ^ mask) for i in range(lax.axis_size('c...  57.5 us
    pallas_call x3, Pallas kernels, product(): pl.pallas_call(product_kernel, grid=(width // tile,), out_shape=jax.Shape...  41.7 us
    unnamed x101, local copies, waits for them, and re-layouts  25.7 us
    dot_general x1, matrix products, body(): mixed_grad = ein('rd,fd->rf', ffw_grad_all, down_weight)  17 us
  transfers between devices with their start and end apart: 17, of which 4 were waited for; matrix products, arithmetic and copies ran while one was open for 19% of the time, Pallas kernels for 49%

profile of v4, /device:TPU:0, one launch (start us, length us, event | category | flops | bytes accessed | tf_op | source)
XLA Modules:
  0.0 748.1 jit_solution(18306840235437162789)
XLA Ops:
  4.6 1.3 copy.60
  6.7 21.6 %enter.1 = bf16[5,2,4,16,2304]{4,3,2,1,0:T(8,128)(2,1)S(1)} custom-call(bf16[5,2,16,2304]{3,2,1,0:T(8,128)(2,1)S(1)} %bitcast.122, bf16[1,2304]{1,0:T(2,128)(2,1)S(1)} %reshape.269.refs_1_.refs_3_), custom_call_target="tpu_custom_call" | custom-call | flops 180000000 | tf_op jit(solution)/shard_map/enter/pallas_call | solution.py:178
  28.3 2.7 fusion.20.q
  31.1 1.8 fusion.22.v
  32.9 1.8 fusion.24.k
  35.4 2.3 multiply_sine_fusion
  37.8 65.2 %attend.1 = (bf16[10,8,128,256]{3,2,1,0:T(8,128)(2,1)}, f32[5,128,512]{2,1,0:T(8,128)}, bf16[5,128,512]{2,1,0:T(8,128)(2,1)}, f32[5,2,128,1]{3,2,1,0:T(8,128)}, bf16[5,128,512]{2,1,0:T(8,128)(2,1)}) custom-call(f32[5,128,512]{2,1,0:T(8,128)} %fusion.20.q, f32[5,128,256]{2,1,0:T(8,128)} %fusion.24.k, f32[5,128,256]{2,1,0:T(8,128)} %fusion.22.v, ...), custom_call_target="tpu_custom_call" | custom-call | flops 600000000 | tf_op jit(solution)/shard_map/attend/pallas_call | solution.py:287
  103.0 4.4 convolution_convert_fusion.2
  107.3 1.8 copy-done.10
  109.2 37.3 %middle.1 = (bf16[5,2,4,16,2304]{4,3,2,1,0:T(8,128)(2,1)S(1)}, f32[5,2,16,2304]{3,2,1,0:T(8,128)S(1)}, f32[5,2,16,2304]{3,2,1,0:T(8,128)S(1)}) custom-call(bf16[5,2,4,16,2304]{4,3,2,1,0:T(8,128)(2,1)S(1)} %bitcast.137, bf16[5,2,16,2304]{3,2,1,0:T(8,128)(2,1)S(1)} %bitcast.123, bf16[1,2304]{1,0:T(2,128)(2,1)S(1)} %reshape.272.refs_2_.refs_5_, ...), custom_call_target="tpu_custom_call" | custom-call | flops 360000000 | tf_op jit(solution)/shard_map/middle/pallas_call | solution.py:178
  146.5 1.3 constant_dynamic-slice_fusion.8
  148.4 13.4 %fusion.30 = f32[640,2304]{1,0:T(8,128)} fusion(bf16[640,2304]{1,0:T(8,128)(2,1)S(1)} %bitcast.149, bf16[2304,2304]{1,0:T(8,128)(2,1)} %param.23), kind=kOutput, calls=%fused_computation.94 | convolution fusion | flops 6794772480 | bytes 19464192 | tf_op jit(solution)/shard_map/dot_general | solution.py:839
  161.8 11.7 %multiply_convert_fusion.1 = (bf16[640,2304]{1,0:T(8,128)(2,1)}, f32[640,2304]{1,0:T(8,128)}) fusion(f32[640,2304]{1,0:T(8,128)} %fusion.30, bf16[640,2304]{1,0:T(8,128)(2,1)S(1)} %bitcast.150, bf16[2304,2304]{1,0:T(8,128)(2,1)S(1)} %bitcast.167), kind=kOutput, calls=%fused_computation.11 | convolution fusion | flops 6809518080 | bytes 28311552 | tf_op jit(solution)/shard_map/dot_general | solution.py:840
  173.5 2.2 collective-permute-start.7
  175.7 2.1 copy.59
  177.8 11.8 %convolution_convert_fusion.1 = bf16[640,2304]{1,0:T(8,128)(2,1)S(1)} fusion(bf16[640,2304]{1,0:T(8,128)(2,1)} %get-tuple-element.178, bf16[2304,2304]{1,0:T(8,128)(2,1)} %param.25), kind=kOutput, calls=%fused_computation.20 | convolution fusion | flops 6796247040 | bytes 16515072 | tf_op jit(solution)/shard_map/dot_general | solution.py:844
  189.7 37.6 %turn.1 = (bf16[5,2,4,16,2304]{4,3,2,1,0:T(8,128)(2,1)S(1)}, bf16[5,2,16,2304]{3,2,1,0:T(8,128)(2,1)S(1)}, f32[1,2304]{1,0:T(1,128)S(1)}) custom-call(bf16[5,2,4,16,2304]{4,3,2,1,0:T(8,128)(2,1)S(1)} %bitcast.143, f32[5,2,16,2304]{3,2,1,0:T(8,128)S(1)} %copy-done.4, bf16[5,2,16,2304]{3,2,1,0:T(8,128)(2,1)S(1)} %bitcast.125, bf16[1,2304]{1,0:T(2,128)(2,1)S(1)} %reshape.277.refs_3_), custom_call_target="tpu_custom_call" | custom-call | flops 360000000 | tf_op jit(solution)/shard_map/turn/pallas_call | solution.py:178
  227.3 1.5 constant_dynamic-slice_fusion.1
  229.7 17.0 %multiply_convert_fusion = (bf16[640,2304]{1,0:T(8,128)(2,1)S(1)}, bf16[640,2304]{1,0:T(8,128)(2,1)}) fusion(f32[640,2304]{1,0:T(8,128)} %fusion.30, f32[640,2304]{1,0:T(8,128)} %get-tuple-element.179, bf16[640,2304]{1,0:T(8,128)(2,1)S(1)} %bitcast.136, bf16[2304,2304]{1,0:T(8,128)(2,1)} %param.25), kind=kOutput, calls=%fused_computation.10 | convolution fusion | flops 6830161920 | bytes 31260672 | tf_op jit(solution)/shard_map/rd,fd->rf/dot_general | solution.py:860
  246.8 5.0 constant_dynamic-slice_fusion.2
  251.8 12.3 %fusion.31 = f32[640,2304]{1,0:T(8,128)} fusion(bf16[640,2304]{1,0:T(8,128)(2,1)S(1)} %copy-done.29, bf16[2304,2304]{1,0:T(8,128)(2,1)} %param.23), kind=kOutput, calls=%fused_computation.95 | convolution fusion | flops 6794772480 | bytes 19464192 | tf_op jit(solution)/shard_map/rf,df->rd/dot_general | solution.py:871
  265.5 1.2 collective-permute-start.5
  266.7 13.8 %add_convert_fusion = bf16[640,2304]{1,0:T(8,128)(2,1)} fusion(f32[640,2304]{1,0:T(8,128)} %fusion.31, bf16[640,2304]{1,0:T(8,128)(2,1)} %copy-done.28, bf16[2304,2304]{1,0:T(8,128)(2,1)} %param.24), kind=kOutput, calls=%fused_computation.9 | convolution fusion | flops 6797721600 | bytes 22413312 | tf_op jit(solution)/shard_map/rf,df->rd/dot_general | solution.py:871
  280.4 18.3 %collective-permute-done.2.got = bf16[5,2,2,2,16,1152]{5,4,3,2,1,0:T(8,128)(2,1)} collective-permute-done((bf16[5,2,2,2,16,1152]{5,4,3,2,1,0:T(8,128)(2,1)}, bf16[5,2,2,2,16,1152]{5,4,3,2,1,0:T(8,128)(2,1)}, u32[]{:S(2)}, u32[]{:S(2)}) %collective-permute-start.2) | collective-permute-done | bytes 1474592 | tf_op jit(solution)/shard_map/ppermute | solution.py:434
  299.2 14.0 %gate_product.1 = bf16[2304,1152]{1,0:T(8,128)(2,1)S(1)} custom-call(bf16[640,2304]{1,0:T(8,128)(2,1)S(1)} %bitcast.151, bf16[320,2304]{1,0:T(8,128)(2,1)} %collective-permute-done.1.far, bf16[320,2304]{1,0:T(8,128)(2,1)} %collective-permute-done.4.near, bf16[5,2,2,2,16,1152]{5,4,3,2,1,0:T(8,128)(2,1)S(1)} %bitcast.146, ...), custom_call_target="tpu_custom_call" | custom-call | flops 6794772480 | tf_op jit(solution)/shard_map/gate_product/pallas_call | solution.py:515
  313.3 2.4 copy-done.8
  315.7 35.3 %collective-permute-done.5.got = bf16[5,2,2,2,16,1152]{5,4,3,2,1,0:T(8,128)(2,1)} collective-permute-done((bf16[5,2,2,2,16,1152]{5,4,3,2,1,0:T(8,128)(2,1)}, bf16[5,2,2,2,16,1152]{5,4,3,2,1,0:T(8,128)(2,1)}, u32[]{:S(2)}, u32[]{:S(2)}) %collective-permute-start.5) | collective-permute-done | bytes 1474592 | tf_op jit(solution)/shard_map/ppermute | solution.py:434
  351.0 14.0 %up_product.1 = bf16[2304,1152]{1,0:T(8,128)(2,1)S(1)} custom-call(bf16[640,2304]{1,0:T(8,128)(2,1)S(1)} %bitcast.152, bf16[320,2304]{1,0:T(8,128)(2,1)} %collective-permute-done.far, bf16[320,2304]{1,0:T(8,128)(2,1)} %collective-permute-done.3.near, bf16[5,2,2,2,16,1152]{5,4,3,2,1,0:T(8,128)(2,1)S(1)} %bitcast.145, ...), custom_call_target="tpu_custom_call" | custom-call | flops 6794772480 | tf_op jit(solution)/shard_map/up_product/pallas_call | solution.py:515
  365.0 2.4 copy-done.6
  367.4 3.6 dynamic-slice_bitcast_fusion.2
  371.3 1.7 dynamic-slice_bitcast_fusion
  373.0 1.3 collective-permute-start.11
  374.3 13.7 %down_product.1 = bf16[1152,2304]{1,0:T(8,128)(2,1)S(1)} custom-call(bf16[640,1152]{1,0:T(8,128)(2,1)S(1)} %copy-done.16, bf16[320,1152]{1,0:T(8,128)(2,1)} %collective-permute-done.6.far, bf16[320,1152]{1,0:T(8,128)(2,1)} %collective-permute-done.8.near, bf16[5,2,2,2,16,2304]{5,4,3,2,1,0:T(8,128)(2,1)} %bitcast.23.mine, ...), custom_call_target="tpu_custom_call" | custom-call | flops 6794772480 | tf_op jit(solution)/shard_map/down_product/pallas_call | solution.py:515
  388.0 2.3 copy-done.9
  390.3 1.7 dynamic-slice_bitcast_fusion.1
  392.7 2.5 copy.53
  396.4 1.4 copy-done.5
  397.7 1.8 copy-done.13
  399.6 1.4 copy-done.15
  400.9 37.8 %middle_back.1 = (bf16[5,2,4,16,2304]{4,3,2,1,0:T(8,128)(2,1)S(1)}, f32[5,2,16,2304]{3,2,1,0:T(8,128)S(1)}, f32[1,2304]{1,0:T(1,128)S(1)}, f32[1,2304]{1,0:T(1,128)S(1)}) custom-call(bf16[5,2,4,16,2304]{4,3,2,1,0:T(8,128)(2,1)S(1)} %bitcast.142, f32[5,2,16,2304]{3,2,1,0:T(8,128)S(1)} %copy-done.5, f32[5,2,16,2304]{3,2,1,0:T(8,128)S(1)} %copy-done.15, ...), custom_call_target="tpu_custom_call" | custom-call | flops 360000000 | tf_op jit(solution)/shard_map/middle_back/pallas_call | solution.py:178
  438.7 3.5 convolution_convert_fusion.4
  442.3 2.8 fusion.18.refs_2_
  445.1 2.4 fusion.9
  447.5 1.5 copy-done.22
  449.1 2.7 collective-permute-start.12
  451.9 103.3 %attend_back.1 = bf16[5,128,1024]{2,1,0:T(8,128)(2,1)} custom-call(bf16[5,128,512]{2,1,0:T(8,128)(2,1)} %get-tuple-element.72.refs_0_, bf16[10,8,128,256]{3,2,1,0:T(8,128)(2,1)} %get-tuple-element.73.refs_1_, f32[5,128,512]{2,1,0:T(8,128)} %fusion.18.refs_2_, f32[5,128,512]{2,1,0:T(8,128)} %get-tuple-element.98.refs_3_, ...), custom_call_target="tpu_custom_call" | custom-call | flops 600000000 | tf_op jit(solution)/shard_map/attend_back/pallas_call | solution.py:400
  555.2 3.2 fusion.7
  558.4 1.3 dynamic-slice_bitcast_fusion.3
  559.7 3.3 fusion.8
  563.1 1.3 dynamic-slice_bitcast_fusion.4
  564.4 2.4 collective-permute-start.13
  566.8 3.9 convolution_convert_fusion.3
  570.7 20.2 %leave.1 = (f32[5,2,16,2304]{3,2,1,0:T(8,128)S(1)}, f32[1,2304]{1,0:T(1,128)S(1)}) custom-call(bf16[5,2,4,16,2304]{4,3,2,1,0:T(8,128)(2,1)S(1)} %bitcast.144, bf16[5,2,16,2304]{3,2,1,0:T(8,128)(2,1)S(1)} %bitcast.124, f32[5,2,16,2304]{3,2,1,0:T(8,128)S(1)} %get-tuple-element.101.refs_2_, bf16[1,2304]{1,0:T(2,128)(2,1)S(1)} %copy-done.21), custom_call_target="tpu_custom_call" | custom-call | flops 180000000 | tf_op jit(solution)/shard_map/leave/pallas_call | solution.py:178
  591.5 5.7 convolution_convert_fusion
  597.2 127.3 %weights_scatter.1 = (f32[6,48,512]{2,1,0:T(8,128)}, f32[6,48,1024]{2,1,0:T(8,128)}, f32[4,2304]{1,0:T(4,128)}) custom-call(bf16[8,6,48,512]{3,2,1,0:T(8,128)(2,1)} %bitcast.158, bf16[8,6,48,1024]{3,2,1,0:T(8,128)(2,1)} %bitcast.156, f32[4,2304]{1,0:T(4,128)} %pad_maximum_fusion.refs_2_), custom_call_target="tpu_custom_call" | custom-call | flops 800000000 | tf_op jit(solution)/shard_map/weights_scatter/pallas_call | solution.py:636
  724.6 2.1 slice.28
  726.6 2.2 copy.54
  729.8 1.8 fusion.16
  731.9 1.8 fusion.17
  734.9 1.5 dynamic-slice_reduce_fusion
  736.4 3.1 convert_bitcast_fusion
  739.5 2.8 collective-permute-done.16
  742.5 1.7 maximum_convert_fusion.1
  745.4 1.7 maximum_convert_fusion
  (142 shorter events, 16.4 us)
Async XLA Ops:
  0.6 102.3 %copy-start = (bf16[512,2304]{1,0:T(8,128)(2,1)S(1)}, bf16[512,2304]{1,0:T(8,128)(2,1)}, u32[]{:S(2)}) copy-start(bf16[512,2304]{1,0:T(8,128)(2,1)} %param.20) | copy-start | bytes 7077892
  4.6 23.7 %copy-start.36 = (bf16[2304,512]{1,0:T(8,128)(2,1)S(1)}, bf16[2304,512]{1,0:T(8,128)(2,1)}, u32[]{:S(2)}) copy-start(bf16[2304,512]{1,0:T(8,128)(2,1)} %param.17) | copy-start | bytes 7077892
  6.7 24.4 %copy-start.20 = (bf16[1,2304]{1,0:T(2,128)(2,1)}, bf16[1,2304]{1,0:T(2,128)(2,1)S(1)}, u32[]{:S(2)}) copy-start(bf16[1,2304]{1,0:T(2,128)(2,1)S(1)} %reshape.269.refs_1_.refs_3_) | copy-start | bytes 13828
  28.3 4.6 copy-start.11
  28.3 2.8 copy-start.40
  31.1 1.8 copy-start.38
  32.8 2.5 copy-start.33
  32.8 2.5 copy-start.34
  107.3 1.8 copy-start.10
  146.5 15.3 %copy-start.3 = (f32[5,2,16,2304]{3,2,1,0:T(8,128)}, f32[5,2,16,2304]{3,2,1,0:T(8,128)S(1)}, u32[]{:S(2)}) copy-start(f32[5,2,16,2304]{3,2,1,0:T(8,128)S(1)} %get-tuple-element.70.refs_1_) | copy-start | bytes 4423684
  146.5 15.3 %copy-start.14 = (f32[5,2,16,2304]{3,2,1,0:T(8,128)}, f32[5,2,16,2304]{3,2,1,0:T(8,128)S(1)}, u32[]{:S(2)}) copy-start(f32[5,2,16,2304]{3,2,1,0:T(8,128)S(1)} %get-tuple-element.95.refs_2_) | copy-start | bytes 4423684
  146.5 15.3 %copy-start.17 = (bf16[5,2,4,16,2304]{4,3,2,1,0:T(8,128)(2,1)}, bf16[5,2,4,16,2304]{4,3,2,1,0:T(8,128)(2,1)S(1)}, u32[]{:S(2)}) copy-start(bf16[5,2,4,16,2304]{4,3,2,1,0:T(8,128)(2,1)S(1)} %get-tuple-element.66) | copy-start | bytes 8847364
  147.9 13.9 %slice-start.2 = ((s8[10616832]{0:T(1024)(128)(4,1)}), s8[4194304]{0:T(1024)(128)(4,1)S(1)}, s32[]{:S(2)}) async-start(s8[10616832]{0:T(1024)(128)(4,1)} %bitcast.166), calls=%async_computation.2 | async-start | bytes 8388608
  147.9 13.9 %slice-start.3 = ((s8[10616832]{0:T(1024)(128)(4,1)}), s8[4194304]{0:T(1024)(128)(4,1)S(1)}, s32[]{:S(2)}) async-start(s8[10616832]{0:T(1024)(128)(4,1)} %bitcast.166), calls=%async_computation.3 | async-start | bytes 8388608
  147.9 13.9 %slice-start.4 = ((s8[10616832]{0:T(1024)(128)(4,1)}), s8[2228224]{0:T(1024)(128)(4,1)S(1)}, s32[]{:S(2)}) async-start(s8[10616832]{0:T(1024)(128)(4,1)} %bitcast.166), calls=%async_computation.4 | async-start | bytes 4456448
  147.9 41.8 %collective-permute-start = (bf16[320,2304]{1,0:T(8,128)(2,1)}, bf16[320,2304]{1,0:T(8,128)(2,1)}, u32[]{:S(2)}, u32[]{:S(2)}) collective-permute-start(bf16[320,2304]{1,0:T(8,128)(2,1)} %bitcast.12), channel_id=1, source_target_pairs={{0,8},{4,12},{8,0},{12,4},{16,24},{20,28},{24,16},{28,20},{1,9},{5... | collective-permute-start | bytes 4423688 | tf_op jit(solution)/shard_map/ppermute | solution.py:434
  147.9 41.8 %collective-permute-start.1 = (bf16[320,2304]{1,0:T(8,128)(2,1)}, bf16[320,2304]{1,0:T(8,128)(2,1)}, u32[]{:S(2)}, u32[]{:S(2)}) collective-permute-start(bf16[320,2304]{1,0:T(8,128)(2,1)} %bitcast.12), channel_id=1, source_target_pairs={{0,4},{4,0},{8,12},{12,8},{16,20},{20,16},{24,28},{28,24},{1,5},{5... | collective-permute-start | bytes 4423688 | tf_op jit(solution)/shard_map/ppermute | solution.py:434
  161.8 16.0 %copy-start.35 = (bf16[2304]{0:T(1024)(128)(2,1)S(1)}, bf16[2304]{0:T(1024)(128)(2,1)}, u32[]{:S(2)}) copy-start(bf16[2304]{0:T(1024)(128)(2,1)} %param.26) | copy-start | bytes 13828
  173.5 193.8 %collective-permute-start.7 = (bf16[5,2,2,2,16,2304]{5,4,3,2,1,0:T(8,128)(2,1)}, bf16[5,2,2,2,16,2304]{5,4,3,2,1,0:T(8,128)(2,1)}, u32[]{:S(2)}, u32[]{:S(2)}) collective-permute-start(bf16[5,2,2,2,16,2304]{5,4,3,2,1,0:T(8,128)(2,1)} %bitcast.23.mine), channel_id=1, source_target_pairs={{0,16},{4,20},{8,24},{12,28},{16,0},{20,4},{24,8},{28,12},{1,17},{... | collective-permute-start | bytes 8847368 | tf_op jit(solution)/shard_map/ppermute | solution.py:434
  177.8 11.9 %copy-start.1 = (bf16[16,5,2,2304]{3,0,2,1:T(8,128)(2,1)S(1)}, bf16[16,5,2,2304]{3,0,2,1:T(8,128)(2,1)}, u32[]{:S(2)}) copy-start(bf16[16,5,2,2304]{3,0,2,1:T(8,128)(2,1)} %copy.59) | copy-start | bytes 2211844
  177.8 11.9 %copy-start.4 = (f32[5,2,16,2304]{3,2,1,0:T(8,128)S(1)}, f32[5,2,16,2304]{3,2,1,0:T(8,128)}, u32[]{:S(2)}) copy-start(f32[5,2,16,2304]{3,2,1,0:T(8,128)} %copy-done.3) | copy-start | bytes 4423684
  227.3 1.5 copy-start.19
  246.7 5.0 copy-start.28
  246.8 5.0 copy-start.29
  264.1 35.2 %copy-start.18 = (bf16[5,2,4,16,2304]{4,3,2,1,0:T(8,128)(2,1)S(1)}, bf16[5,2,4,16,2304]{4,3,2,1,0:T(8,128)(2,1)}, u32[]{:S(2)}) copy-start(bf16[5,2,4,16,2304]{4,3,2,1,0:T(8,128)(2,1)} %copy-done.17) | copy-start | bytes 8847364
  264.1 34.6 %collective-permute-start.2 = (bf16[5,2,2,2,16,1152]{5,4,3,2,1,0:T(8,128)(2,1)}, bf16[5,2,2,2,16,1152]{5,4,3,2,1,0:T(8,128)(2,1)}, u32[]{:S(2)}, u32[]{:S(2)}) collective-permute-start(bf16[5,2,2,2,16,1152]{5,4,3,2,1,0:T(8,128)(2,1)} %bitcast.19), channel_id=1, source_target_pairs={{0,4},{4,0},{8,12},{12,8},{16,20},{20,16},{24,28},{28,24},{1,5},{5... | collective-permute-start | bytes 4423688 | tf_op jit(solution)/shard_map/ppermute | solution.py:434
  265.0 34.3 %collective-permute-start.3 = (bf16[320,2304]{1,0:T(8,128)(2,1)}, bf16[320,2304]{1,0:T(8,128)(2,1)}, u32[]{:S(2)}, u32[]{:S(2)}) collective-permute-start(bf16[320,2304]{1,0:T(8,128)(2,1)} %collective-permute-done.far), channel_id=1, source_target_pairs={{0,1},{1,0},{2,3},{3,2},{4,5},{5,4},{6,7},{7,6},{8,9},{9,8},{10,11... | collective-permute-start | bytes 4423688 | tf_op jit(solution)/shard_map/ppermute | solution.py:438
  265.0 34.3 %collective-permute-start.4 = (bf16[320,2304]{1,0:T(8,128)(2,1)}, bf16[320,2304]{1,0:T(8,128)(2,1)}, u32[]{:S(2)}, u32[]{:S(2)}) collective-permute-start(bf16[320,2304]{1,0:T(8,128)(2,1)} %collective-permute-done.1.far), channel_id=1, source_target_pairs={{0,1},{1,0},{2,3},{3,2},{4,5},{5,4},{6,7},{7,6},{8,9},{9,8},{10,11... | collective-permute-start | bytes 4423688 | tf_op jit(solution)/shard_map/ppermute | solution.py:438
  265.5 85.5 %collective-permute-start.5 = (bf16[5,2,2,2,16,1152]{5,4,3,2,1,0:T(8,128)(2,1)}, bf16[5,2,2,2,16,1152]{5,4,3,2,1,0:T(8,128)(2,1)}, u32[]{:S(2)}, u32[]{:S(2)}) collective-permute-start(bf16[5,2,2,2,16,1152]{5,4,3,2,1,0:T(8,128)(2,1)} %bitcast.20), channel_id=1, source_target_pairs={{0,8},{4,12},{8,0},{12,4},{16,24},{20,28},{24,16},{28,20},{1,9},{5... | collective-permute-start | bytes 4423688 | tf_op jit(solution)/shard_map/ppermute | solution.py:434
  298.7 68.7 %collective-permute-start.6 = (bf16[320,1152]{1,0:T(8,128)(2,1)}, bf16[320,1152]{1,0:T(8,128)(2,1)}, u32[]{:S(2)}, u32[]{:S(2)}) collective-permute-start(bf16[320,1152]{1,0:T(8,128)(2,1)} %bitcast.163), channel_id=1, source_target_pairs={{0,16},{4,20},{8,24},{12,28},{16,0},{20,4},{24,8},{28,12},{1,17},{... | collective-permute-start | bytes 2211848 | tf_op jit(solution)/shard_map/ppermute | solution.py:434
  313.3 2.4 copy-start.8
  365.0 2.4 copy-start.6
  367.4 6.9 collective-permute-start.8
  367.4 3.9 copy-start.7
  371.0 3.3 copy-start.16
  371.0 74.0 %collective-permute-start.9 = (bf16[2,2,288,1152]{3,2,1,0:T(8,128)(2,1)}, bf16[2,2,288,1152]{3,2,1,0:T(8,128)(2,1)}, u32[]{:S(2)}, u32[]{:S(2)}) collective-permute-start(bf16[2,2,288,1152]{3,2,1,0:T(8,128)(2,1)} %dynamic-slice_bitcast_fusion.2), channel_id=1, source_target_pairs={{0,8},{4,12},{8,0},{12,4},{16,24},{20,28},{24,16},{28,20},{1,9},{5... | collective-permute-start | bytes 7962632 | tf_op jit(solution)/shard_map/ppermute | solution.py:434
  373.0 182.2 %collective-permute-start.11 = (bf16[2,2,288,1152]{3,2,1,0:T(8,128)(2,1)}, bf16[2,2,288,1152]{3,2,1,0:T(8,128)(2,1)}, u32[]{:S(2)}, u32[]{:S(2)}) collective-permute-start(bf16[2,2,288,1152]{3,2,1,0:T(8,128)(2,1)} %dynamic-slice_bitcast_fusion), channel_id=1, source_target_pairs={{0,4},{4,0},{8,12},{12,8},{16,20},{20,16},{24,28},{28,24},{1,5},{5... | collective-permute-start | bytes 7962632 | tf_op jit(solution)/shard_map/ppermute | solution.py:434
  388.0 2.3 copy-start.9
  392.0 163.2 %collective-permute-start.10 = (bf16[2,288,2304]{2,1,0:T(8,128)(2,1)}, bf16[2,288,2304]{2,1,0:T(8,128)(2,1)}, u32[]{:S(2)}, u32[]{:S(2)}) collective-permute-start(bf16[2,288,2304]{2,1,0:T(8,128)(2,1)} %dynamic-slice_bitcast_fusion.1), channel_id=1, source_target_pairs={{0,4},{4,0},{8,12},{12,8},{16,20},{20,16},{24,28},{28,24},{1,5},{5... | collective-permute-start | bytes 7962632 | tf_op jit(solution)/shard_map/ppermute | solution.py:434
  396.4 1.4 copy-start.5
  397.7 1.8 copy-start.13
  399.6 1.4 copy-start.15
  400.9 37.8 %copy-start.42 = (bf16[5,128,512]{2,1,0:T(8,128)(2,1)S(1)}, bf16[5,128,512]{2,1,0:T(8,128)(2,1)}, u32[]{:S(2)}) copy-start(bf16[5,128,512]{2,1,0:T(8,128)(2,1)} %get-tuple-element.65) | copy-start | bytes 1966084
  438.7 6.3 slice-start
  442.3 2.8 slice-start.1
  447.5 1.5 copy-start.22
  449.1 280.6 %collective-permute-start.12 = (bf16[2,288,1152]{2,1,0:T(8,128)(2,1)S(1)}, bf16[2,288,1152]{2,1,0:T(8,128)(2,1)}, u32[]{:S(2)}, u32[]{:S(2)}) collective-permute-start(bf16[2,288,1152]{2,1,0:T(8,128)(2,1)S(1)} %dynamic-slice_bitcast_fusion.5), channel_id=1, source_target_pairs={{0,16},{4,20},{8,24},{12,28},{16,0},{20,4},{24,8},{28,12},{1,17},{... | collective-permute-start | bytes 3981320 | tf_op jit(solution)/shard_map/ppermute | solution.py:434
  558.4 4.7 copy-start.24
  559.6 7.2 copy-start.30
  559.6 7.2 copy-start.37
  559.6 7.2 copy-start.39
  559.6 7.2 copy-start.41
  559.6 170.1 %collective-permute-start.14 = (bf16[288,2304]{1,0:T(8,128)(2,1)}, bf16[288,2304]{1,0:T(8,128)(2,1)}, u32[]{:S(2)}, u32[]{:S(2)}) collective-permute-start(bf16[288,2304]{1,0:T(8,128)(2,1)} %dynamic-slice_bitcast_fusion.3), channel_id=1, source_target_pairs={{0,8},{4,12},{8,0},{12,4},{16,24},{20,28},{24,16},{28,20},{1,9},{5... | collective-permute-start | bytes 3981320 | tf_op jit(solution)/shard_map/ppermute | solution.py:434
  563.1 3.7 copy-start.26
  564.4 165.4 %collective-permute-start.13 = (bf16[2,288,1152]{2,1,0:T(8,128)(2,1)}, bf16[2,288,1152]{2,1,0:T(8,128)(2,1)}, u32[]{:S(2)}, u32[]{:S(2)}) collective-permute-start(bf16[2,288,1152]{2,1,0:T(8,128)(2,1)} %dynamic-slice_bitcast_fusion.4), channel_id=1, source_target_pairs={{0,16},{4,20},{8,24},{12,28},{16,0},{20,4},{24,8},{28,12},{1,17},{... | collective-permute-start | bytes 3981320 | tf_op jit(solution)/shard_map/ppermute | solution.py:434
  566.8 3.9 copy-start.21
  570.7 20.8 %copy-start.12 = (bf16[5,2,4,16,2304]{4,3,2,1,0:T(8,128)(2,1)S(1)}, bf16[5,2,4,16,2304]{4,3,2,1,0:T(8,128)(2,1)}, u32[]{:S(2)}) copy-start(bf16[5,2,4,16,2304]{4,3,2,1,0:T(8,128)(2,1)} %copy-done.11) | copy-start | bytes 8847364
  724.5 4.3 copy-start.31
  724.6 5.2 copy-start.27
  729.7 2.1 copy-start.23
  731.6 4.8 copy-start.25
  731.7 10.7 %collective-permute-start.16 = (bf16[288,1152]{1,0:T(8,128)(2,1)S(1)}, bf16[288,1152]{1,0:T(8,128)(2,1)S(1)}, u32[]{:S(2)}, u32[]{:S(2)}) collective-permute-start(bf16[288,1152]{1,0:T(8,128)(2,1)S(1)} %dynamic-slice_bitcast_fusion.6), channel_id=1, source_target_pairs={{0,8},{4,12},{8,0},{12,4},{16,24},{20,28},{24,16},{28,20},{1,9},{5... | collective-permute-start | bytes 1990664 | tf_op jit(solution)/shard_map/ppermute | solution.py:434
  733.7 11.5 %collective-permute-start.15 = (bf16[288,1152]{1,0:T(8,128)(2,1)S(1)}, bf16[288,1152]{1,0:T(8,128)(2,1)S(1)}, u32[]{:S(2)}, u32[]{:S(2)}) collective-permute-start(bf16[288,1152]{1,0:T(8,128)(2,1)S(1)} %dynamic-slice_bitcast_fusion.7), channel_id=1, source_target_pairs={{0,4},{4,0},{8,12},{12,8},{16,20},{20,16},{24,28},{28,24},{1,5},{5... | collective-permute-start | bytes 1990664 | tf_op jit(solution)/shard_map/ppermute | solution.py:434
  744.2 2.9 copy-start.32
  (1 other events, 1.1 us)

commit v5 on v4

--- a/solution.py
+++ b/solution.py
@@ -12,6 +12,8 @@
 CAP = 50.0
 BASE = 10000.0
 MIB = 1 << 20
+TILE = 768
+BACK_TILE = 384
 F32 = jnp.float32
 BF16 = jnp.bfloat16
 VMEM = pltpu.VMEM
@@ -525,9 +527,7 @@
         ],
         out_specs=pl.BlockSpec((tile, cols), lambda i: (i, 0)),
         compiler_params=pltpu.CompilerParams(vmem_limit_bytes=40 * MIB),
-        cost_estimate=pl.CostEstimate(
-            flops=4 * rows * width * cols, bytes_accessed=0, transcendentals=0
-        ),
+        cost_estimate=takes(1),
         name=name,
     )(own, far, near, mine, got)
 
@@ -584,10 +584,12 @@
         for sub in subs(order, 0):
             copy(n, 0, sub).start()
 
+    hops = tp_steps + steps
     gains_send[0] = gains[...]
-    for step in range(tp_steps + steps):
+
+    def hop(step):
         axis, bit, at = ("tp", step, me_tp) if step < tp_steps else ("ctx", step - tp_steps, me)
-        go = remote(
+        return remote(
             axis,
             gains_send.at[step],
             gains_landed.at[step],
@@ -595,27 +597,41 @@
             step,
             flipped(at, 1 << bit),
         )
-        go.start()
-        go.wait_recv()
+
+    def end_hop(step):
+        hop(step).wait_recv()
         both = gains_send[step] + gains_landed[step]
-        if step + 1 < tp_steps + steps:
+        if step + 1 < hops:
             gains_send[step + 1] = both
+            hop(step + 1).start()
         else:
             gains_out[...] = both
-        go.wait_send()
-
-    for n, got in scatter_events([order for _, _, order in plan]):
+
+    hop(0).start()
+    for step in range(tp_steps):
+        end_hop(step)
+    orders = [order for _, _, order in plan]
+    events = scatter_events(orders)
+    first_done = max(k for k, (n, step) in enumerate(events) if step == 0)
+
+    for k, (n, got) in enumerate(events):
         p, item, order = plan[n]
         for sub in subs(order, got):
             copy(n, got, sub).wait_recv()
         step = got + 1
         if step == steps:
             outs[p][item] = total_of(n, 0, steps)
-            continue
-        for sub in subs(order, step):
-            mask = 1 << order[step] | sub
-            sendbuf[p][without(mask, order[0]), item] = total_of(n, mask, step).astype(BF16)
-            copy(n, step, sub).start()
+        else:
+            for sub in subs(order, step):
+                mask = 1 << order[step] | sub
+                sendbuf[p][without(mask, order[0]), item] = total_of(n, mask, step).astype(BF16)
+                copy(n, step, sub).start()
+        if k == first_done:
+            end_hop(tp_steps)
+    for step in range(tp_steps + 1, hops):
+        end_hop(step)
+    for step in range(hops):
+        hop(step).wait_send()
     for step in range(steps):
         for n, (_, _, order) in enumerate(plan):
             for sub in subs(order, step):
@@ -713,8 +729,174 @@
     tokens_grad[item] = resid_grad[item] + dv
 
 
-def gelu_times(gate, up_val):
-    return jax.nn.gelu(gate, approximate=True) * up_val
+GELU_A, GELU_B = 0.7978845608028654, 0.044715
+
+
+def ffw_kernel(rows, gate_w, up_w, down_w, gate_out, up_out, mixed_out, part, total):
+    step = pl.program_id(0)
+    value = rows[...]
+    gate = jnp.dot(value, gate_w[...], preferred_element_type=F32)
+    up = jnp.dot(value, up_w[...], preferred_element_type=F32)
+    tanh = jnp.tanh(GELU_A * (gate + GELU_B * (gate * gate * gate)))
+    mixed = (0.5 * gate * (1.0 + tanh) * up).astype(BF16)
+    gate_out[...], up_out[...], mixed_out[...] = gate, up, mixed
+    term = jnp.dot(mixed, down_w[...], preferred_element_type=F32)
+
+    @pl.when(step == 0)
+    def _():
+        total[...] = term
+
+    @pl.when(step > 0)
+    def _():
+        total[...] += term
+
+    @pl.when(step == pl.num_programs(0) - 1)
+    def _():
+        part[...] = total[...].astype(BF16)
+
+
+def hidden_grad_kernel(bits, grad, gate, up, down_w, gate_give, up_give, gate_keep, up_keep):
+    first, alike = pl.program_id(0) < pl.num_programs(0) // 2, bits[1] == 1
+    mixed_grad = lax.dot_general(
+        grad[...], down_w[...], (((1,), (1,)), ((), ())), preferred_element_type=F32
+    )
+    v = gate[...]
+    square = v * v
+    tanh = jnp.tanh(GELU_A * (v + GELU_B * (square * v)))
+    half = 0.5 * (1.0 + tanh)
+    slope = half + 0.5 * v * (1.0 - tanh * tanh) * (GELU_A * (1.0 + 3.0 * GELU_B * square))
+    gate_g = (mixed_grad * up[...] * slope).astype(BF16)
+    up_g = (mixed_grad * (half * v)).astype(BF16)
+
+    @pl.when(first)
+    def _():
+        gate_give[...] = gate_g
+
+    @pl.when(jnp.logical_not(first))
+    def _():
+        gate_keep[...] = gate_g
+
+    @pl.when(first == alike)
+    def _():
+        up_give[...] = up_g
+
+    @pl.when(first != alike)
+    def _():
+        up_keep[...] = up_g
+
+
+def hidden_specs(rows, width, half_steps, tile):
+    def at(i, bits):
+        which = jnp.where(i < half_steps, 1 - bits[0], bits[0])
+        return which * half_steps + jnp.where(i < half_steps, i, i - half_steps)
+
+    def early(i):
+        return jnp.minimum(i, half_steps - 1)
+
+    def late(i):
+        return jnp.maximum(i - half_steps, 0)
+
+    def block(shape, index):
+        return pl.BlockSpec(shape, index)
+
+    return dict(
+        cols=block((rows, tile), lambda i, bits: (0, at(i, bits))),
+        tall=block((width, tile), lambda i, bits: (0, at(i, bits))),
+        flat=block((tile, width), lambda i, bits: (at(i, bits), 0)),
+        held=block((rows, width), lambda i, bits: (0, 0)),
+        gate_give=block((rows, tile), lambda i, bits: (0, early(i))),
+        gate_keep=block((rows, tile), lambda i, bits: (0, late(i))),
+        up_give=block((rows, tile), lambda i, bits: (0, jnp.where(bits[1] == 1, early(i), late(i)))),
+        up_keep=block((rows, tile), lambda i, bits: (0, jnp.where(bits[1] == 1, late(i), early(i)))),
+    )
+
+
+HALVES = ("gate_give", "up_give", "gate_keep", "up_keep")
+
+
+def hidden_grads(bits, grad, gate, up, down_w):
+    rows, width = grad.shape
+    hidden = gate.shape[1]
+    half_steps, tile = hidden // 2 // BACK_TILE, BACK_TILE
+    spec = hidden_specs(rows, width, half_steps, tile)
+    return pl.pallas_call(
+        hidden_grad_kernel,
+        grid_spec=pltpu.PrefetchScalarGridSpec(
+            num_scalar_prefetch=1,
+            grid=(2 * half_steps,),
+            in_specs=[spec["held"], spec["cols"], spec["cols"], spec["flat"]],
+            out_specs=[spec[name] for name in HALVES],
+        ),
+        out_shape=[jax.ShapeDtypeStruct((rows, hidden // 2), BF16)] * 4,
+        compiler_params=pltpu.CompilerParams(vmem_limit_bytes=48 * MIB),
+        cost_estimate=takes(1),
+        name="hidden_grads",
+    )(bits, grad, gate, up, down_w)
+
+
+def input_grad_kernel(bits, gate_give, up_give, gate_keep, up_keep, gate_w, up_w, part, total):
+    step = pl.program_id(0)
+    first, alike = step < pl.num_programs(0) // 2, bits[1] == 1
+    across = (((1,), (1,)), ((), ()))
+    gate_g = jnp.where(first, gate_give[...], gate_keep[...])
+    up_g = jnp.where(first == alike, up_give[...], up_keep[...])
+    term = lax.dot_general(gate_g, gate_w[...], across, preferred_element_type=F32)
+    term = term + lax.dot_general(up_g, up_w[...], across, preferred_element_type=F32)
+
+    @pl.when(step == 0)
+    def _():
+        total[...] = term
+
+    @pl.when(step > 0)
+    def _():
+        total[...] += term
+
+    @pl.when(step == pl.num_programs(0) - 1)
+    def _():
+        part[...] = total[...].astype(BF16)
+
+
+def input_grad(bits, halves, gate_w, up_w):
+    rows = halves[0].shape[0]
+    width, hidden = gate_w.shape
+    half_steps, tile = hidden // 2 // BACK_TILE, BACK_TILE
+    spec = hidden_specs(rows, width, half_steps, tile)
+    return pl.pallas_call(
+        input_grad_kernel,
+        grid_spec=pltpu.PrefetchScalarGridSpec(
+            num_scalar_prefetch=1,
+            grid=(2 * half_steps,),
+            in_specs=[spec[name] for name in HALVES] + [spec["tall"]] * 2,
+            out_specs=spec["held"],
+            scratch_shapes=[VMEM((rows, width), F32)],
+        ),
+        out_shape=jax.ShapeDtypeStruct((rows, width), BF16),
+        compiler_params=pltpu.CompilerParams(vmem_limit_bytes=48 * MIB),
+        cost_estimate=takes(1),
+        name="input_grad",
+    )(bits, *halves, gate_w, up_w)
+
+
+def ffw_call(kernel, name, ins, weights, outs):
+    rows, width = ins[0].shape
+    hidden = weights[0].shape[1]
+    tile = TILE
+    cols = pl.BlockSpec((rows, tile), lambda i: (0, i))
+    tall = pl.BlockSpec((width, tile), lambda i: (0, i))
+    flat = pl.BlockSpec((tile, width), lambda i: (i, 0))
+    held = pl.BlockSpec((rows, width), lambda i: (0, 0))
+    return pl.pallas_call(
+        kernel,
+        grid=(hidden // tile,),
+        out_shape=[jax.ShapeDtypeStruct((rows, hidden), t) for t in outs]
+        + [jax.ShapeDtypeStruct((rows, width), BF16)],
+        in_specs=[held] + [cols] * (len(ins) - 1) + [tall, tall, flat],
+        out_specs=[cols] * len(outs) + [held],
+        scratch_shapes=[VMEM((rows, width), F32)],
+        compiler_params=pltpu.CompilerParams(vmem_limit_bytes=56 * MIB),
+        cost_estimate=takes(1),
+        name=name,
+    )(*ins, *weights)
 
 
 def body(
@@ -810,13 +992,6 @@
     def core_rows(value):
         return pick(by_core(value), core, 3).reshape(all_rows // 2, value.shape[-1])
 
-    def halves(value, b):
-        bit = (ctx_rank >> b) & 1
-        cut = value.shape[1] // 2
-        return [
-            by_core(lax.dynamic_slice_in_dim(value, at * cut, cut, 1)) for at in (bit, 1 - bit)
-        ]
-
     def owner_cols(value):
         bit = (ctx_rank >> far_bit) & 1
         cut = value.shape[1] // 2
@@ -836,12 +1011,9 @@
     ffw_send = core_rows(ffw_all)
     ffw_all, ffw_send = lax.optimization_barrier((ffw_all, ffw_send))
     ffw_far, ffw_far_low = Sent(ffw_send, next_bit), Sent(ffw_send, low_bit)
-    gate = dot(ffw_all, gate_weight)
-    up = dot(ffw_all, up_weight)
-    mixed, mixed_back = jax.vjp(gelu_times, gate, up)
-    mixed = mixed.astype(BF16)
+    ffw_weights = (gate_weight, up_weight, down_weight)
+    gate, up, mixed, part = ffw_call(ffw_kernel, "ffw", [ffw_all], ffw_weights, [F32, F32, BF16])
     mixed_sent = Sent(by_core(mixed), far_bit)
-    part = dot(mixed, down_weight).astype(BF16)
     part = pin(part, ffw_far, ffw_far_low)
     ffw_near, ffw_near_low = CoreSent(ffw_far.gots[0]), CoreSent(ffw_far_low.gots[0])
     ffw_grad_all, layer_out, ffw_out_gain_part = tp_exchange(
@@ -852,25 +1024,18 @@
         [jax.ShapeDtypeStruct(own, BF16), gain_shape],
         by_owner(part),
     )
-    ffw_grad_all = ffw_grad_all.reshape(all_rows, width)
+    ffw_grad_all = pin(ffw_grad_all.reshape(all_rows, width), ffw_near, ffw_near_low)
     grad_half, grad_give = owner_cols(ffw_grad_all)
     grad_send = core_rows(grad_give)
     ffw_grad_all, grad_send = lax.optimization_barrier((ffw_grad_all, grad_send))
     grad_far = Sent(grad_send, far_bit)
-    mixed_grad = ein("rd,fd->rf", ffw_grad_all, down_weight)
-    gate_grad, up_grad = mixed_back(mixed_grad)
-    gate_grad = gate_grad.astype(BF16)
-    up_grad = up_grad.astype(BF16)
-    gate_half, gate_give = halves(gate_grad, low_bit)
-    up_half, up_give = halves(up_grad, next_bit)
-    gate_grad, up_grad, gate_give, up_give = lax.optimization_barrier(
-        (gate_grad, up_grad, gate_give, up_give)
-    )
+    gate_bit, up_bit = (ctx_rank >> low_bit) & 1, (ctx_rank >> next_bit) & 1
+    bits = jnp.stack([gate_bit, (gate_bit == up_bit).astype(jnp.int32)])
+    hidden = hidden_grads(bits, ffw_grad_all, gate, up, down_weight)
+    gate_give, up_give, gate_half, up_half = [by_core(h) for h in hidden]
     gate_sent, up_sent = Sent(gate_give, low_bit), Sent(up_give, next_bit)
-    part = (
-        ein("rf,df->rd", gate_grad, gate_weight) + ein("rf,df->rd", up_grad, up_weight)
-    ).astype(BF16)
-    part = pin(part, gate_sent, ffw_near, ffw_near_low)
+    part = input_grad(bits, hidden, gate_weight, up_weight)
+    part = pin(part, gate_sent)
     gate_part = product(
         ffw_all, ffw_far_low.gots[0], ffw_near_low.gots[0], gate_half, gate_sent.gots[0], "gate_product"
     )

time: 752 us -> 743 us (0.988)
  matrix products: 107 us -> 26.5 us
  Pallas kernels: 492 us -> 551 us
  waiting for transfers between devices: 57.5 us -> 67.9 us
    pallas_call x0 -> x3, Pallas kernels: none -> 80.2 us  [the longest x1 32.8 us: ffw_call(): pl.pallas_call(kernel, grid=(hidden // tile,), out_shape=[jax.ShapeDtypeS...]
    dot_general x6 -> x0, matrix products: 80 us -> none  [the longest x1 17 us: body(): mixed_grad = ein('rd,fd->rf', ffw_grad_all, down_weight)]
    pallas_call x1, Pallas kernels: 127 us -> 107 us  [weights_scatter(): pl.pallas_call(functools.partial(weights_scatter_kernel, count, tp_count,...]
    ppermute x14, waiting for transfers between devices: 57.5 us -> 67.8 us  [send_ctx(): lax.ppermute(value, 'ctx', [(i, i ^ mask) for i in range(lax.axis_size('c...]
    unnamed x101 -> x109, local copies, waits for them, and re-layouts: 25.7 us -> 30.1 us
  transfers between devices with their start and end apart: 17 -> 17, of which waited for: 4 -> 5; matrix products, arithmetic and copies ran while one was open for 19% -> 7% of each run, Pallas kernels for 49% -> 58%
where the time goes in v5:
time: 743 us; the launch traced here: 734 us
  Pallas kernels  551 us (74%)
  waiting for transfers between devices  67.9 us (9%)
  local copies, waits for them, and re-layouts  52.8 us (7%)
  matrix products  26.5 us (4%)
  other arithmetic  21 us (3%)
  starting transfers between devices  14 us (2%)
    pallas_call x5, Pallas kernels, tp_exchange(): pl.pallas_call(functools.partial(tp_kernel, fn, count, items, len(ins), l...  154 us
    pallas_call x1, Pallas kernels, weights_scatter(): pl.pallas_call(functools.partial(weights_scatter_kernel, count, tp_count,...  107 us
    pallas_call x1, Pallas kernels, attend_back_some(): pl.pallas_call(functools.partial(attend_back_kernel, count, seqs, heads),...  103 us
    ppermute x14, waiting for transfers between devices, send_ctx(): lax.ppermute(value, 'ctx', [(i, i ^ mask) for i in range(lax.axis_size('c...  67.8 us
    pallas_call x1, Pallas kernels, attend_all(): pl.pallas_call(functools.partial(attend_kernel, count, seqs, heads), out_...  65.2 us
    pallas_call x3, Pallas kernels, product(): pl.pallas_call(product_kernel, grid=(width // tile,), out_shape=jax.Shape...  40.8 us
    pallas_call x1, Pallas kernels, ffw_call(): pl.pallas_call(kernel, grid=(hidden // tile,), out_shape=[jax.ShapeDtypeS...  32.8 us
    unnamed x109, local copies, waits for them, and re-layouts  30.1 us
  transfers between devices with their start and end apart: 17, of which 5 were waited for; matrix products, arithmetic and copies ran while one was open for 7% of the time, Pallas kernels for 58%

profile of v5, /device:TPU:0, one launch (start us, length us, event | category | flops | bytes accessed | tf_op | source)
XLA Modules:
  0.0 734.5 jit_solution(5258329144711472006)
XLA Ops:
  2.6 1.1 convert_reduce_fusion
  4.6 1.3 copy.60
  6.7 21.6 %enter.1 = bf16[5,2,4,16,2304]{4,3,2,1,0:T(8,128)(2,1)S(1)} custom-call(bf16[5,2,16,2304]{3,2,1,0:T(8,128)(2,1)S(1)} %bitcast.129, bf16[1,2304]{1,0:T(2,128)(2,1)S(1)} %reshape.269.refs_1_.refs_3_), custom_call_target="tpu_custom_call" | custom-call | flops 180000000 | tf_op jit(solution)/shard_map/enter/pallas_call | solution.py:180
  28.3 2.7 fusion.13.q
  31.1 1.8 fusion.15.v
  32.9 1.8 fusion.17.k
  35.4 2.1 multiply_sine_fusion
  37.5 65.2 %attend.1 = (bf16[10,8,128,256]{3,2,1,0:T(8,128)(2,1)}, f32[5,128,512]{2,1,0:T(8,128)}, bf16[5,128,512]{2,1,0:T(8,128)(2,1)}, f32[5,2,128,1]{3,2,1,0:T(8,128)}, bf16[5,128,512]{2,1,0:T(8,128)(2,1)}) custom-call(f32[5,128,512]{2,1,0:T(8,128)} %fusion.13.q, f32[5,128,256]{2,1,0:T(8,128)} %fusion.17.k, f32[5,128,256]{2,1,0:T(8,128)} %fusion.15.v, ...), custom_call_target="tpu_custom_call" | custom-call | flops 600000000 | tf_op jit(solution)/shard_map/attend/pallas_call | solution.py:289
  102.7 4.3 convolution_convert_fusion.1
  107.0 1.8 copy-done.20
  108.8 37.3 %middle.1 = (bf16[5,2,4,16,2304]{4,3,2,1,0:T(8,128)(2,1)S(1)}, f32[5,2,16,2304]{3,2,1,0:T(8,128)S(1)}, f32[5,2,16,2304]{3,2,1,0:T(8,128)S(1)}) custom-call(bf16[5,2,4,16,2304]{4,3,2,1,0:T(8,128)(2,1)S(1)} %bitcast.138, bf16[5,2,16,2304]{3,2,1,0:T(8,128)(2,1)S(1)} %bitcast.130, bf16[1,2304]{1,0:T(2,128)(2,1)S(1)} %reshape.272.refs_2_.refs_5_, ...), custom_call_target="tpu_custom_call" | custom-call | flops 360000000 | tf_op jit(solution)/shard_map/middle/pallas_call | solution.py:180
  147.3 1.4 constant_dynamic-slice_fusion.4
  149.6 32.8 %ffw.1 = (f32[640,2304]{1,0:T(8,128)}, f32[640,2304]{1,0:T(8,128)}, bf16[640,2304]{1,0:T(8,128)(2,1)}, bf16[640,2304]{1,0:T(8,128)(2,1)}) custom-call(bf16[640,2304]{1,0:T(8,128)(2,1)} %bitcast.113, bf16[2304,2304]{1,0:T(8,128)(2,1)} %gate_w.3, bf16[2304,2304]{1,0:T(8,128)(2,1)} %up_w.3, bf16[2304,2304]{1,0:T(8,128)(2,1)} %down_w.3), custom_call_target="tpu_custom_call" | custom-call | flops 10000000 | tf_op jit(solution)/shard_map/ffw/pallas_call | solution.py:888
  182.3 1.2 collective-permute-done.far
  184.0 2.6 collective-permute-start.7
  186.7 1.2 copy.59
  187.9 1.4 copy-done.12
  189.3 1.8 copy-done.23
  191.1 37.6 %turn.1 = (bf16[5,2,4,16,2304]{4,3,2,1,0:T(8,128)(2,1)S(1)}, bf16[5,2,16,2304]{3,2,1,0:T(8,128)(2,1)S(1)}, f32[1,2304]{1,0:T(1,128)S(1)}) custom-call(bf16[5,2,4,16,2304]{4,3,2,1,0:T(8,128)(2,1)S(1)} %bitcast.143, f32[5,2,16,2304]{3,2,1,0:T(8,128)S(1)} %copy-done.12, bf16[5,2,16,2304]{3,2,1,0:T(8,128)(2,1)S(1)} %bitcast.132, ...), custom_call_target="tpu_custom_call" | custom-call | flops 360000000 | tf_op jit(solution)/shard_map/turn/pallas_call | solution.py:180
  228.7 1.8 constant_dynamic-slice_fusion.1
  231.9 18.8 %hidden_grads.1 = (bf16[640,1152]{1,0:T(8,128)(2,1)}, bf16[640,1152]{1,0:T(8,128)(2,1)}, bf16[640,1152]{1,0:T(8,128)(2,1)S(1)}, bf16[640,1152]{1,0:T(8,128)(2,1)S(1)}) custom-call(s32[2]{0:T(128)S(1)} %get-tuple-element.183.bits, bf16[640,2304]{1,0:T(8,128)(2,1)} %bitcast.127, f32[640,2304]{1,0:T(8,128)} %get-tuple-element.85.gate, ...), custom_call_target="tpu_custom_call" | custom-call | flops 10000000 | tf_op jit(solution)/shard_map/hidden_grads/pallas_call | solution.py:822
  253.8 1.7 collective-permute-start.6
  255.5 1.4 copy-done.15
  256.8 1.4 copy-done.18
  258.2 28.6 %input_grad.1 = bf16[640,2304]{1,0:T(8,128)(2,1)} custom-call(s32[2]{0:T(128)S(1)} %get-tuple-element.183.bits, bf16[640,1152]{1,0:T(8,128)(2,1)} %get-tuple-element.87.gate_give, bf16[640,1152]{1,0:T(8,128)(2,1)} %get-tuple-element.88.up_give, bf16[640,1152]{1,0:T(8,128)(2,1)S(1)} %copy-done.18, bf16[640,1152]{1,0:T(8,128)(2,1)S(1)} %copy-done.15, ...), custom_call_target="tpu_custom_call" | custom-call | flops 10000000 | tf_op jit(solution)/shard_map/input_grad/pallas_call | solution.py:864
  287.6 14.1 %gate_product.1 = bf16[2304,1152]{1,0:T(8,128)(2,1)S(1)} custom-call(bf16[640,2304]{1,0:T(8,128)(2,1)S(1)} %bitcast.114, bf16[320,2304]{1,0:T(8,128)(2,1)} %collective-permute-done.1.far, bf16[320,2304]{1,0:T(8,128)(2,1)} %collective-permute-done.3.near, bf16[5,2,2,2,16,1152]{5,4,3,2,1,0:T(8,128)(2,1)S(1)} %bitcast.135, ...), custom_call_target="tpu_custom_call" | custom-call | flops 10000000 | tf_op jit(solution)/shard_map/gate_product/pallas_call | solution.py:517
  301.7 60.0 %collective-permute-done.5.got = bf16[5,2,2,2,16,1152]{5,4,3,2,1,0:T(8,128)(2,1)} collective-permute-done((bf16[5,2,2,2,16,1152]{5,4,3,2,1,0:T(8,128)(2,1)}, bf16[5,2,2,2,16,1152]{5,4,3,2,1,0:T(8,128)(2,1)}, u32[]{:S(2)}, u32[]{:S(2)}) %collective-permute-start.5) | collective-permute-done | bytes 1474592 | tf_op jit(solution)/shard_map/ppermute | solution.py:436
  361.7 14.0 %up_product.1 = bf16[2304,1152]{1,0:T(8,128)(2,1)S(1)} custom-call(bf16[640,2304]{1,0:T(8,128)(2,1)S(1)} %bitcast.115, bf16[320,2304]{1,0:T(8,128)(2,1)} %collective-permute-done.far, bf16[320,2304]{1,0:T(8,128)(2,1)} %collective-permute-done.2.near, bf16[5,2,2,2,16,1152]{5,4,3,2,1,0:T(8,128)(2,1)S(1)} %bitcast.134, ...), custom_call_target="tpu_custom_call" | custom-call | flops 10000000 | tf_op jit(solution)/shard_map/up_product/pallas_call | solution.py:517
  375.7 2.0 dynamic-slice_bitcast_fusion.2
  378.8 3.6 dynamic-slice_bitcast_fusion
  382.9 12.8 %down_product.1 = bf16[1152,2304]{1,0:T(8,128)(2,1)S(1)} custom-call(bf16[640,1152]{1,0:T(8,128)(2,1)S(1)} %copy-done.10, bf16[320,1152]{1,0:T(8,128)(2,1)} %collective-permute-done.6.far, bf16[320,1152]{1,0:T(8,128)(2,1)} %collective-permute-done.8.near, bf16[5,2,2,2,16,2304]{5,4,3,2,1,0:T(8,128)(2,1)S(1)} %bitcast.137, ...), custom_call_target="tpu_custom_call" | custom-call | flops 10000000 | tf_op jit(solution)/shard_map/down_product/pallas_call | solution.py:517
  395.7 1.8 dynamic-slice_bitcast_fusion.1
  397.5 1.3 copy-done.5
  398.8 1.5 collective-permute-start.10
  400.3 2.5 copy.53
  402.9 1.8 copy-done.7
  404.7 1.4 copy-done.13
  406.1 1.4 copy-done.25
  407.5 37.6 %middle_back.1 = (bf16[5,2,4,16,2304]{4,3,2,1,0:T(8,128)(2,1)S(1)}, f32[5,2,16,2304]{3,2,1,0:T(8,128)S(1)}, f32[1,2304]{1,0:T(1,128)S(1)}, f32[1,2304]{1,0:T(1,128)S(1)}) custom-call(bf16[5,2,4,16,2304]{4,3,2,1,0:T(8,128)(2,1)S(1)} %bitcast.128, f32[5,2,16,2304]{3,2,1,0:T(8,128)S(1)} %copy-done.13, f32[5,2,16,2304]{3,2,1,0:T(8,128)S(1)} %copy-done.25, ...), custom_call_target="tpu_custom_call" | custom-call | flops 360000000 | tf_op jit(solution)/shard_map/middle_back/pallas_call | solution.py:180
  445.1 3.4 convolution_convert_fusion.3
  448.5 2.8 fusion.11.refs_2_
  451.4 2.4 fusion.2
  453.8 1.5 copy-done.29
  455.3 1.3 dynamic-slice_bitcast_fusion.5
  456.6 2.9 collective-permute-start.12
  459.4 103.0 %attend_back.1 = bf16[5,128,1024]{2,1,0:T(8,128)(2,1)} custom-call(bf16[5,128,512]{2,1,0:T(8,128)(2,1)} %get-tuple-element.78.refs_0_, bf16[10,8,128,256]{3,2,1,0:T(8,128)(2,1)} %get-tuple-element.79.refs_1_, f32[5,128,512]{2,1,0:T(8,128)} %fusion.11.refs_2_, f32[5,128,512]{2,1,0:T(8,128)} %get-tuple-element.108.refs_3_, ...), custom_call_target="tpu_custom_call" | custom-call | flops 600000000 | tf_op jit(solution)/shard_map/attend_back/pallas_call | solution.py:402
  562.4 3.2 fusion
  565.6 1.3 dynamic-slice_bitcast_fusion.3
  567.0 2.5 fusion.1
  569.7 2.6 collective-permute-start.13
  572.3 3.9 convolution_convert_fusion.2
  576.2 20.5 %leave.1 = (f32[5,2,16,2304]{3,2,1,0:T(8,128)S(1)}, f32[1,2304]{1,0:T(1,128)S(1)}) custom-call(bf16[5,2,4,16,2304]{4,3,2,1,0:T(8,128)(2,1)S(1)} %bitcast.144, bf16[5,2,16,2304]{3,2,1,0:T(8,128)(2,1)S(1)} %bitcast.131, f32[5,2,16,2304]{3,2,1,0:T(8,128)S(1)} %copy-done.27, bf16[1,2304]{1,0:T(2,128)(2,1)S(1)} %reshape.269.refs_1_.refs_3_), custom_call_target="tpu_custom_call" | custom-call | flops 180000000 | tf_op jit(solution)/shard_map/leave/pallas_call | solution.py:180
  597.3 5.8 convolution_convert_fusion
  603.1 107.1 %weights_scatter.1 = (f32[6,48,512]{2,1,0:T(8,128)}, f32[6,48,1024]{2,1,0:T(8,128)}, f32[4,2304]{1,0:T(4,128)}) custom-call(bf16[8,6,48,512]{3,2,1,0:T(8,128)(2,1)} %bitcast.151, bf16[8,6,48,1024]{3,2,1,0:T(8,128)(2,1)} %bitcast.149, f32[4,2304]{1,0:T(4,128)} %pad_maximum_fusion.refs_2_), custom_call_target="tpu_custom_call" | custom-call | flops 800000000 | tf_op jit(solution)/shard_map/weights_scatter/pallas_call | solution.py:652
  710.2 2.1 slice.28
  712.3 2.2 copy.54
  715.9 1.2 copy-done.30
  717.2 1.6 fusion.10
  719.1 1.5 dynamic-slice_reduce_fusion
  720.7 3.1 convert_bitcast_fusion
  723.8 4.6 collective-permute-done.16
  728.5 1.7 maximum_convert_fusion.1
  730.2 1.2 collective-permute-done.15
  731.6 1.7 maximum_convert_fusion
  (146 shorter events, 17.5 us)
Async XLA Ops:
  0.6 102.0 %copy-start = (bf16[512,2304]{1,0:T(8,128)(2,1)S(1)}, bf16[512,2304]{1,0:T(8,128)(2,1)}, u32[]{:S(2)}) copy-start(bf16[512,2304]{1,0:T(8,128)(2,1)} %param.20) | copy-start | bytes 7077892
  4.6 23.7 %copy-start.41 = (bf16[2304,512]{1,0:T(8,128)(2,1)S(1)}, bf16[2304,512]{1,0:T(8,128)(2,1)}, u32[]{:S(2)}) copy-start(bf16[2304,512]{1,0:T(8,128)(2,1)} %param.17) | copy-start | bytes 7077892
  6.0 101.0 %copy-start.8 = (bf16[16,5,2,2304]{3,0,2,1:T(8,128)(2,1)}, bf16[16,5,2,2304]{3,0,2,1:T(8,128)(2,1)S(1)}, u32[]{:S(2)}) copy-start(bf16[16,5,2,2304]{3,0,2,1:T(8,128)(2,1)S(1)} %copy.60) | copy-start | bytes 2211844
  28.3 4.5 copy-start.21
  28.3 2.8 copy-start.45
  31.1 1.8 copy-start.43
  32.9 2.5 copy-start.38
  32.9 2.5 copy-start.39
  107.0 1.8 copy-start.20
  147.3 2.3 copy-start.1
  147.3 35.1 %copy-start.11 = (f32[5,2,16,2304]{3,2,1,0:T(8,128)}, f32[5,2,16,2304]{3,2,1,0:T(8,128)S(1)}, u32[]{:S(2)}) copy-start(f32[5,2,16,2304]{3,2,1,0:T(8,128)S(1)} %get-tuple-element.76.refs_1_) | copy-start | bytes 4423684
  148.7 39.2 %copy-start.40 = (bf16[2304]{0:T(1024)(128)(2,1)S(1)}, bf16[2304]{0:T(1024)(128)(2,1)}, u32[]{:S(2)}) copy-start(bf16[2304]{0:T(1024)(128)(2,1)} %param.26) | copy-start | bytes 13828
  148.7 34.9 %collective-permute-start = (bf16[320,2304]{1,0:T(8,128)(2,1)}, bf16[320,2304]{1,0:T(8,128)(2,1)}, u32[]{:S(2)}, u32[]{:S(2)}) collective-permute-start(bf16[320,2304]{1,0:T(8,128)(2,1)} %bitcast.12), channel_id=1, source_target_pairs={{0,8},{4,12},{8,0},{12,4},{16,24},{20,28},{24,16},{28,20},{1,9},{5... | collective-permute-start | bytes 4423688 | tf_op jit(solution)/shard_map/ppermute | solution.py:436
  148.7 34.9 %collective-permute-start.1 = (bf16[320,2304]{1,0:T(8,128)(2,1)}, bf16[320,2304]{1,0:T(8,128)(2,1)}, u32[]{:S(2)}, u32[]{:S(2)}) collective-permute-start(bf16[320,2304]{1,0:T(8,128)(2,1)} %bitcast.12), channel_id=1, source_target_pairs={{0,4},{4,0},{8,12},{12,8},{16,20},{20,16},{24,28},{28,24},{1,5},{5... | collective-permute-start | bytes 4423688 | tf_op jit(solution)/shard_map/ppermute | solution.py:436
  183.5 45.1 %collective-permute-start.2 = (bf16[320,2304]{1,0:T(8,128)(2,1)}, bf16[320,2304]{1,0:T(8,128)(2,1)}, u32[]{:S(2)}, u32[]{:S(2)}) collective-permute-start(bf16[320,2304]{1,0:T(8,128)(2,1)} %collective-permute-done.far), channel_id=1, source_target_pairs={{0,1},{1,0},{2,3},{3,2},{4,5},{5,4},{6,7},{7,6},{8,9},{9,8},{10,11... | collective-permute-start | bytes 4423688 | tf_op jit(solution)/shard_map/ppermute | solution.py:440
  183.5 45.2 %collective-permute-start.3 = (bf16[320,2304]{1,0:T(8,128)(2,1)}, bf16[320,2304]{1,0:T(8,128)(2,1)}, u32[]{:S(2)}, u32[]{:S(2)}) collective-permute-start(bf16[320,2304]{1,0:T(8,128)(2,1)} %collective-permute-done.1.far), channel_id=1, source_target_pairs={{0,1},{1,0},{2,3},{3,2},{4,5},{5,4},{6,7},{7,6},{8,9},{9,8},{10,11... | collective-permute-start | bytes 4423688 | tf_op jit(solution)/shard_map/ppermute | solution.py:440
  184.0 191.6 %collective-permute-start.7 = (bf16[5,2,2,2,16,2304]{5,4,3,2,1,0:T(8,128)(2,1)}, bf16[5,2,2,2,16,2304]{5,4,3,2,1,0:T(8,128)(2,1)}, u32[]{:S(2)}, u32[]{:S(2)}) collective-permute-start(bf16[5,2,2,2,16,2304]{5,4,3,2,1,0:T(8,128)(2,1)} %bitcast.136), channel_id=1, source_target_pairs={{0,16},{4,20},{8,24},{12,28},{16,0},{20,4},{24,8},{28,12},{1,17},{... | collective-permute-start | bytes 8847368 | tf_op jit(solution)/shard_map/ppermute | solution.py:436
  187.9 1.4 copy-start.12
  189.3 1.8 copy-start.23
  228.7 2.0 copy-start.6
  228.7 2.3 copy-start.28
  253.0 34.6 %collective-permute-start.4 = (bf16[5,2,2,2,16,1152]{5,4,3,2,1,0:T(8,128)(2,1)}, bf16[5,2,2,2,16,1152]{5,4,3,2,1,0:T(8,128)(2,1)}, u32[]{:S(2)}, u32[]{:S(2)}) collective-permute-start(bf16[5,2,2,2,16,1152]{5,4,3,2,1,0:T(8,128)(2,1)} %bitcast.21), channel_id=1, source_target_pairs={{0,4},{4,0},{8,12},{12,8},{16,20},{20,16},{24,28},{28,24},{1,5},{5... | collective-permute-start | bytes 4423688 | tf_op jit(solution)/shard_map/ppermute | solution.py:436
  253.5 108.2 %collective-permute-start.5 = (bf16[5,2,2,2,16,1152]{5,4,3,2,1,0:T(8,128)(2,1)}, bf16[5,2,2,2,16,1152]{5,4,3,2,1,0:T(8,128)(2,1)}, u32[]{:S(2)}, u32[]{:S(2)}) collective-permute-start(bf16[5,2,2,2,16,1152]{5,4,3,2,1,0:T(8,128)(2,1)} %bitcast.23), channel_id=1, source_target_pairs={{0,8},{4,12},{8,0},{12,4},{16,24},{20,28},{24,16},{28,20},{1,9},{5... | collective-permute-start | bytes 4423688 | tf_op jit(solution)/shard_map/ppermute | solution.py:436
  253.8 121.9 %collective-permute-start.6 = (bf16[320,1152]{1,0:T(8,128)(2,1)}, bf16[320,1152]{1,0:T(8,128)(2,1)}, u32[]{:S(2)}, u32[]{:S(2)}) collective-permute-start(bf16[320,1152]{1,0:T(8,128)(2,1)} %bitcast.20), channel_id=1, source_target_pairs={{0,16},{4,20},{8,24},{12,28},{16,0},{20,4},{24,8},{28,12},{1,17},{... | collective-permute-start | bytes 2211848 | tf_op jit(solution)/shard_map/ppermute | solution.py:436
  256.8 1.4 copy-start.18
  258.2 29.4 %copy-start.2 = (bf16[5,2,4,16,2304]{4,3,2,1,0:T(8,128)(2,1)S(1)}, bf16[5,2,4,16,2304]{4,3,2,1,0:T(8,128)(2,1)}, u32[]{:S(2)}) copy-start(bf16[5,2,4,16,2304]{4,3,2,1,0:T(8,128)(2,1)} %copy-done.1) | copy-start | bytes 8847364
  287.6 74.0 %copy-start.16 = (bf16[640,1152]{1,0:T(8,128)(2,1)S(1)}, bf16[640,1152]{1,0:T(8,128)(2,1)}, u32[]{:S(2)}) copy-start(bf16[640,1152]{1,0:T(8,128)(2,1)} %copy-done.14) | copy-start | bytes 4423684
  301.7 74.1 %copy-start.4 = (bf16[2304,1152]{1,0:T(8,128)(2,1)}, bf16[2304,1152]{1,0:T(8,128)(2,1)S(1)}, u32[]{:S(2)}) copy-start(bf16[2304,1152]{1,0:T(8,128)(2,1)S(1)} %gate_product.1) | copy-start | bytes 15925252
  375.6 3.2 copy-start.3
  375.7 7.3 collective-permute-start.8
  378.8 72.5 %collective-permute-start.9 = (bf16[2,2,288,1152]{3,2,1,0:T(8,128)(2,1)}, bf16[2,2,288,1152]{3,2,1,0:T(8,128)(2,1)}, u32[]{:S(2)}, u32[]{:S(2)}) collective-permute-start(bf16[2,2,288,1152]{3,2,1,0:T(8,128)(2,1)} %dynamic-slice_bitcast_fusion.2), channel_id=1, source_target_pairs={{0,8},{4,12},{8,0},{12,4},{16,24},{20,28},{24,16},{28,20},{1,9},{5... | collective-permute-start | bytes 7962632 | tf_op jit(solution)/shard_map/ppermute | solution.py:436
  378.8 4.1 copy-start.10
  378.8 4.1 copy-start.19
  382.4 180.0 %collective-permute-start.11 = (bf16[2,2,288,1152]{3,2,1,0:T(8,128)(2,1)}, bf16[2,2,288,1152]{3,2,1,0:T(8,128)(2,1)}, u32[]{:S(2)}, u32[]{:S(2)}) collective-permute-start(bf16[2,2,288,1152]{3,2,1,0:T(8,128)(2,1)} %dynamic-slice_bitcast_fusion), channel_id=1, source_target_pairs={{0,4},{4,0},{8,12},{12,8},{16,20},{20,16},{24,28},{28,24},{1,5},{5... | collective-permute-start | bytes 7962632 | tf_op jit(solution)/shard_map/ppermute | solution.py:436
  395.7 3.1 copy-start.5
  398.8 163.6 %collective-permute-start.10 = (bf16[2,288,2304]{2,1,0:T(8,128)(2,1)}, bf16[2,288,2304]{2,1,0:T(8,128)(2,1)}, u32[]{:S(2)}, u32[]{:S(2)}) collective-permute-start(bf16[2,288,2304]{2,1,0:T(8,128)(2,1)} %dynamic-slice_bitcast_fusion.1), channel_id=1, source_target_pairs={{0,4},{4,0},{8,12},{12,8},{16,20},{20,16},{24,28},{28,24},{1,5},{5... | collective-permute-start | bytes 7962632 | tf_op jit(solution)/shard_map/ppermute | solution.py:436
  402.9 1.8 copy-start.7
  404.7 1.4 copy-start.13
  407.5 37.6 %copy-start.47 = (bf16[5,128,512]{2,1,0:T(8,128)(2,1)S(1)}, bf16[5,128,512]{2,1,0:T(8,128)(2,1)}, u32[]{:S(2)}) copy-start(bf16[5,128,512]{2,1,0:T(8,128)(2,1)} %get-tuple-element.70) | copy-start | bytes 1966084
  445.1 3.5 copy-start.26
  445.1 6.3 slice-start.2
  448.5 2.8 slice-start.3
  453.8 1.5 copy-start.29
  455.3 111.6 %slice-start = ((s8[5308416]{0:T(1024)(128)(4,1)}), s8[4194304]{0:T(1024)(128)(4,1)S(1)}, s32[]{:S(2)}) async-start(s8[5308416]{0:T(1024)(128)(4,1)} %bitcast.117), calls=%async_computation | async-start | bytes 8388608
  456.6 258.8 %collective-permute-start.12 = (bf16[2,288,1152]{2,1,0:T(8,128)(2,1)}, bf16[2,288,1152]{2,1,0:T(8,128)(2,1)}, u32[]{:S(2)}, u32[]{:S(2)}) collective-permute-start(bf16[2,288,1152]{2,1,0:T(8,128)(2,1)} %dynamic-slice_bitcast_fusion.5), channel_id=1, source_target_pairs={{0,16},{4,20},{8,24},{12,28},{16,0},{20,4},{24,8},{28,12},{1,17},{... | collective-permute-start | bytes 3981320 | tf_op jit(solution)/shard_map/ppermute | solution.py:436
  459.4 107.5 %slice-start.1 = ((s8[5308416]{0:T(1024)(128)(4,1)}), s8[1114112]{0:T(1024)(128)(4,1)S(1)}, s32[]{:S(2)}) async-start(s8[5308416]{0:T(1024)(128)(4,1)} %bitcast.117), calls=%async_computation.1 | async-start | bytes 2228224
  565.6 3.9 copy-start.31
  566.9 148.5 %collective-permute-start.14 = (bf16[288,2304]{1,0:T(8,128)(2,1)}, bf16[288,2304]{1,0:T(8,128)(2,1)}, u32[]{:S(2)}, u32[]{:S(2)}) collective-permute-start(bf16[288,2304]{1,0:T(8,128)(2,1)} %dynamic-slice_bitcast_fusion.3), channel_id=1, source_target_pairs={{0,8},{4,12},{8,0},{12,4},{16,24},{20,28},{24,16},{28,20},{1,9},{5... | collective-permute-start | bytes 3981320 | tf_op jit(solution)/shard_map/ppermute | solution.py:436
  566.9 5.3 copy-start.42
  566.9 5.3 copy-start.46
  569.5 2.7 copy-start.33
  569.5 2.7 copy-start.35
  569.5 2.7 copy-start.44
  569.7 145.7 %collective-permute-start.13 = (bf16[2,288,1152]{2,1,0:T(8,128)(2,1)S(1)}, bf16[2,288,1152]{2,1,0:T(8,128)(2,1)S(1)}, u32[]{:S(2)}, u32[]{:S(2)}) collective-permute-start(bf16[2,288,1152]{2,1,0:T(8,128)(2,1)S(1)} %dynamic-slice_bitcast_fusion.4), channel_id=1, source_target_pairs={{0,16},{4,20},{8,24},{12,28},{16,0},{20,4},{24,8},{28,12},{1,17},{... | collective-permute-start | bytes 3981320 | tf_op jit(solution)/shard_map/ppermute | solution.py:436
  572.2 3.9 copy-start.9
  572.3 3.9 copy-start.27
  576.1 21.2 %copy-start.22 = (bf16[5,2,4,16,2304]{4,3,2,1,0:T(8,128)(2,1)S(1)}, bf16[5,2,4,16,2304]{4,3,2,1,0:T(8,128)(2,1)}, u32[]{:S(2)}) copy-start(bf16[5,2,4,16,2304]{4,3,2,1,0:T(8,128)(2,1)} %copy-done.21) | copy-start | bytes 8847364
  710.2 4.3 copy-start.36
  710.2 5.2 copy-start.34
  715.4 1.8 copy-start.30
  715.8 4.8 copy-start.32
  715.8 12.5 %collective-permute-start.16 = (bf16[288,1152]{1,0:T(8,128)(2,1)S(1)}, bf16[288,1152]{1,0:T(8,128)(2,1)S(1)}, u32[]{:S(2)}, u32[]{:S(2)}) collective-permute-start(bf16[288,1152]{1,0:T(8,128)(2,1)S(1)} %dynamic-slice_bitcast_fusion.6), channel_id=1, source_target_pairs={{0,8},{4,12},{8,0},{12,4},{16,24},{20,28},{24,16},{28,20},{1,9},{5... | collective-permute-start | bytes 1990664 | tf_op jit(solution)/shard_map/ppermute | solution.py:436
  718.9 12.5 %collective-permute-start.15 = (bf16[288,1152]{1,0:T(8,128)(2,1)S(1)}, bf16[288,1152]{1,0:T(8,128)(2,1)S(1)}, u32[]{:S(2)}, u32[]{:S(2)}) collective-permute-start(bf16[288,1152]{1,0:T(8,128)(2,1)S(1)} %dynamic-slice_bitcast_fusion.7), channel_id=1, source_target_pairs={{0,4},{4,0},{8,12},{12,8},{16,20},{20,16},{24,28},{28,24},{1,5},{5... | collective-permute-start | bytes 1990664 | tf_op jit(solution)/shard_map/ppermute | solution.py:436
  731.5 1.7 copy-start.37
  (5 other events, 6.1 us)

commit v6 on v5

--- a/solution.py
+++ b/solution.py
@@ -1076,9 +1076,11 @@
     attn_grad = pin(attn_grad, gates)
     gates.step()
     qkv_grad = attend_back(queries, kv_all, attn_grad, attn, sums, cosine, sine, *where, 16)
-    qkv_grad = pin(qkv_grad, down, ups).reshape(all_rows, -1)
+    qkv_grad = pin(qkv_grad, down, ups, gates).reshape(all_rows, -1)
     ups.step()
     down.step()
+    gate_own, gate_give = owner_pieces(gates.finish(), low_bit)
+    gate_sent = Sent(gate_give, low_bit)
     qkv_weight = jnp.concatenate([query_weight, key_weight, value_weight], 1)
     part = ein("rh,dh->rd", qkv_grad, qkv_weight).astype(BF16)
     qkv_part = ein("rd,rh->dh", normed_all, qkv_grad).astype(BF16)
@@ -1095,9 +1097,7 @@
         [attn_in_gain_part, attn_out_gain_part, ffw_in_gain_part, ffw_out_gain_part], 0
     )
     (output_sum, qkv_sum), gains = weights_scatter([output_part, qkv_part], gains, 8)
-    gains = pin(gains, gates, ups, down)
-    gate_own, gate_give = owner_pieces(gates.finish(), low_bit)
-    gate_sent = Sent(gate_give, low_bit)
+    gains = pin(gains, gate_sent, ups, down)
     up_own, up_give = owner_pieces(ups.finish(), next_bit)
     up_sent = Sent(up_give, next_bit)
     down_sum = down.finish().astype(F32)

time: 743 us -> 737 us (level)
  Pallas kernels: 551 us -> 543 us
    pallas_call x1, Pallas kernels: 107 us -> 99.2 us  [weights_scatter(): pl.pallas_call(functools.partial(weights_scatter_kernel, count, tp_count,...]
    unnamed x109 -> x115, local copies, waits for them, and re-layouts: 30.1 us -> 30.5 us
  transfers between devices with their start and end apart: 17 -> 17, of which waited for: 5 -> 4; matrix products, arithmetic and copies ran while one was open for 7% -> 7% of each run, Pallas kernels for 58% -> 58%
where the time goes in v6:
time: 737 us; the launch traced here: 728 us
  Pallas kernels  543 us (74%)
  waiting for transfers between devices  61.9 us (8%)
  local copies, waits for them, and re-layouts  52.6 us (7%)
  matrix products  28.4 us (4%)
  other arithmetic  22.5 us (3%)
  starting transfers between devices  17.2 us (2%)
    pallas_call x5, Pallas kernels, tp_exchange(): pl.pallas_call(functools.partial(tp_kernel, fn, count, items, len(ins), l...  154 us
    pallas_call x1, Pallas kernels, attend_back_some(): pl.pallas_call(functools.partial(attend_back_kernel, count, seqs, heads),...  104 us
    pallas_call x1, Pallas kernels, weights_scatter(): pl.pallas_call(functools.partial(weights_scatter_kernel, count, tp_count,...  99.2 us
    pallas_call x1, Pallas kernels, attend_all(): pl.pallas_call(functools.partial(attend_kernel, count, seqs, heads), out_...  65.2 us
    ppermute x14, waiting for transfers between devices, send_ctx(): lax.ppermute(value, 'ctx', [(i, i ^ mask) for i in range(lax.axis_size('c...  61.9 us
    pallas_call x3, Pallas kernels, product(): pl.pallas_call(product_kernel, grid=(width // tile,), out_shape=jax.Shape...  40.8 us
    pallas_call x1, Pallas kernels, ffw_call(): pl.pallas_call(kernel, grid=(hidden // tile,), out_shape=[jax.ShapeDtypeS...  32.9 us
    unnamed x115, local copies, waits for them, and re-layouts  30.5 us
  transfers between devices with their start and end apart: 17, of which 4 were waited for; matrix products, arithmetic and copies ran while one was open for 7% of the time, Pallas kernels for 58%

profile of v6, /device:TPU:0, one launch (start us, length us, event | category | flops | bytes accessed | tf_op | source)
XLA Modules:
  0.0 727.8 jit_solution(8515500346238134475)
XLA Ops:
  4.6 1.3 copy.60
  6.7 21.6 %enter.1 = bf16[5,2,4,16,2304]{4,3,2,1,0:T(8,128)(2,1)S(1)} custom-call(bf16[5,2,16,2304]{3,2,1,0:T(8,128)(2,1)S(1)} %bitcast.129, bf16[1,2304]{1,0:T(2,128)(2,1)S(1)} %reshape.269.refs_1_.refs_3_), custom_call_target="tpu_custom_call" | custom-call | flops 180000000 | tf_op jit(solution)/shard_map/enter/pallas_call | solution.py:180
  28.3 2.7 fusion.13.q
  31.1 1.8 fusion.15.v
  32.9 1.8 fusion.17.k
  35.4 2.1 multiply_sine_fusion
  37.5 65.2 %attend.1 = (bf16[10,8,128,256]{3,2,1,0:T(8,128)(2,1)}, f32[5,128,512]{2,1,0:T(8,128)}, bf16[5,128,512]{2,1,0:T(8,128)(2,1)}, f32[5,2,128,1]{3,2,1,0:T(8,128)}, bf16[5,128,512]{2,1,0:T(8,128)(2,1)}) custom-call(f32[5,128,512]{2,1,0:T(8,128)} %fusion.13.q, f32[5,128,256]{2,1,0:T(8,128)} %fusion.17.k, f32[5,128,256]{2,1,0:T(8,128)} %fusion.15.v, ...), custom_call_target="tpu_custom_call" | custom-call | flops 600000000 | tf_op jit(solution)/shard_map/attend/pallas_call | solution.py:289
  102.6 4.3 convolution_convert_fusion.1
  107.0 1.8 copy-done.20
  108.8 37.3 %middle.1 = (bf16[5,2,4,16,2304]{4,3,2,1,0:T(8,128)(2,1)S(1)}, f32[5,2,16,2304]{3,2,1,0:T(8,128)S(1)}, f32[5,2,16,2304]{3,2,1,0:T(8,128)S(1)}) custom-call(bf16[5,2,4,16,2304]{4,3,2,1,0:T(8,128)(2,1)S(1)} %bitcast.138, bf16[5,2,16,2304]{3,2,1,0:T(8,128)(2,1)S(1)} %bitcast.130, bf16[1,2304]{1,0:T(2,128)(2,1)S(1)} %reshape.272.refs_2_.refs_5_, ...), custom_call_target="tpu_custom_call" | custom-call | flops 360000000 | tf_op jit(solution)/shard_map/middle/pallas_call | solution.py:180
  147.3 1.3 constant_dynamic-slice_fusion.4
  149.3 32.9 %ffw.1 = (f32[640,2304]{1,0:T(8,128)}, f32[640,2304]{1,0:T(8,128)}, bf16[640,2304]{1,0:T(8,128)(2,1)}, bf16[640,2304]{1,0:T(8,128)(2,1)}) custom-call(bf16[640,2304]{1,0:T(8,128)(2,1)} %bitcast.113, bf16[2304,2304]{1,0:T(8,128)(2,1)} %gate_w.3, bf16[2304,2304]{1,0:T(8,128)(2,1)} %up_w.3, bf16[2304,2304]{1,0:T(8,128)(2,1)} %down_w.3), custom_call_target="tpu_custom_call" | custom-call | flops 10000000 | tf_op jit(solution)/shard_map/ffw/pallas_call | solution.py:888
  182.2 1.3 collective-permute-done.far
  184.0 2.6 collective-permute-start.7
  186.6 1.2 copy.59
  187.8 1.4 copy-done.13
  189.2 1.8 copy-done.23
  191.0 37.6 %turn.1 = (bf16[5,2,4,16,2304]{4,3,2,1,0:T(8,128)(2,1)S(1)}, bf16[5,2,16,2304]{3,2,1,0:T(8,128)(2,1)S(1)}, f32[1,2304]{1,0:T(1,128)S(1)}) custom-call(bf16[5,2,4,16,2304]{4,3,2,1,0:T(8,128)(2,1)S(1)} %bitcast.143, f32[5,2,16,2304]{3,2,1,0:T(8,128)S(1)} %copy-done.13, bf16[5,2,16,2304]{3,2,1,0:T(8,128)(2,1)S(1)} %bitcast.132, ...), custom_call_target="tpu_custom_call" | custom-call | flops 360000000 | tf_op jit(solution)/shard_map/turn/pallas_call | solution.py:180
  228.6 1.9 constant_dynamic-slice_fusion.1
  231.9 18.9 %hidden_grads.1 = (bf16[640,1152]{1,0:T(8,128)(2,1)}, bf16[640,1152]{1,0:T(8,128)(2,1)}, bf16[640,1152]{1,0:T(8,128)(2,1)S(1)}, bf16[640,1152]{1,0:T(8,128)(2,1)S(1)}) custom-call(s32[2]{0:T(128)S(1)} %get-tuple-element.185.bits, bf16[640,2304]{1,0:T(8,128)(2,1)} %bitcast.127, f32[640,2304]{1,0:T(8,128)} %get-tuple-element.86.gate, ...), custom_call_target="tpu_custom_call" | custom-call | flops 10000000 | tf_op jit(solution)/shard_map/hidden_grads/pallas_call | solution.py:822
  253.8 1.4 copy-done.16
  255.2 1.4 copy-done.18
  256.5 28.7 %input_grad.1 = bf16[640,2304]{1,0:T(8,128)(2,1)} custom-call(s32[2]{0:T(128)S(1)} %get-tuple-element.185.bits, bf16[640,1152]{1,0:T(8,128)(2,1)} %get-tuple-element.88.gate_give, bf16[640,1152]{1,0:T(8,128)(2,1)} %get-tuple-element.89.up_give, bf16[640,1152]{1,0:T(8,128)(2,1)S(1)} %copy-done.18, bf16[640,1152]{1,0:T(8,128)(2,1)S(1)} %copy-done.16, ...), custom_call_target="tpu_custom_call" | custom-call | flops 10000000 | tf_op jit(solution)/shard_map/input_grad/pallas_call | solution.py:864
  285.2 2.4 collective-permute-done.4.got
  287.6 14.0 %gate_product.1 = bf16[2304,1152]{1,0:T(8,128)(2,1)S(1)} custom-call(bf16[640,2304]{1,0:T(8,128)(2,1)S(1)} %bitcast.114, bf16[320,2304]{1,0:T(8,128)(2,1)} %collective-permute-done.1.far, bf16[320,2304]{1,0:T(8,128)(2,1)} %collective-permute-done.3.near, bf16[5,2,2,2,16,1152]{5,4,3,2,1,0:T(8,128)(2,1)S(1)} %bitcast.135, ...), custom_call_target="tpu_custom_call" | custom-call | flops 10000000 | tf_op jit(solution)/shard_map/gate_product/pallas_call | solution.py:517
  301.6 1.7 dynamic-slice_bitcast_fusion.2
  303.3 1.4 copy-done.6
  305.0 1.8 collective-permute-start.6
  306.8 54.9 %collective-permute-done.5.got = bf16[5,2,2,2,16,1152]{5,4,3,2,1,0:T(8,128)(2,1)} collective-permute-done((bf16[5,2,2,2,16,1152]{5,4,3,2,1,0:T(8,128)(2,1)}, bf16[5,2,2,2,16,1152]{5,4,3,2,1,0:T(8,128)(2,1)}, u32[]{:S(2)}, u32[]{:S(2)}) %collective-permute-start.5) | collective-permute-done | bytes 1474592 | tf_op jit(solution)/shard_map/ppermute | solution.py:436
  361.7 14.0 %up_product.1 = bf16[2304,1152]{1,0:T(8,128)(2,1)S(1)} custom-call(bf16[640,2304]{1,0:T(8,128)(2,1)S(1)} %bitcast.115, bf16[320,2304]{1,0:T(8,128)(2,1)} %collective-permute-done.far, bf16[320,2304]{1,0:T(8,128)(2,1)} %collective-permute-done.2.near, bf16[5,2,2,2,16,1152]{5,4,3,2,1,0:T(8,128)(2,1)S(1)} %bitcast.134, ...), custom_call_target="tpu_custom_call" | custom-call | flops 10000000 | tf_op jit(solution)/shard_map/up_product/pallas_call | solution.py:517
  375.7 2.4 copy-done.4
  378.1 3.6 dynamic-slice_bitcast_fusion
  382.2 12.8 %down_product.1 = bf16[1152,2304]{1,0:T(8,128)(2,1)S(1)} custom-call(bf16[640,1152]{1,0:T(8,128)(2,1)S(1)} %copy-done.11, bf16[320,1152]{1,0:T(8,128)(2,1)} %collective-permute-done.6.far, bf16[320,1152]{1,0:T(8,128)(2,1)} %collective-permute-done.8.near, bf16[5,2,2,2,16,2304]{5,4,3,2,1,0:T(8,128)(2,1)S(1)} %bitcast.137, ...), custom_call_target="tpu_custom_call" | custom-call | flops 10000000 | tf_op jit(solution)/shard_map/down_product/pallas_call | solution.py:517
  395.1 1.7 dynamic-slice_bitcast_fusion.1
  396.7 2.2 copy-done.5
  399.0 1.5 collective-permute-start.10
  400.5 37.7 %middle_back.1 = (bf16[5,2,4,16,2304]{4,3,2,1,0:T(8,128)(2,1)S(1)}, f32[5,2,16,2304]{3,2,1,0:T(8,128)S(1)}, f32[1,2304]{1,0:T(1,128)S(1)}, f32[1,2304]{1,0:T(1,128)S(1)}) custom-call(bf16[5,2,4,16,2304]{4,3,2,1,0:T(8,128)(2,1)S(1)} %bitcast.128, f32[5,2,16,2304]{3,2,1,0:T(8,128)S(1)} %copy-done.14, f32[5,2,16,2304]{3,2,1,0:T(8,128)S(1)} %copy-done.25, ...), custom_call_target="tpu_custom_call" | custom-call | flops 360000000 | tf_op jit(solution)/shard_map/middle_back/pallas_call | solution.py:180
  438.3 2.8 fusion.11.refs_2_
  441.1 1.4 slice-done.3
  442.5 2.4 fusion.2
  445.1 1.4 copy-done.33
  446.4 2.9 collective-permute-start.12
  449.4 1.4 copy.53
  450.8 5.4 convolution_convert_fusion.3
  456.2 103.6 %attend_back.1 = bf16[5,128,1024]{2,1,0:T(8,128)(2,1)} custom-call(bf16[5,128,512]{2,1,0:T(8,128)(2,1)} %get-tuple-element.79.refs_0_, bf16[10,8,128,256]{3,2,1,0:T(8,128)(2,1)} %get-tuple-element.80.refs_1_, f32[5,128,512]{2,1,0:T(8,128)} %fusion.11.refs_2_, f32[5,128,512]{2,1,0:T(8,128)} %get-tuple-element.109.refs_3_, ...), custom_call_target="tpu_custom_call" | custom-call | flops 600000000 | tf_op jit(solution)/shard_map/attend_back/pallas_call | solution.py:402
  559.9 3.2 fusion
  563.1 1.3 dynamic-slice_bitcast_fusion.3
  564.4 2.3 collective-permute-start.15
  566.7 2.5 fusion.1
  569.5 2.5 copy-done.34
  571.9 2.2 fusion.10
  575.9 3.8 convolution_convert_fusion.2
  579.7 5.8 convolution_convert_fusion
  585.5 20.2 %leave.1 = (f32[5,2,16,2304]{3,2,1,0:T(8,128)S(1)}, f32[1,2304]{1,0:T(1,128)S(1)}) custom-call(bf16[5,2,4,16,2304]{4,3,2,1,0:T(8,128)(2,1)S(1)} %bitcast.144, bf16[5,2,16,2304]{3,2,1,0:T(8,128)(2,1)S(1)} %bitcast.131, f32[5,2,16,2304]{3,2,1,0:T(8,128)S(1)} %copy-done.27, bf16[1,2304]{1,0:T(2,128)(2,1)S(1)} %reshape.269.refs_1_.refs_3_), custom_call_target="tpu_custom_call" | custom-call | flops 180000000 | tf_op jit(solution)/shard_map/leave/pallas_call | solution.py:180
  606.3 99.2 %weights_scatter.1 = (f32[6,48,512]{2,1,0:T(8,128)}, f32[6,48,1024]{2,1,0:T(8,128)}, f32[4,2304]{1,0:T(4,128)}) custom-call(bf16[8,6,48,512]{3,2,1,0:T(8,128)(2,1)} %bitcast.151, bf16[8,6,48,1024]{3,2,1,0:T(8,128)(2,1)} %bitcast.149, f32[4,2304]{1,0:T(4,128)} %pad_maximum_fusion.refs_2_), custom_call_target="tpu_custom_call" | custom-call | flops 800000000 | tf_op jit(solution)/shard_map/weights_scatter/pallas_call | solution.py:652
  705.5 2.1 slice.28
  707.6 2.2 copy.54
  711.1 2.5 collective-permute-start.16
  713.7 1.2 bitcast_select_fusion.3
  714.9 1.7 maximum_convert_fusion
  716.6 1.5 dynamic-slice_reduce_fusion
  718.1 3.1 convert_bitcast_fusion
  721.2 3.3 collective-permute-done.16
  724.7 1.7 maximum_convert_fusion.1
  (152 shorter events, 18.2 us)
Async XLA Ops:
  0.6 102.0 %copy-start = (bf16[512,2304]{1,0:T(8,128)(2,1)S(1)}, bf16[512,2304]{1,0:T(8,128)(2,1)}, u32[]{:S(2)}) copy-start(bf16[512,2304]{1,0:T(8,128)(2,1)} %param.20) | copy-start | bytes 7077892
  4.6 23.7 %copy-start.44 = (bf16[2304,512]{1,0:T(8,128)(2,1)S(1)}, bf16[2304,512]{1,0:T(8,128)(2,1)}, u32[]{:S(2)}) copy-start(bf16[2304,512]{1,0:T(8,128)(2,1)} %param.17) | copy-start | bytes 7077892
  6.0 101.0 %copy-start.9 = (bf16[16,5,2,2304]{3,0,2,1:T(8,128)(2,1)}, bf16[16,5,2,2304]{3,0,2,1:T(8,128)(2,1)S(1)}, u32[]{:S(2)}) copy-start(bf16[16,5,2,2304]{3,0,2,1:T(8,128)(2,1)S(1)} %copy.60) | copy-start | bytes 2211844
  28.3 4.5 copy-start.21
  28.3 2.8 copy-start.48
  31.1 1.8 copy-start.46
  32.8 2.5 copy-start.41
  32.9 2.5 copy-start.42
  107.0 1.8 copy-start.20
  147.3 2.1 copy-start.2
  147.3 34.9 %copy-start.12 = (f32[5,2,16,2304]{3,2,1,0:T(8,128)}, f32[5,2,16,2304]{3,2,1,0:T(8,128)S(1)}, u32[]{:S(2)}) copy-start(f32[5,2,16,2304]{3,2,1,0:T(8,128)S(1)} %get-tuple-element.77.refs_1_) | copy-start | bytes 4423684
  148.6 39.2 %copy-start.43 = (bf16[2304]{0:T(1024)(128)(2,1)S(1)}, bf16[2304]{0:T(1024)(128)(2,1)}, u32[]{:S(2)}) copy-start(bf16[2304]{0:T(1024)(128)(2,1)} %param.26) | copy-start | bytes 13828
  148.6 34.9 %collective-permute-start = (bf16[320,2304]{1,0:T(8,128)(2,1)}, bf16[320,2304]{1,0:T(8,128)(2,1)}, u32[]{:S(2)}, u32[]{:S(2)}) collective-permute-start(bf16[320,2304]{1,0:T(8,128)(2,1)} %bitcast.12), channel_id=1, source_target_pairs={{0,8},{4,12},{8,0},{12,4},{16,24},{20,28},{24,16},{28,20},{1,9},{5... | collective-permute-start | bytes 4423688 | tf_op jit(solution)/shard_map/ppermute | solution.py:436
  148.6 34.9 %collective-permute-start.1 = (bf16[320,2304]{1,0:T(8,128)(2,1)}, bf16[320,2304]{1,0:T(8,128)(2,1)}, u32[]{:S(2)}, u32[]{:S(2)}) collective-permute-start(bf16[320,2304]{1,0:T(8,128)(2,1)} %bitcast.12), channel_id=1, source_target_pairs={{0,4},{4,0},{8,12},{12,8},{16,20},{20,16},{24,28},{28,24},{1,5},{5... | collective-permute-start | bytes 4423688 | tf_op jit(solution)/shard_map/ppermute | solution.py:436
  183.5 45.1 %collective-permute-start.2 = (bf16[320,2304]{1,0:T(8,128)(2,1)}, bf16[320,2304]{1,0:T(8,128)(2,1)}, u32[]{:S(2)}, u32[]{:S(2)}) collective-permute-start(bf16[320,2304]{1,0:T(8,128)(2,1)} %collective-permute-done.far), channel_id=1, source_target_pairs={{0,1},{1,0},{2,3},{3,2},{4,5},{5,4},{6,7},{7,6},{8,9},{9,8},{10,11... | collective-permute-start | bytes 4423688 | tf_op jit(solution)/shard_map/ppermute | solution.py:440
  183.5 45.2 %collective-permute-start.3 = (bf16[320,2304]{1,0:T(8,128)(2,1)}, bf16[320,2304]{1,0:T(8,128)(2,1)}, u32[]{:S(2)}, u32[]{:S(2)}) collective-permute-start(bf16[320,2304]{1,0:T(8,128)(2,1)} %collective-permute-done.1.far), channel_id=1, source_target_pairs={{0,1},{1,0},{2,3},{3,2},{4,5},{5,4},{6,7},{7,6},{8,9},{9,8},{10,11... | collective-permute-start | bytes 4423688 | tf_op jit(solution)/shard_map/ppermute | solution.py:440
  184.0 194.0 %collective-permute-start.7 = (bf16[5,2,2,2,16,2304]{5,4,3,2,1,0:T(8,128)(2,1)}, bf16[5,2,2,2,16,2304]{5,4,3,2,1,0:T(8,128)(2,1)}, u32[]{:S(2)}, u32[]{:S(2)}) collective-permute-start(bf16[5,2,2,2,16,2304]{5,4,3,2,1,0:T(8,128)(2,1)} %bitcast.136), channel_id=1, source_target_pairs={{0,16},{4,20},{8,24},{12,28},{16,0},{20,4},{24,8},{28,12},{1,17},{... | collective-permute-start | bytes 8847368 | tf_op jit(solution)/shard_map/ppermute | solution.py:436
  189.2 1.8 copy-start.23
  228.6 2.1 copy-start.7
  228.6 2.3 copy-start.28
  253.0 34.6 %collective-permute-start.4 = (bf16[5,2,2,2,16,1152]{5,4,3,2,1,0:T(8,128)(2,1)}, bf16[5,2,2,2,16,1152]{5,4,3,2,1,0:T(8,128)(2,1)}, u32[]{:S(2)}, u32[]{:S(2)}) collective-permute-start(bf16[5,2,2,2,16,1152]{5,4,3,2,1,0:T(8,128)(2,1)} %bitcast.21), channel_id=1, source_target_pairs={{0,4},{4,0},{8,12},{12,8},{16,20},{20,16},{24,28},{28,24},{1,5},{5... | collective-permute-start | bytes 4423688 | tf_op jit(solution)/shard_map/ppermute | solution.py:436
  253.5 108.2 %collective-permute-start.5 = (bf16[5,2,2,2,16,1152]{5,4,3,2,1,0:T(8,128)(2,1)}, bf16[5,2,2,2,16,1152]{5,4,3,2,1,0:T(8,128)(2,1)}, u32[]{:S(2)}, u32[]{:S(2)}) collective-permute-start(bf16[5,2,2,2,16,1152]{5,4,3,2,1,0:T(8,128)(2,1)} %bitcast.23), channel_id=1, source_target_pairs={{0,8},{4,12},{8,0},{12,4},{16,24},{20,28},{24,16},{28,20},{1,9},{5... | collective-permute-start | bytes 4423688 | tf_op jit(solution)/shard_map/ppermute | solution.py:436
  256.5 31.1 %copy-start.3 = (bf16[5,2,4,16,2304]{4,3,2,1,0:T(8,128)(2,1)S(1)}, bf16[5,2,4,16,2304]{4,3,2,1,0:T(8,128)(2,1)}, u32[]{:S(2)}) copy-start(bf16[5,2,4,16,2304]{4,3,2,1,0:T(8,128)(2,1)} %copy-done.2) | copy-start | bytes 8847364
  301.6 3.2 copy-start.6
  301.6 3.4 copy-start.39
  304.8 136.3 %collective-permute-start.9 = (bf16[2,2,288,1152]{3,2,1,0:T(8,128)(2,1)}, bf16[2,2,288,1152]{3,2,1,0:T(8,128)(2,1)}, u32[]{:S(2)}, u32[]{:S(2)}) collective-permute-start(bf16[2,2,288,1152]{3,2,1,0:T(8,128)(2,1)} %dynamic-slice_bitcast_fusion.2), channel_id=1, source_target_pairs={{0,8},{4,12},{8,0},{12,4},{16,24},{20,28},{24,16},{28,20},{1,9},{5... | collective-permute-start | bytes 7962632 | tf_op jit(solution)/shard_map/ppermute | solution.py:436
  305.0 73.0 %collective-permute-start.6 = (bf16[320,1152]{1,0:T(8,128)(2,1)S(1)}, bf16[320,1152]{1,0:T(8,128)(2,1)}, u32[]{:S(2)}, u32[]{:S(2)}) collective-permute-start(bf16[320,1152]{1,0:T(8,128)(2,1)S(1)} %bitcast.156), channel_id=1, source_target_pairs={{0,16},{4,20},{8,24},{12,28},{16,0},{20,4},{24,8},{28,12},{1,17},{... | collective-permute-start | bytes 2211848 | tf_op jit(solution)/shard_map/ppermute | solution.py:436
  375.7 2.4 copy-start.4
  378.0 4.1 collective-permute-start.8
  378.1 4.1 copy-start.11
  378.1 4.1 copy-start.19
  381.7 178.2 %collective-permute-start.11 = (bf16[2,2,288,1152]{3,2,1,0:T(8,128)(2,1)}, bf16[2,2,288,1152]{3,2,1,0:T(8,128)(2,1)}, u32[]{:S(2)}, u32[]{:S(2)}) collective-permute-start(bf16[2,2,288,1152]{3,2,1,0:T(8,128)(2,1)} %dynamic-slice_bitcast_fusion), channel_id=1, source_target_pairs={{0,4},{4,0},{8,12},{12,8},{16,20},{20,16},{24,28},{28,24},{1,5},{5... | collective-permute-start | bytes 7962632 | tf_op jit(solution)/shard_map/ppermute | solution.py:436
  382.2 18.4 %copy-start.25 = (f32[5,2,16,2304]{3,2,1,0:T(8,128)S(1)}, f32[5,2,16,2304]{3,2,1,0:T(8,128)}, u32[]{:S(2)}) copy-start(f32[5,2,16,2304]{3,2,1,0:T(8,128)} %copy-done.24) | copy-start | bytes 4423684
  395.0 4.0 copy-start.5
  395.0 5.5 copy-start.8
  395.0 5.5 copy-start.14
  399.0 160.9 %collective-permute-start.10 = (bf16[2,288,2304]{2,1,0:T(8,128)(2,1)}, bf16[2,288,2304]{2,1,0:T(8,128)(2,1)}, u32[]{:S(2)}, u32[]{:S(2)}) collective-permute-start(bf16[2,288,2304]{2,1,0:T(8,128)(2,1)} %dynamic-slice_bitcast_fusion.1), channel_id=1, source_target_pairs={{0,4},{4,0},{8,12},{12,8},{16,20},{20,16},{24,28},{28,24},{1,5},{5... | collective-permute-start | bytes 7962632 | tf_op jit(solution)/shard_map/ppermute | solution.py:436
  400.5 40.6 %slice-start.2 = ((s8[5308416]{0:T(1024)(128)(4,1)}), s8[1114112]{0:T(1024)(128)(4,1)S(1)}, s32[]{:S(2)}) async-start(s8[5308416]{0:T(1024)(128)(4,1)} %bitcast.123), calls=%async_computation.2 | async-start | bytes 2228224
  438.3 2.8 copy-start.26
  438.3 6.6 copy-start.30
  438.3 4.2 slice-start.3
  444.9 4.4 copy-start.29
  445.0 5.9 copy-start.50
  446.4 113.4 %collective-permute-start.12 = (bf16[2,288,1152]{2,1,0:T(8,128)(2,1)S(1)}, bf16[2,288,1152]{2,1,0:T(8,128)(2,1)}, u32[]{:S(2)}, u32[]{:S(2)}) collective-permute-start(bf16[2,288,1152]{2,1,0:T(8,128)(2,1)S(1)} %dynamic-slice_bitcast_fusion.5), channel_id=1, source_target_pairs={{0,16},{4,20},{8,24},{12,28},{16,0},{20,4},{24,8},{28,12},{1,17},{... | collective-permute-start | bytes 3981320 | tf_op jit(solution)/shard_map/ppermute | solution.py:436
  450.8 115.9 %slice-start = ((s8[5308416]{0:T(1024)(128)(4,1)}), s8[4194304]{0:T(1024)(128)(4,1)S(1)}, s32[]{:S(2)}) async-start(s8[5308416]{0:T(1024)(128)(4,1)} %bitcast.117), calls=%async_computation | async-start | bytes 8388608
  456.2 110.5 %slice-start.1 = ((s8[5308416]{0:T(1024)(128)(4,1)}), s8[1114112]{0:T(1024)(128)(4,1)S(1)}, s32[]{:S(2)}) async-start(s8[5308416]{0:T(1024)(128)(4,1)} %bitcast.117), calls=%async_computation.1 | async-start | bytes 2228224
  563.1 6.1 copy-start.31
  564.4 146.4 %collective-permute-start.15 = (bf16[288,2304]{1,0:T(8,128)(2,1)}, bf16[288,2304]{1,0:T(8,128)(2,1)}, u32[]{:S(2)}, u32[]{:S(2)}) collective-permute-start(bf16[288,2304]{1,0:T(8,128)(2,1)} %dynamic-slice_bitcast_fusion.3), channel_id=1, source_target_pairs={{0,8},{4,12},{8,0},{12,4},{16,24},{20,28},{24,16},{28,20},{1,9},{5... | collective-permute-start | bytes 3981320 | tf_op jit(solution)/shard_map/ppermute | solution.py:436
  566.7 9.1 %copy-start.49 = (bf16[2304,256]{1,0:T(8,128)(2,1)S(1)}, bf16[2304,256]{1,0:T(8,128)(2,1)}, u32[]{:S(2)}) copy-start(bf16[2304,256]{1,0:T(8,128)(2,1)} %param.19) | copy-start | bytes 3538948
  569.2 4.9 copy-start.35
  569.2 2.7 copy-start.34
  569.4 6.5 copy-start.37
  569.4 6.5 copy-start.45
  569.4 6.5 copy-start.47
  569.4 141.3 %collective-permute-start.14 = (bf16[2,288,1152]{2,1,0:T(8,128)(2,1)S(1)}, bf16[2,288,1152]{2,1,0:T(8,128)(2,1)S(1)}, u32[]{:S(2)}, u32[]{:S(2)}) collective-permute-start(bf16[2,288,1152]{2,1,0:T(8,128)(2,1)S(1)} %dynamic-slice_bitcast_fusion.4), channel_id=1, source_target_pairs={{0,16},{4,20},{8,24},{12,28},{16,0},{20,4},{24,8},{28,12},{1,17},{... | collective-permute-start | bytes 3981320 | tf_op jit(solution)/shard_map/ppermute | solution.py:436
  575.0 135.7 %collective-permute-start.13 = (bf16[288,1152]{1,0:T(8,128)(2,1)}, bf16[288,1152]{1,0:T(8,128)(2,1)}, u32[]{:S(2)}, u32[]{:S(2)}) collective-permute-start(bf16[288,1152]{1,0:T(8,128)(2,1)} %dynamic-slice_bitcast_fusion.7), channel_id=1, source_target_pairs={{0,4},{4,0},{8,12},{12,8},{16,20},{20,16},{24,28},{28,24},{1,5},{5... | collective-permute-start | bytes 1990664 | tf_op jit(solution)/shard_map/ppermute | solution.py:436
  575.8 3.9 copy-start.22
  579.7 5.8 copy-start.10
  579.7 5.8 copy-start.27
  705.5 4.3 copy-start.38
  705.5 5.2 copy-start.36
  711.1 13.4 %collective-permute-start.16 = (bf16[288,1152]{1,0:T(8,128)(2,1)S(1)}, bf16[288,1152]{1,0:T(8,128)(2,1)S(1)}, u32[]{:S(2)}, u32[]{:S(2)}) collective-permute-start(bf16[288,1152]{1,0:T(8,128)(2,1)S(1)} %dynamic-slice_bitcast_fusion.6), channel_id=1, source_target_pairs={{0,8},{4,12},{8,0},{12,4},{16,24},{20,28},{24,16},{28,20},{1,9},{5... | collective-permute-start | bytes 1990664 | tf_op jit(solution)/shard_map/ppermute | solution.py:436
  714.9 3.2 copy-start.32
  724.6 2.8 copy-start.1
  (8 other events, 10.7 us)
